TPU v7x, 256 devices: a whole 4x4x8 slice. The times are simulated.
256 devices in a mesh: ctx: 32 (over y, z), exp: 8 (over x, core).
Axes of the slice: x: 4, y: 4, z: 8, core: 2. Of those that a mesh axis runs over, the one named last changes fastest.
Arguments:
- hidden: bfloat16 [2048, 4096], P(('ctx', 'exp')), may hold values from -1.1953125 to 1.1953125
- queries: bfloat16 [2048, 4096], P('ctx', 'exp'), may hold values from -8 to 8
- keys: bfloat16 [2048, 256], P('ctx'), may hold values from -3 to 3
- values: bfloat16 [2048, 256], P('ctx'), may hold values from -6 to 6
- out_weight: bfloat16 [4096, 4096], P('exp', 'ctx'), may hold values from -0.09375 to 0.09375
- norm_gain: float32 [4096], replicated, may hold values from 0.5 to 1.5
- w_gate: bfloat16 [256, 4096, 384], P(('ctx', 'exp')), may hold values from -0.09375 to 0.09375
- w_up: bfloat16 [256, 4096, 384], P(('ctx', 'exp')), may hold values from -0.09375 to 0.09375
- w_down: bfloat16 [256, 384, 4096], P(('ctx', 'exp')), may hold values from -0.15625 to 0.15625
- routes: int32 [2048, 8], P(('ctx', 'exp')), may hold values from 0 to 63, all different within a row; in each aligned block of 8 rows (0 to 7, 8 to 15, ...) at most 2 rows name the same one
- gates: float32 [2048, 8], P(('ctx', 'exp')), may hold values from 0.05 to 0.5
Outputs:
- attended: bfloat16 [2048, 4096], P(('ctx', 'exp'))
- mixed: bfloat16 [2048, 4096], P(('ctx', 'exp'))
Inputs may be any that keep to these rules, and one draw needn't show every extreme that they name: `routes`: each token names 8 different experts. In each aligned block of 8 rows (the rows of one device) no expert is named by more than 2 rows, and in some blocks one expert is named by exactly 2 rows.
All inputs are finite; a program needn't handle non-finite values.
Results may differ from a plain program's by a relative error of at most 0.025.
Values may be sent and summed in bfloat16 or wider, within the bound.
No kernel may reach another device: no remote copies, remote signals or barrier semaphores. Data moves between devices by JAX's collectives and lax.ppermute only.
A program may use at most 128 MiB of HBM per device.

v0:
```python
import jax
import jax.numpy as jnp
from jax import lax
from jax.sharding import PartitionSpec as P

D = 4096
HEAD_SIZE = 128
QUERY_HEADS = 32
KEY_VALUE_HEADS = 2
PARTS_SIZE = 4
TOPK = 8


def on_device(
    hidden, queries, keys, values, out_weight, norm_gain, w_gate, w_up, w_down, routes, gates
):
    ctx_count = lax.axis_size("ctx")
    lane_count = lax.axis_size("exp")
    groups = ctx_count // PARTS_SIZE
    experts = groups * lane_count
    local_rows = routes.shape[0]
    capacity = min(local_rows, 2 * ((local_rows * TOPK + experts - 1) // experts))
    scale = HEAD_SIZE ** (-0.5)
    rows_ctx = queries.shape[0]
    heads_per_device = queries.shape[1] // HEAD_SIZE
    key_value_head = lax.axis_index("exp") * heads_per_device // (QUERY_HEADS // KEY_VALUE_HEADS)
    key_head = lax.dynamic_slice_in_dim(keys, key_value_head * HEAD_SIZE, HEAD_SIZE, 1)
    value_head = lax.dynamic_slice_in_dim(values, key_value_head * HEAD_SIZE, HEAD_SIZE, 1)
    query_rows = queries.reshape(rows_ctx, heads_per_device, HEAD_SIZE)
    query_pos = lax.axis_index("ctx") * rows_ctx + jnp.arange(rows_ctx, dtype=jnp.int32)
    highest = jnp.full((rows_ctx, heads_per_device), -1e30, jnp.float32)
    key_piece = lax.all_gather(key_head, "ctx", axis=0, tiled=True)
    value_piece = lax.all_gather(value_head, "ctx", axis=0, tiled=True)
    scores = (
        jnp.einsum("qhd,kd->qhk", query_rows, key_piece, preferred_element_type=jnp.float32) * scale
    )
    key_pos = jnp.arange(key_piece.shape[0], dtype=jnp.int32)
    visible = (key_pos[None, :] <= query_pos[:, None])[:, None, :]
    scores = jnp.where(visible, scores, -1e30)
    peak = jnp.maximum(highest, jnp.max(scores, axis=-1))
    weights = jnp.where(visible, jnp.exp(scores - peak[..., None]), 0.0)
    totals = jnp.sum(weights, axis=-1)
    accumulated = jnp.einsum(
        "qhk,kd->qhd", weights.astype(jnp.bfloat16), value_piece, preferred_element_type=jnp.float32
    )
    highest, totals, accumulated = (peak, totals, accumulated)
    attention = (
        (accumulated / totals[..., None])
        .reshape(rows_ctx, heads_per_device * HEAD_SIZE)
        .astype(jnp.bfloat16)
    )
    partial_sums = jnp.dot(
        attention,
        lax.all_gather(out_weight, "ctx", axis=1, tiled=True),
        preferred_element_type=jnp.float32,
    )
    projected = lax.psum_scatter(
        partial_sums.astype(jnp.bfloat16), "exp", scatter_dimension=0, tiled=True
    ).astype(jnp.float32)
    residual = hidden.astype(jnp.float32) + projected
    attended = residual.astype(jnp.bfloat16)
    mean_square = jnp.mean(residual * residual, axis=-1, keepdims=True)
    normed = (residual * lax.rsqrt(mean_square + 1e-06) * norm_gain).astype(jnp.bfloat16)
    flat_routes = routes.reshape(-1)
    expert_ids = jnp.arange(experts, dtype=jnp.int32)
    onehot = (flat_routes[:, None] == expert_ids[None, :]).astype(jnp.int32)
    earlier = jnp.cumsum(onehot, axis=0) - onehot
    slot_index = jnp.sum(earlier * onehot, axis=1)
    position = flat_routes * capacity + slot_index
    spread_table = (
        jnp.arange(experts * capacity, dtype=jnp.int32)[:, None] == position[None, :]
    ).astype(jnp.bfloat16)
    repeated = jnp.repeat(normed, TOPK, axis=0)
    outbox = jnp.dot(spread_table, repeated, preferred_element_type=jnp.float32).astype(
        jnp.bfloat16
    )
    copies = jnp.broadcast_to(
        outbox.reshape(1, groups, lane_count, capacity, D),
        (PARTS_SIZE, groups, lane_count, capacity, D),
    ).reshape(ctx_count, lane_count, capacity, D)
    inbound = lax.all_to_all(
        lax.all_to_all(copies, "ctx", split_axis=0, concat_axis=0, tiled=True),
        "exp",
        split_axis=1,
        concat_axis=1,
        tiled=True,
    )
    row_block = inbound.reshape(-1, D)
    gate_h = jnp.dot(row_block, w_gate[0], preferred_element_type=jnp.float32)
    up_h = jnp.dot(row_block, w_up[0], preferred_element_type=jnp.float32)
    inner = (jax.nn.silu(gate_h) * up_h).astype(jnp.bfloat16)
    expert_out = jnp.dot(inner, w_down[0], preferred_element_type=jnp.float32).astype(jnp.bfloat16)
    partial_value = lax.all_to_all(
        lax.all_to_all(
            expert_out.reshape(inbound.shape), "exp", split_axis=1, concat_axis=1, tiled=True
        ),
        "ctx",
        split_axis=0,
        concat_axis=0,
        tiled=True,
    )
    returned = jnp.sum(
        partial_value.astype(jnp.float32).reshape(PARTS_SIZE, experts, capacity, D), axis=0
    ).reshape(experts * capacity, D)
    gathered = jnp.take(returned, position, axis=0)
    weighted = gathered * gates.reshape(-1)[:, None]
    moe = jnp.sum(weighted.reshape(local_rows, TOPK, D), axis=1)
    mixed = (residual + moe).astype(jnp.bfloat16)
    return (attended, mixed)


def solution(mesh):
    return jax.shard_map(
        on_device,
        mesh=mesh,
        in_specs=(
            P(("ctx", "exp"), None),
            P("ctx", "exp"),
            P("ctx", None),
            P("ctx", None),
            P("exp", "ctx"),
            P(),
            P(("ctx", "exp"), None, None),
            P(("ctx", "exp"), None, None),
            P(("ctx", "exp"), None, None),
            P(("ctx", "exp"), None),
            P(("ctx", "exp"), None),
        ),
        out_specs=(P(("ctx", "exp"), None), P(("ctx", "exp"), None)),
        check_vma=False,
    )
```

profile of v0, /device:TPU:2, one launch (start us, length us, event | category | flops | bytes accessed | tf_op | source)
XLA Modules:
  0.0 566.3 jit_solution(15155196866765272245)
XLA Ops:
  9.6 53.1 %all_gather.9 = bf16[2048,128]{1,0:T(8,128)(2,1)S(1)} all-gather(bf16[64,128]{1,0:T(8,128)(2,1)S(1)} %constant_dynamic-slice_fusion.1), channel_id=1, replica_groups=mesh['ctx'=32,'exp'=8] {'ctx'}, dimensions={0}, use_global_device_ids=true | all-gather | bytes 540672 | tf_op jit(solution)/shard_map/all_gather | solution.py:32
  62.6 48.5 %all_gather.10 = bf16[2048,128]{1,0:T(8,128)(2,1)S(1)} all-gather(bf16[64,128]{1,0:T(8,128)(2,1)S(1)} %constant_dynamic-slice_fusion), channel_id=1, replica_groups=mesh['ctx'=32,'exp'=8] {'ctx'}, dimensions={0}, use_global_device_ids=true | all-gather | bytes 540672 | tf_op jit(solution)/shard_map/all_gather | solution.py:33
  113.9 3.8 convolution_convert_fusion.2
  118.2 27.1 %reduce-scatter.2.cloned.1.call-done = bf16[8,4096]{1,0:T(8,128)(2,1)} async-done(((bf16[64,4096]{1,0:T(8,128)(2,1)}), bf16[8,4096]{1,0:T(8,128)(2,1)}) %reduce-scatter.2.cloned.1.call-update) | async-done | bytes 65552 | tf_op jit(solution)/shard_map/reduce_scatter | solution.py:57
  148.7 2.5 broadcast_in_dim.57
  151.2 7.6 %broadcast_in_dim.58 = bf16[4,8,8,2,4096]{4,3,2,1,0:T(2,128)(2,1)} broadcast(bf16[8,8,2,4096]{3,2,1,0:T(2,128)(2,1)} %broadcast_in_dim.57), dimensions={1,2,3,4} | broadcast | bytes 5242880 | tf_op jit(solution)/shard_map/broadcast_in_dim | solution.py:77
  158.8 104.9 %all_to_all.20 = bf16[32,8,2,4096]{3,2,1,0:T(2,128)(2,1)} all-to-all(bf16[32,8,2,4096]{3,2,1,0:T(2,128)(2,1)} %bitcast.64), channel_id=1, replica_groups=mesh['ctx'=32,'exp'=8] {'ctx'}, dimensions={0} | all-to-all | bytes 8388608 | tf_op jit(solution)/shard_map/all_to_all | solution.py:82
  263.7 9.9 %copy.28 = bf16[32,8,2,4096]{3,2,0,1:T(2,128)(2,1)} copy(bf16[32,8,2,4096]{3,2,1,0:T(2,128)(2,1)} %all_to_all.20) | data formatting | bytes 8388608 | tf_op jit(solution)/shard_map/all_to_all | solution.py:82
  273.6 55.6 %all_to_all.21 = bf16[32,8,2,4096]{3,2,0,1:T(2,128)(2,1)} all-to-all(bf16[32,8,2,4096]{3,2,0,1:T(2,128)(2,1)} %copy.28), channel_id=1, replica_groups=mesh['ctx'=32,'exp'=8] {'exp'}, dimensions={1} | all-to-all | bytes 8388608 | tf_op jit(solution)/shard_map/all_to_all | solution.py:81
  329.2 10.1 %copy.29 = bf16[32,8,2,4096]{3,2,1,0:T(2,128)(2,1)} copy(bf16[32,8,2,4096]{3,2,0,1:T(2,128)(2,1)} %all_to_all.21) | data formatting | bytes 8388608 | tf_op jit(solution)/shard_map/all_to_all | solution.py:81
  339.3 7.2 %reshape.130 = bf16[512,4096]{1,0:T(8,128)(2,1)} reshape(bf16[32,8,2,4096]{3,2,1,0:T(2,128)(2,1)} %copy.29) | data formatting | bytes 8388608 | tf_op jit(solution)/shard_map/reshape | solution.py:88
  346.5 6.4 %fusion.3 = f32[512,384]{1,0:T(8,128)} fusion(bf16[512,4096]{1,0:T(8,128)(2,1)} %reshape.130, bf16[1,4096,384]{2,1,0:T(8,128)(2,1)} %param.17), kind=kOutput, calls=%fused_computation.8 | convolution fusion | flops 1610612736 | bytes 8126464 | tf_op jit(solution)/shard_map/dot_general | solution.py:89
  353.0 9.8 %convolution_convert_fusion = bf16[512,4096]{1,0:T(8,128)(2,1)} fusion(bf16[1,384,4096]{2,1,0:T(8,128)(2,1)S(1)} %copy-done, bf16[512,4096]{1,0:T(8,128)(2,1)} %reshape.130, bf16[1,4096,384]{2,1,0:T(8,128)(2,1)} %param.18, f32[512,384]{1,0:T(8,128)} %fusion.3), kind=kOutput, calls=%fused_computation.2 | convolution fusion | flops 3224502272 | bytes 15466496 | tf_op jit(solution)/shard_map/dot_general | solution.py:92
  362.7 7.6 %reshape.131 = bf16[32,8,2,4096]{3,2,1,0:T(2,128)(2,1)} reshape(bf16[512,4096]{1,0:T(8,128)(2,1)} %convolution_convert_fusion) | data formatting | bytes 8388608 | tf_op jit(solution)/shard_map/reshape | solution.py:95
  370.4 9.9 %copy.30 = bf16[32,8,2,4096]{3,2,0,1:T(2,128)(2,1)} copy(bf16[32,8,2,4096]{3,2,1,0:T(2,128)(2,1)} %reshape.131) | data formatting | bytes 8388608 | tf_op jit(solution)/shard_map/reshape | solution.py:95
  380.3 53.9 %all_to_all.22 = bf16[32,8,2,4096]{3,2,0,1:T(2,128)(2,1)S(1)} all-to-all(bf16[32,8,2,4096]{3,2,0,1:T(2,128)(2,1)} %copy.30), channel_id=1, replica_groups=mesh['ctx'=32,'exp'=8] {'exp'}, dimensions={1} | all-to-all | bytes 8388608 | tf_op jit(solution)/shard_map/all_to_all | solution.py:94
  434.2 6.5 %copy.31 = bf16[32,8,2,4096]{3,1,2,0:T(8,128)(2,1)} copy(bf16[32,8,2,4096]{3,2,0,1:T(2,128)(2,1)S(1)} %all_to_all.22) | data formatting | bytes 8388608 | tf_op jit(solution)/shard_map/all_to_all | solution.py:94
  440.7 6.1 %all-to-all-start.3 = ((bf16[32,8,2,4096]{3,1,2,0:T(8,128)(2,1)}), bf16[32,8,2,4096]{3,1,2,0:T(8,128)(2,1)}, u32[]{:S(2)}, u32[]{:S(2)}) async-start(bf16[32,8,2,4096]{3,1,2,0:T(8,128)(2,1)} %copy.31), calls=%async_computation.4 | async-start | bytes 8388608 | tf_op jit(solution)/shard_map/all_to_all | solution.py:93
  447.0 96.2 %all-to-all-done.3 = bf16[32,8,2,4096]{3,1,2,0:T(8,128)(2,1)} async-done(((bf16[32,8,2,4096]{3,1,2,0:T(8,128)(2,1)}), bf16[32,8,2,4096]{3,1,2,0:T(8,128)(2,1)}, u32[]{:S(2)}, u32[]{:S(2)}) %all-to-all-start.3) | async-done | bytes 4194336 | tf_op jit(solution)/shard_map/all_to_all | solution.py:93
  543.2 2.5 copy.32
  546.5 2.9 copy.33
  549.4 3.7 reshape.134
  553.1 4.0 gather_fusion
  557.2 1.6 fusion.19
  (44 shorter events, 10.5 us)
Async XLA Ops:
  7.2 345.8 %copy-start = (bf16[1,384,4096]{2,1,0:T(8,128)(2,1)S(1)}, bf16[1,384,4096]{2,1,0:T(8,128)(2,1)}, u32[]{:S(2)}) copy-start(bf16[1,384,4096]{2,1,0:T(8,128)(2,1)} %param.19) | copy-start | bytes 9437188
  7.2 106.7 %all-gather.2.cloned.1.call-start = ((), (), s32[]{:S(2)}) async-start(), calls=%async_computation.5 | async-start | bytes 4325376 | tf_op jit(solution)/shard_map/all_gather | solution.py:54
  7.9 137.4 %reduce-scatter.2.cloned.1.call-start = ((), (), s32[]{:S(2)}) async-start(), calls=%async_computation.6 | async-start | bytes 589824 | tf_op jit(solution)/shard_map/reduce_scatter | solution.py:57
  113.8 3.9 copy-start.4
  113.8 31.5 %copy-start.2 = (bf16[8,4096]{1,0:T(8,128)(2,1)S(1)}, bf16[8,4096]{1,0:T(8,128)(2,1)}, u32[]{:S(2)}) copy-start(bf16[8,4096]{1,0:T(8,128)(2,1)} %param.11) | copy-start | bytes 196612
  113.8 32.5 %copy-start.5 = (f32[4096]{0:T(1024)S(1)}, f32[4096]{0:T(1024)}, u32[]{:S(2)}) copy-start(f32[4096]{0:T(1024)} %param.16) | copy-start | bytes 49156
  440.7 102.5 %all-to-all-start.3 = ((bf16[32,8,2,4096]{3,1,2,0:T(8,128)(2,1)}), bf16[32,8,2,4096]{3,1,2,0:T(8,128)(2,1)}, u32[]{:S(2)}, u32[]{:S(2)}) async-start(bf16[32,8,2,4096]{3,1,2,0:T(8,128)(2,1)} %copy.31), calls=%async_computation.4 | async-start | bytes 8388608 | tf_op jit(solution)/shard_map/all_to_all | solution.py:93
  553.1 4.1 copy-start.6
  553.1 5.7 %copy-start.3 = (bf16[8,4096]{1,0:T(8,128)(2,1)S(1)}, bf16[8,4096]{1,0:T(8,128)(2,1)}, u32[]{:S(2)}) copy-start(bf16[8,4096]{1,0:T(8,128)(2,1)} %reduce-scatter.2.cloned.1.call-done) | copy-start | bytes 196612
  553.1 6.4 %copy-start.1 = (bf16[1,384,4096]{2,1,0:T(8,128)(2,1)S(1)}, bf16[1,384,4096]{2,1,0:T(8,128)(2,1)}, u32[]{:S(2)}) copy-start(bf16[1,384,4096]{2,1,0:T(8,128)(2,1)} %param.19) | copy-start | bytes 9437188
Sparse Core Ops, SparseCore 0:
  10.5 88.1 all-gather.1
  117.8 27.4 reduce-scatter.1
where the time goes:
time: 567 us; the launch traced here: 566 us
  blocking collectives  316 us (56%)
  waiting for transfers between devices  124 us (22%)
  local copies, waits for them, and re-layouts  76.4 us (13%)
  matrix products  23.4 us (4%)
  between operations  14.2 us (3%)
  starting transfers between devices  6.2 us (1%)
  other arithmetic  6.07 us (1%)
    all_to_all x1, blocking collectives, on_device(): lax.all_to_all(copies, 'ctx', split_axis=0, concat_axis=0, tiled=True)  105 us
    all_to_all x1, waiting for transfers between devices, on_device(): lax.all_to_all(lax.all_to_all(expert_out.reshape(inbound.shape), 'exp', s...  96.2 us
    all_to_all x1, blocking collectives, on_device(): lax.all_to_all(lax.all_to_all(copies, 'ctx', split_axis=0, concat_axis=0,...  55.6 us
    all_to_all x1, blocking collectives, on_device(): lax.all_to_all(expert_out.reshape(inbound.shape), 'exp', split_axis=1, co...  53.9 us
    all_gather x1, blocking collectives, on_device(): key_piece = lax.all_gather(key_head, 'ctx', axis=0, tiled=True)  53.1 us
    all_gather x1, blocking collectives, on_device(): value_piece = lax.all_gather(value_head, 'ctx', axis=0, tiled=True)  48.5 us
    reduce_scatter x1, waiting for transfers between devices, on_device(): lax.psum_scatter(partial_sums.astype(jnp.bfloat16), 'exp', scatter_dimens...  27.1 us
    reshape x2, local copies, waits for them, and re-layouts, on_device(): expert_out.reshape(inbound.shape)  17.6 us
  transfers between devices with their start and end apart: 3, of which 2 were waited for; matrix products, arithmetic and copies ran while one was open for 1% of the time, Pallas kernels for 0%

commit v1 on v0

v1 whole, which is shorter than its diff:
```python
import jax
import jax.numpy as jnp
from jax import lax
from jax.sharding import Mesh
from jax.sharding import PartitionSpec as P

D = 4096
HEAD_SIZE = 128
QUERY_HEADS = 32
KEY_VALUE_HEADS = 2
TOPK = 8
MOST = 2
Y, Z, X, CORE = 4, 8, 4, 2
CTX = ("y", "z")
EXP = ("x", "core")
LANES = X * CORE
BF16 = jnp.bfloat16
F32 = jnp.float32


def spread(block, axes, count):
    return lax.all_to_all(
        jnp.broadcast_to(block[None], (count,) + block.shape), axes, 0, 0, tiled=True
    )


def swap(blocks, axes):
    return lax.all_to_all(blocks, axes, 0, 0, tiled=True)


def shift(block, step):
    return lax.ppermute(block, "y", [(i, (i + step) % Y) for i in range(Y)])


def on_device(
    hidden, queries, keys, values, out_weight, norm_gain, w_gate, w_up, w_down, routes, gates
):
    rows_ctx = queries.shape[0]
    heads = queries.shape[1] // HEAD_SIZE
    rows = routes.shape[0]
    lane = lax.axis_index(EXP)
    ctx = lax.axis_index(CTX)
    group = lax.axis_index("z")
    scale = HEAD_SIZE ** (-0.5)

    weight_piece = lax.all_gather(out_weight, "z", axis=0, tiled=False)

    table = jnp.concatenate([routes.astype(F32), gates], axis=1)
    table = spread(table, "z", Z).reshape(Z, rows, 2 * TOPK)
    routes_z = table[..., :TOPK].astype(jnp.int32)
    gates_z = table[..., TOPK:]
    own = group * LANES + jnp.arange(LANES, dtype=jnp.int32)
    named = routes_z[:, :, :, None] == own
    hit = jnp.any(named, axis=2)
    gate = jnp.sum(jnp.where(named, gates_z[..., None], 0.0), axis=2)
    earlier = jnp.cumsum(hit.astype(jnp.int32), axis=1) - hit.astype(jnp.int32)
    slots = jnp.arange(MOST, dtype=jnp.int32)
    chosen = hit[..., None] & (earlier[..., None] == slots)
    same = jnp.eye(Z, dtype=bool)
    pick = chosen.transpose(2, 0, 3, 1)[:, :, :, None, :] & same[None, :, None, :, None]
    pick = pick.reshape(LANES * Z * MOST, Z * rows)
    place = jnp.where(
        chosen.transpose(0, 1, 2, 3)[:, :, :, None, :] & same[:, None, None, :, None],
        gate[:, :, :, None, None],
        0.0,
    ).reshape(Z * rows, LANES * Z * MOST)
    place_high = place.astype(BF16)
    place_low = (place - place_high.astype(F32)).astype(BF16)

    head = lane * heads // (QUERY_HEADS // KEY_VALUE_HEADS)
    key_head = lax.dynamic_slice_in_dim(keys, head * HEAD_SIZE, HEAD_SIZE, 1)
    value_head = lax.dynamic_slice_in_dim(values, head * HEAD_SIZE, HEAD_SIZE, 1)
    both = spread(jnp.concatenate([key_head, value_head], axis=1), CTX, Y * Z)
    both = both.reshape(Y * Z * rows_ctx, 2 * HEAD_SIZE)
    key_piece, value_piece = both[:, :HEAD_SIZE], both[:, HEAD_SIZE:]
    query_rows = queries.reshape(rows_ctx, heads, HEAD_SIZE)
    query_pos = ctx * rows_ctx + jnp.arange(rows_ctx, dtype=jnp.int32)
    scores = jnp.einsum("qhd,kd->qhk", query_rows, key_piece, preferred_element_type=F32) * scale
    key_pos = jnp.arange(key_piece.shape[0], dtype=jnp.int32)
    visible = (key_pos[None, :] <= query_pos[:, None])[:, None, :]
    scores = jnp.where(visible, scores, -1e30)
    peak = jnp.max(scores, axis=-1)
    weights = jnp.where(visible, jnp.exp(scores - peak[..., None]), 0.0)
    totals = jnp.sum(weights, axis=-1)
    accumulated = jnp.einsum(
        "qhk,kd->qhd", weights.astype(BF16), value_piece, preferred_element_type=F32
    )
    attention = (
        (accumulated / totals[..., None]).reshape(rows_ctx, heads * HEAD_SIZE).astype(BF16)
    )

    attention_y = spread(attention, "y", Y).reshape(Y * rows_ctx, heads * HEAD_SIZE)
    partial = jnp.einsum("rf,zfc->rzc", attention_y, weight_piece, preferred_element_type=F32)
    width = D // Y
    partial = partial.astype(BF16).reshape(Y, LANES, rows, width).transpose(1, 0, 2, 3)
    summed = jnp.sum(swap(partial, EXP).astype(F32), axis=0).astype(BF16)
    projected = swap(summed, "y").transpose(1, 0, 2).reshape(rows, D)
    residual = hidden.astype(F32) + projected.astype(F32)
    attended = residual.astype(BF16)
    mean_square = jnp.mean(residual * residual, axis=-1, keepdims=True)
    normed = (residual * lax.rsqrt(mean_square + 1e-06) * norm_gain).astype(BF16)

    normed_z = spread(normed, "z", Z).reshape(Z * rows, D)
    outbox = jnp.dot(pick.astype(BF16), normed_z, preferred_element_type=F32).astype(BF16)
    inbox = swap(outbox.reshape(LANES, Z * MOST, D), EXP).reshape(LANES * Z * MOST, D)
    half = inbox.shape[0] // 2
    before = shift(inbox, 1)
    after = shift(inbox, -1)
    across = jnp.concatenate([shift(after[:half], -1), shift(before[half:], 1)], axis=0)

    def expert(block):
        gate_h = jnp.dot(block, w_gate[0], preferred_element_type=F32)
        up_h = jnp.dot(block, w_up[0], preferred_element_type=F32)
        inner = (jax.nn.silu(gate_h) * up_h).astype(BF16)
        return jnp.dot(inner, w_down[0], preferred_element_type=F32).astype(BF16)

    out_own = expert(inbox)
    out_near = expert(jnp.concatenate([before, after], axis=0))
    out_before, out_after = out_near[: 2 * half], out_near[2 * half :]
    out_across = expert(across)

    far_after = shift(out_across[:half], 1)
    far_before = shift(out_across[half:], -1)
    to_after = jnp.concatenate(
        [
            (out_after[:half].astype(F32) + far_after.astype(F32)).astype(BF16),
            out_after[half:],
        ],
        axis=0,
    )
    to_before = jnp.concatenate(
        [
            out_before[:half],
            (out_before[half:].astype(F32) + far_before.astype(F32)).astype(BF16),
        ],
        axis=0,
    )
    returned = (
        out_own.astype(F32) + shift(to_after, 1).astype(F32) + shift(to_before, -1).astype(F32)
    ).astype(BF16)
    back = swap(returned.reshape(LANES, Z * MOST, D), EXP).reshape(LANES * Z * MOST, D)
    moe_z = jnp.dot(place_high, back, preferred_element_type=F32) + jnp.dot(
        place_low, back, preferred_element_type=F32
    )
    moe = jnp.sum(swap(moe_z.astype(BF16).reshape(Z, rows, D), "z").astype(F32), axis=0)
    mixed = (residual + moe).astype(BF16)
    return (attended, mixed)


def solution(mesh):
    fine = Mesh(mesh.devices.reshape(Y, Z, X, CORE), CTX + EXP)
    every = CTX + EXP
    return jax.shard_map(
        on_device,
        mesh=fine,
        in_specs=(
            P(every, None),
            P(CTX, EXP),
            P(CTX, None),
            P(CTX, None),
            P(EXP, CTX),
            P(),
            P(every, None, None),
            P(every, None, None),
            P(every, None, None),
            P(every, None),
            P(every, None),
        ),
        out_specs=(P(every, None), P(every, None)),
        check_vma=False,
    )
```

time: 567 us -> 298 us (0.53)
  blocking collectives: 316 us -> 38.5 us
  local copies, waits for them, and re-layouts: 76.4 us -> 22.9 us
  starting transfers between devices: 6.2 us -> 48.4 us
  matrix products: 23.4 us -> 32.7 us
  waiting for transfers between devices: 124 us -> 133 us
    all_to_all x3 -> x2, blocking collectives: 214 us -> 38.5 us  [swap(): return lax.all_to_all(blocks, axes, 0, 0, tiled=True)]
    all_gather x2 -> x0, blocking collectives: 102 us -> none  [the longest x1 53.1 us: on_device(): key_piece = lax.all_gather(key_head, 'ctx', axis=0, tiled=True)]
    ppermute x0 -> x8, waiting for transfers between devices: none -> 53.6 us  [shift(): return lax.ppermute(block, 'y', [(i, (i + step) % Y) for i in range(Y)])]
    all_to_all x1 -> x7, starting transfers between devices: 6.12 us -> 37.5 us  [the longest x4 23.7 us: spread(): lax.all_to_all(jnp.broadcast_to(block[None], (count,) + block.shape), axe...]
    all_to_all x4 -> x1, local copies, waits for them, and re-layouts: 29 us -> 0.51 us  [spread(): lax.all_to_all(jnp.broadcast_to(block[None], (count,) + block.shape), axe...]
    reduce_scatter x1 -> x0, waiting for transfers between devices: 27.1 us -> none  [on_device(): lax.psum_scatter(partial_sums.astype(jnp.bfloat16), 'exp', scatter_dimens...]
    reshape x5 -> x1, local copies, waits for them, and re-layouts: 28.6 us -> 2.1 us  [on_device(): partial.astype(BF16).reshape(Y, LANES, rows, width).transpose(1, 0, 2, 3)]
    all_to_all x1 -> x7, waiting for transfers between devices: 96.2 us -> 72.9 us  [the longest x4 50.4 us: spread(): lax.all_to_all(jnp.broadcast_to(block[None], (count,) + block.shape), axe...]
  transfers between devices with their start and end apart: 3 -> 16, of which waited for: 2 -> 13; matrix products, arithmetic and copies ran while one was open for 1% -> 9% of each run, Pallas kernels for 0% -> 0%
where the time goes in v1:
time: 298 us; the launch traced here: 297 us
  waiting for transfers between devices  133 us (45%)
  starting transfers between devices  48.4 us (16%)
  blocking collectives  38.5 us (13%)
  matrix products  32.7 us (11%)
  local copies, waits for them, and re-layouts  22.9 us (8%)
  between operations  14.5 us (5%)
  other arithmetic  7.26 us (2%)
    ppermute x8, waiting for transfers between devices, shift(): return lax.ppermute(block, 'y', [(i, (i + step) % Y) for i in range(Y)])  53.6 us
    all_to_all x4, waiting for transfers between devices, spread(): lax.all_to_all(jnp.broadcast_to(block[None], (count,) + block.shape), axe...  50.4 us
    all_to_all x2, blocking collectives, swap(): return lax.all_to_all(blocks, axes, 0, 0, tiled=True)  38.5 us
    all_to_all x4, starting transfers between devices, spread(): lax.all_to_all(jnp.broadcast_to(block[None], (count,) + block.shape), axe...  23.7 us
    all_to_all x3, waiting for transfers between devices, swap(): return lax.all_to_all(blocks, axes, 0, 0, tiled=True)  22.5 us
    dot_general x3, matrix products, expert(): return jnp.dot(inner, w_down[0], preferred_element_type=F32).astype(BF16)  16.2 us
    all_to_all x3, starting transfers between devices, swap(): return lax.all_to_all(blocks, axes, 0, 0, tiled=True)  13.8 us
    ppermute x8, starting transfers between devices, shift(): return lax.ppermute(block, 'y', [(i, (i + step) % Y) for i in range(Y)])  10.8 us
  transfers between devices with their start and end apart: 16, of which 13 were waited for; matrix products, arithmetic and copies ran while one was open for 9% of the time, Pallas kernels for 0%

profile of v1, /device:TPU:2, one launch (start us, length us, event | category | flops | bytes accessed | tf_op | source)
XLA Modules:
  0.0 296.8 jit_solution(13782315839540007704)
XLA Ops:
  9.2 11.6 %all-to-all-start = ((bf16[32,64,256]{2,1,0:T(8,128)(2,1)}), bf16[32,64,256]{2,1,0:T(8,128)(2,1)}, u32[]{:S(2)}, u32[]{:S(2)}) async-start(bf16[32,64,256]{2,1,0:T(8,128)(2,1)} %broadcast_in_dim.51), calls=%async_computation | async-start | bytes 2097152 | tf_op jit(solution)/shard_map/all_to_all | solution.py:22
  21.7 29.9 %all-to-all-done = bf16[32,64,256]{2,1,0:T(8,128)(2,1)} async-done(((bf16[32,64,256]{2,1,0:T(8,128)(2,1)}), bf16[32,64,256]{2,1,0:T(8,128)(2,1)}, u32[]{:S(2)}, u32[]{:S(2)}) %all-to-all-start) | async-done | bytes 1048608 | tf_op jit(solution)/shard_map/all_to_all | solution.py:22
  51.7 3.1 %fusion.76 = (f32[64,4]{0,1:T(4,128)S(1)}, bf16[64,4,2048]{2,0,1:T(8,128)(2,1)}) fusion(pred[64,2048]{1,0:T(8,128)(4,1)S(1)} %iota_compare_fusion, bf16[2048,256]{1,0:T(8,128)(2,1)} %bitcast, bf16[64,512]{1,0:T(8,128)(2,1)S(1)} %copy-done.17), kind=kOutput, calls=%fused_computation.100 | convolution fusion | flops 137365504 | bytes 1901568 | tf_op jit(solution)/shard_map/sub | solution.py:83
  57.3 3.4 %all-to-all-start.1 = ((bf16[4,64,512]{2,1,0:T(8,128)(2,1)}), bf16[4,64,512]{2,1,0:T(8,128)(2,1)S(1)}, u32[]{:S(2)}, u32[]{:S(2)}) async-start(bf16[4,64,512]{2,1,0:T(8,128)(2,1)} %broadcast_in_dim.54), calls=%async_computation.1 | async-start | bytes 524288 | tf_op jit(solution)/shard_map/all_to_all | solution.py:22
  60.7 5.4 %all-gather.3.cloned.1.call-done = bf16[4096,128]{1,0:T(8,128)(2,1)} async-done(((bf16[512,128]{1,0:T(8,128)(2,1)}), bf16[4096,128]{1,0:T(8,128)(2,1)}) %all-gather.3.cloned.1.call-update) | async-done | bytes 1048592 | tf_op jit(solution)/shard_map/all_gather | solution.py:46
  74.1 4.8 %all-to-all-start.2 = ((bf16[8,4,8,1024]{3,2,1,0:T(8,128)(2,1)}), bf16[8,4,8,1024]{3,2,1,0:T(8,128)(2,1)}, u32[]{:S(2)}, u32[]{:S(2)}) async-start(bf16[8,4,8,1024]{3,2,1,0:T(8,128)(2,1)} %copy.28), calls=%async_computation.2 | async-start | bytes 1048576 | tf_op jit(solution)/shard_map/all_to_all | solution.py:28
  79.7 8.2 %all-to-all-done.2 = bf16[8,4,8,1024]{3,2,1,0:T(8,128)(2,1)} async-done(((bf16[8,4,8,1024]{3,2,1,0:T(8,128)(2,1)}), bf16[8,4,8,1024]{3,2,1,0:T(8,128)(2,1)}, u32[]{:S(2)}, u32[]{:S(2)}) %all-to-all-start.2) | async-done | bytes 524320 | tf_op jit(solution)/shard_map/all_to_all | solution.py:28
  87.9 4.6 %all-to-all-start.4 = ((f32[8,1,128]{2,1,0:T(1,128)}), f32[8,1,128]{2,1,0:T(1,128)S(1)}, u32[]{:S(2)}, u32[]{:S(2)}) async-start(f32[8,1,128]{2,1,0:T(1,128)} %reshape.183), calls=%async_computation.4 | async-start | bytes 8192 | tf_op jit(solution)/shard_map/all_to_all | solution.py:22
  94.3 5.8 %all-to-all-done.4 = f32[8,1,128]{2,1,0:T(1,128)S(1)} async-done(((f32[8,1,128]{2,1,0:T(1,128)}), f32[8,1,128]{2,1,0:T(1,128)S(1)}, u32[]{:S(2)}, u32[]{:S(2)}) %all-to-all-start.4) | async-done | bytes 4128 | tf_op jit(solution)/shard_map/all_to_all | solution.py:22
  100.1 3.3 %all-to-all-start.3 = ((bf16[4,8,1024]{2,1,0:T(8,128)(2,1)}), bf16[4,8,1024]{2,1,0:T(8,128)(2,1)S(1)}, u32[]{:S(2)}, u32[]{:S(2)}) async-start(bf16[4,8,1024]{2,1,0:T(8,128)(2,1)} %reduce_sum.49), calls=%async_computation.3 | async-start | bytes 131072 | tf_op jit(solution)/shard_map/all_to_all | solution.py:28
  104.7 4.2 %all-to-all-done.3 = bf16[4,8,1024]{2,1,0:T(8,128)(2,1)S(1)} async-done(((bf16[4,8,1024]{2,1,0:T(8,128)(2,1)}), bf16[4,8,1024]{2,1,0:T(8,128)(2,1)S(1)}, u32[]{:S(2)}, u32[]{:S(2)}) %all-to-all-start.3) | async-done | bytes 65568 | tf_op jit(solution)/shard_map/all_to_all | solution.py:28
  110.1 4.1 %all-to-all-start.5 = ((bf16[8,8,4096]{2,1,0:T(8,128)(2,1)}), bf16[8,8,4096]{2,1,0:T(8,128)(2,1)}, u32[]{:S(2)}, u32[]{:S(2)}) async-start(bf16[8,8,4096]{2,1,0:T(8,128)(2,1)} %broadcast_in_dim.94), calls=%async_computation.5 | async-start | bytes 1048576 | tf_op jit(solution)/shard_map/all_to_all | solution.py:22
  115.8 13.4 %all-to-all-done.5 = bf16[8,8,4096]{2,1,0:T(8,128)(2,1)} async-done(((bf16[8,8,4096]{2,1,0:T(8,128)(2,1)}), bf16[8,8,4096]{2,1,0:T(8,128)(2,1)}, u32[]{:S(2)}, u32[]{:S(2)}) %all-to-all-start.5) | async-done | bytes 524320 | tf_op jit(solution)/shard_map/all_to_all | solution.py:22
  130.7 18.5 %all_to_all.45 = bf16[8,16,4096]{2,1,0:T(8,128)(2,1)S(1)} all-to-all(bf16[8,16,4096]{2,1,0:T(8,128)(2,1)S(1)} %bitcast.131), channel_id=1, replica_groups=mesh['y'=4,'z'=8,'x'=4,'core'=2] {'x','core'}, dimensions={0} | all-to-all | bytes 2097152 | tf_op jit(solution)/shard_map/all_to_all | solution.py:28
  151.2 22.5 %collective-permute-done.1 = bf16[128,4096]{1,0:T(8,128)(2,1)S(1)} collective-permute-done((bf16[128,4096]{1,0:T(8,128)(2,1)S(1)}, bf16[128,4096]{1,0:T(8,128)(2,1)S(1)}, u32[]{:S(2)}, u32[]{:S(2)}) %collective-permute-start.1) | collective-permute-done | bytes 1048608 | tf_op jit(solution)/shard_map/ppermute | solution.py:32
  182.5 6.4 %convolution_convert_fusion = bf16[256,4096]{1,0:T(8,128)(2,1)} fusion(bf16[1,384,4096]{2,1,0:T(8,128)(2,1)S(1)} %copy-done, f32[256,384]{1,0:T(8,128)} %fusion.9, bf16[256,4096]{1,0:T(8,128)(2,1)} %copy-done.10, bf16[1,4096,384]{2,1,0:T(8,128)(2,1)} %param.17), kind=kOutput, calls=%fused_computation.1 | convolution fusion | flops 1612251136 | bytes 10878976 | tf_op jit(solution)/shard_map/dot_general | solution.py:115
  196.1 4.6 %convolution_convert_fusion.1 = bf16[128,4096]{1,0:T(8,128)(2,1)} fusion(bf16[1,384,4096]{2,1,0:T(8,128)(2,1)S(1)} %copy-done, f32[128,384]{1,0:T(8,128)S(1)} %fusion.7, bf16[128,4096]{1,0:T(8,128)(2,1)} %copy-done.5, bf16[1,4096,384]{2,1,0:T(8,128)(2,1)} %param.17), kind=kOutput, calls=%fused_computation.2 | convolution fusion | flops 806125568 | bytes 8585216 | tf_op jit(solution)/shard_map/dot_general | solution.py:115
  202.2 3.2 %collective-permute-start.6 = (bf16[64,4096]{1,0:T(8,128)(2,1)S(1)}, bf16[64,4096]{1,0:T(8,128)(2,1)S(1)}, u32[]{:S(2)}, u32[]{:S(2)}) collective-permute-start(bf16[64,4096]{1,0:T(8,128)(2,1)S(1)} %get-tuple-element.7), channel_id=1, source_target_pairs={{0,192},{64,0},{128,64},{192,128},{1,193},{65,1},{129,65},{193,129... | collective-permute-start | bytes 1572872 | tf_op jit(solution)/shard_map/ppermute | solution.py:32
  205.5 9.0 %collective-permute-done.4 = bf16[64,4096]{1,0:T(8,128)(2,1)S(1)} collective-permute-done((bf16[64,4096]{1,0:T(8,128)(2,1)S(1)}, bf16[64,4096]{1,0:T(8,128)(2,1)S(1)}, u32[]{:S(2)}, u32[]{:S(2)}) %collective-permute-start.4) | collective-permute-done | bytes 524320 | tf_op jit(solution)/shard_map/ppermute | solution.py:32
  218.9 17.8 %collective-permute-done.7 = bf16[128,4096]{1,0:T(8,128)(2,1)S(1)} collective-permute-done((bf16[128,4096]{1,0:T(8,128)(2,1)S(1)}, bf16[128,4096]{1,0:T(8,128)(2,1)S(1)}, u32[]{:S(2)}, u32[]{:S(2)}) %collective-permute-start.7) | collective-permute-done | bytes 1048608 | tf_op jit(solution)/shard_map/ppermute | solution.py:32
  240.4 5.2 %add_convert_fusion = bf16[128,4096]{1,0:T(8,128)(2,1)} fusion(bf16[128,4096]{1,0:T(8,128)(2,1)} %copy-done.7, bf16[128,4096]{1,0:T(8,128)(2,1)} %collective-permute-done.5, bf16[1,384,4096]{2,1,0:T(8,128)(2,1)S(1)} %copy-done, bf16[128,4096]{1,0:T(8,128)(2,1)} %bitcast.129, bf16[1,4096,384]{2,1,0:T(8,128)(2,1)} %param.18, f32[128,384]{1,0:T(8,128)S(1)} %fusion.17), kind=kOutput, calls=%fused_computation.30 | convolution fusion | flops 809271296 | bytes 10682368 | tf_op jit(solution)/shard_map/dot_general | solution.py:115
  245.7 5.7 %all-to-all-start.7 = ((bf16[8,16,4096]{2,1,0:T(8,128)(2,1)}), bf16[8,16,4096]{2,1,0:T(8,128)(2,1)}, u32[]{:S(2)}, u32[]{:S(2)}) async-start(bf16[8,16,4096]{2,1,0:T(8,128)(2,1)} %bitcast.132), calls=%async_computation.7 | async-start | bytes 2097152 | tf_op jit(solution)/shard_map/all_to_all | solution.py:28
  255.9 10.1 %all-to-all-done.7 = bf16[8,16,4096]{2,1,0:T(8,128)(2,1)} async-done(((bf16[8,16,4096]{2,1,0:T(8,128)(2,1)}), bf16[8,16,4096]{2,1,0:T(8,128)(2,1)}, u32[]{:S(2)}, u32[]{:S(2)}) %all-to-all-start.7) | async-done | bytes 1048608 | tf_op jit(solution)/shard_map/all_to_all | solution.py:28
  269.2 20.0 %all_to_all.46 = bf16[8,8,4096]{2,1,0:T(8,128)(2,1)S(1)} all-to-all(bf16[8,8,4096]{2,1,0:T(8,128)(2,1)S(1)} %fusion.3), channel_id=1, replica_groups=mesh['y'=4,'z'=8,'x'=4,'core'=2] {'z'}, dimensions={0} | all-to-all | bytes 1048576 | tf_op jit(solution)/shard_map/all_to_all | solution.py:28
  (118 shorter events, 57.3 us)
Async XLA Ops:
  7.2 175.3 %copy-start = (bf16[1,384,4096]{2,1,0:T(8,128)(2,1)S(1)}, bf16[1,384,4096]{2,1,0:T(8,128)(2,1)}, u32[]{:S(2)}) copy-start(bf16[1,384,4096]{2,1,0:T(8,128)(2,1)} %param.19) | copy-start | bytes 9437188
  7.2 44.5 %copy-start.17 = (bf16[64,512]{1,0:T(8,128)(2,1)S(1)}, bf16[64,512]{1,0:T(8,128)(2,1)}, u32[]{:S(2)}) copy-start(bf16[64,512]{1,0:T(8,128)(2,1)} %param.12) | copy-start | bytes 196612
  9.2 42.5 %all-to-all-start = ((bf16[32,64,256]{2,1,0:T(8,128)(2,1)}), bf16[32,64,256]{2,1,0:T(8,128)(2,1)}, u32[]{:S(2)}, u32[]{:S(2)}) async-start(bf16[32,64,256]{2,1,0:T(8,128)(2,1)} %broadcast_in_dim.51), calls=%async_computation | async-start | bytes 2097152 | tf_op jit(solution)/shard_map/all_to_all | solution.py:22
  20.8 45.3 %all-gather.3.cloned.1.call-start = ((), (), s32[]{:S(2)}) async-start(), calls=%async_computation.9 | async-start | bytes 1179648 | tf_op jit(solution)/shard_map/all_gather | solution.py:46
  57.3 10.1 %all-to-all-start.1 = ((bf16[4,64,512]{2,1,0:T(8,128)(2,1)}), bf16[4,64,512]{2,1,0:T(8,128)(2,1)S(1)}, u32[]{:S(2)}, u32[]{:S(2)}) async-start(bf16[4,64,512]{2,1,0:T(8,128)(2,1)} %broadcast_in_dim.54), calls=%async_computation.1 | async-start | bytes 524288 | tf_op jit(solution)/shard_map/all_to_all | solution.py:22
  70.1 38.9 %copy-start.8 = (bf16[8,4096]{1,0:T(8,128)(2,1)S(1)}, bf16[8,4096]{1,0:T(8,128)(2,1)}, u32[]{:S(2)}) copy-start(bf16[8,4096]{1,0:T(8,128)(2,1)} %param.11) | copy-start | bytes 196612
  70.1 39.0 %copy-start.13 = (f32[4096]{0:T(1024)S(1)}, f32[4096]{0:T(1024)}, u32[]{:S(2)}) copy-start(f32[4096]{0:T(1024)} %param.16) | copy-start | bytes 49156
  74.1 13.8 %all-to-all-start.2 = ((bf16[8,4,8,1024]{3,2,1,0:T(8,128)(2,1)}), bf16[8,4,8,1024]{3,2,1,0:T(8,128)(2,1)}, u32[]{:S(2)}, u32[]{:S(2)}) async-start(bf16[8,4,8,1024]{3,2,1,0:T(8,128)(2,1)} %copy.28), calls=%async_computation.2 | async-start | bytes 1048576 | tf_op jit(solution)/shard_map/all_to_all | solution.py:28
  87.9 12.2 %all-to-all-start.4 = ((f32[8,1,128]{2,1,0:T(1,128)}), f32[8,1,128]{2,1,0:T(1,128)S(1)}, u32[]{:S(2)}, u32[]{:S(2)}) async-start(f32[8,1,128]{2,1,0:T(1,128)} %reshape.183), calls=%async_computation.4 | async-start | bytes 8192 | tf_op jit(solution)/shard_map/all_to_all | solution.py:22
  92.5 11.5 %copy-start.14 = (pred[8,8]{0,1:T(8,128)(4,1)}, pred[8,8]{0,1:T(8,128)(4,1)S(1)}, u32[]{:S(2)}) copy-start(pred[8,8]{0,1:T(8,128)(4,1)S(1)} %iota_compare_fusion.2) | copy-start | bytes 196
  100.1 8.9 %all-to-all-start.3 = ((bf16[4,8,1024]{2,1,0:T(8,128)(2,1)}), bf16[4,8,1024]{2,1,0:T(8,128)(2,1)S(1)}, u32[]{:S(2)}, u32[]{:S(2)}) async-start(bf16[4,8,1024]{2,1,0:T(8,128)(2,1)} %reduce_sum.49), calls=%async_computation.3 | async-start | bytes 131072 | tf_op jit(solution)/shard_map/all_to_all | solution.py:28
  110.1 19.1 %all-to-all-start.5 = ((bf16[8,8,4096]{2,1,0:T(8,128)(2,1)}), bf16[8,8,4096]{2,1,0:T(8,128)(2,1)}, u32[]{:S(2)}, u32[]{:S(2)}) async-start(bf16[8,8,4096]{2,1,0:T(8,128)(2,1)} %broadcast_in_dim.94), calls=%async_computation.5 | async-start | bytes 1048576 | tf_op jit(solution)/shard_map/all_to_all | solution.py:22
  149.2 27.8 %copy-start.3 = (bf16[8,16,4096]{2,1,0:T(8,128)(2,1)}, bf16[8,16,4096]{2,1,0:T(8,128)(2,1)S(1)}, u32[]{:S(2)}) copy-start(bf16[8,16,4096]{2,1,0:T(8,128)(2,1)S(1)} %all_to_all.45) | copy-start | bytes 3145732
  149.2 24.5 %collective-permute-start.1 = (bf16[128,4096]{1,0:T(8,128)(2,1)S(1)}, bf16[128,4096]{1,0:T(8,128)(2,1)S(1)}, u32[]{:S(2)}, u32[]{:S(2)}) collective-permute-start(bf16[128,4096]{1,0:T(8,128)(2,1)S(1)} %bitcast.127), channel_id=1, source_target_pairs={{0,192},{64,0},{128,64},{192,128},{1,193},{65,1},{129,65},{193,129... | collective-permute-start | bytes 3145736 | tf_op jit(solution)/shard_map/ppermute | solution.py:32
  150.4 26.6 %collective-permute-start = (bf16[128,4096]{1,0:T(8,128)(2,1)S(1)}, bf16[128,4096]{1,0:T(8,128)(2,1)S(1)}, u32[]{:S(2)}, u32[]{:S(2)}) collective-permute-start(bf16[128,4096]{1,0:T(8,128)(2,1)S(1)} %bitcast.128), channel_id=1, source_target_pairs={{0,64},{64,128},{128,192},{192,0},{1,65},{65,129},{129,193},{193,1... | collective-permute-start | bytes 3145736 | tf_op jit(solution)/shard_map/ppermute | solution.py:32
  174.6 14.3 %collective-permute-start.2 = (bf16[64,4096]{1,0:T(8,128)(2,1)}, bf16[64,4096]{1,0:T(8,128)(2,1)}, u32[]{:S(2)}, u32[]{:S(2)}) collective-permute-start(bf16[64,4096]{1,0:T(8,128)(2,1)} %slice.59), channel_id=1, source_target_pairs={{0,192},{64,0},{128,64},{192,128},{1,193},{65,1},{129,65},{193,129... | collective-permute-start | bytes 1572872 | tf_op jit(solution)/shard_map/ppermute | solution.py:32
  177.8 13.6 %collective-permute-start.3 = (bf16[64,4096]{1,0:T(8,128)(2,1)}, bf16[64,4096]{1,0:T(8,128)(2,1)}, u32[]{:S(2)}, u32[]{:S(2)}) collective-permute-start(bf16[64,4096]{1,0:T(8,128)(2,1)} %slice.60), channel_id=1, source_target_pairs={{0,64},{64,128},{128,192},{192,0},{1,65},{65,129},{129,193},{193,1... | collective-permute-start | bytes 1572872 | tf_op jit(solution)/shard_map/ppermute | solution.py:32
  202.1 12.5 %collective-permute-start.4 = (bf16[64,4096]{1,0:T(8,128)(2,1)S(1)}, bf16[64,4096]{1,0:T(8,128)(2,1)S(1)}, u32[]{:S(2)}, u32[]{:S(2)}) collective-permute-start(bf16[64,4096]{1,0:T(8,128)(2,1)S(1)} %get-tuple-element.6), channel_id=1, source_target_pairs={{0,64},{64,128},{128,192},{192,0},{1,65},{65,129},{129,193},{193,1... | collective-permute-start | bytes 1572872 | tf_op jit(solution)/shard_map/ppermute | solution.py:32
  202.2 12.4 %collective-permute-start.6 = (bf16[64,4096]{1,0:T(8,128)(2,1)S(1)}, bf16[64,4096]{1,0:T(8,128)(2,1)S(1)}, u32[]{:S(2)}, u32[]{:S(2)}) collective-permute-start(bf16[64,4096]{1,0:T(8,128)(2,1)S(1)} %get-tuple-element.7), channel_id=1, source_target_pairs={{0,192},{64,0},{128,64},{192,128},{1,193},{65,1},{129,65},{193,129... | collective-permute-start | bytes 1572872 | tf_op jit(solution)/shard_map/ppermute | solution.py:32
  215.0 21.8 %collective-permute-start.7 = (bf16[128,4096]{1,0:T(8,128)(2,1)S(1)}, bf16[128,4096]{1,0:T(8,128)(2,1)S(1)}, u32[]{:S(2)}, u32[]{:S(2)}) collective-permute-start(bf16[128,4096]{1,0:T(8,128)(2,1)S(1)} %pad_maximum_fusion.1), channel_id=1, source_target_pairs={{0,192},{64,0},{128,64},{192,128},{1,193},{65,1},{129,65},{193,129... | collective-permute-start | bytes 3145736 | tf_op jit(solution)/shard_map/ppermute | solution.py:32
  218.1 22.3 %collective-permute-start.5 = (bf16[128,4096]{1,0:T(8,128)(2,1)S(1)}, bf16[128,4096]{1,0:T(8,128)(2,1)}, u32[]{:S(2)}, u32[]{:S(2)}) collective-permute-start(bf16[128,4096]{1,0:T(8,128)(2,1)S(1)} %pad_maximum_fusion), channel_id=1, source_target_pairs={{0,64},{64,128},{128,192},{192,0},{1,65},{65,129},{129,193},{193,1... | collective-permute-start | bytes 3145736 | tf_op jit(solution)/shard_map/ppermute | solution.py:32
  245.7 20.3 %all-to-all-start.7 = ((bf16[8,16,4096]{2,1,0:T(8,128)(2,1)}), bf16[8,16,4096]{2,1,0:T(8,128)(2,1)}, u32[]{:S(2)}, u32[]{:S(2)}) async-start(bf16[8,16,4096]{2,1,0:T(8,128)(2,1)} %bitcast.132), calls=%async_computation.7 | async-start | bytes 2097152 | tf_op jit(solution)/shard_map/all_to_all | solution.py:28
  255.9 11.7 %copy-start.12 = (bf16[64,128]{0,1:T(8,128)(2,1)S(1)}, bf16[64,128]{0,1:T(8,128)(2,1)}, u32[]{:S(2)}) copy-start(bf16[64,128]{0,1:T(8,128)(2,1)} %convert_element_type.194) | copy-start | bytes 49156
  267.6 21.7 %copy-start.9 = (bf16[8,4096]{1,0:T(8,128)(2,1)S(1)}, bf16[8,4096]{1,0:T(8,128)(2,1)}, u32[]{:S(2)}) copy-start(bf16[8,4096]{1,0:T(8,128)(2,1)} %param.11) | copy-start | bytes 196612
  (10 other events, 43.0 us)
Sparse Core Ops, SparseCore 0:
  23.5 42.6 all-gather.2

commit v2 on v1

v2 whole, which is shorter than its diff:
```python
import jax
import jax.numpy as jnp
from jax import lax
from jax.sharding import Mesh
from jax.sharding import PartitionSpec as P

D = 4096
HEAD_SIZE = 128
QUERY_HEADS = 32
KEY_VALUE_HEADS = 2
TOPK = 8
MOST = 2
Y, Z, X, CORE = 4, 8, 4, 2
CTX = ("y", "z")
EXP = ("x", "core")
LANES = X * CORE
BF16 = jnp.bfloat16
F32 = jnp.float32


def spread(block, axes, count):
    return lax.all_to_all(
        jnp.broadcast_to(block[None], (count,) + block.shape), axes, 0, 0, tiled=True
    )


def swap(blocks, axes):
    return lax.all_to_all(blocks, axes, 0, 0, tiled=True)


def shift(block, step):
    return lax.ppermute(block, "y", [(i, (i + step) % Y) for i in range(Y)])


def slots_of(routes):
    experts = jnp.arange(Z * LANES, dtype=jnp.int32)
    named = routes[..., None] == experts
    hit = jnp.any(named, axis=-2)
    count = hit.astype(jnp.int32)
    earlier = jnp.cumsum(count, axis=-2) - count
    chosen = hit[..., None] & (earlier[..., None] == jnp.arange(MOST, dtype=jnp.int32))
    return chosen, named


def on_device(
    hidden, queries, keys, values, out_weight, norm_gain, w_gate, w_up, w_down, routes, gates
):
    rows_ctx = queries.shape[0]
    heads = queries.shape[1] // HEAD_SIZE
    rows = routes.shape[0]
    piece = D // Z
    lane = lax.axis_index(EXP)
    ctx = lax.axis_index(CTX)
    core = lax.axis_index("core")
    scale = HEAD_SIZE ** (-0.5)

    weight_y = lax.all_gather(out_weight, "y", axis=0, tiled=False)
    weight_y = weight_y.transpose(1, 0, 2).reshape(out_weight.shape[0], piece)

    head = lane * heads // (QUERY_HEADS // KEY_VALUE_HEADS)
    half_ctx = rows_ctx // CORE
    key_head = lax.dynamic_slice(keys, (core * half_ctx, head * HEAD_SIZE), (half_ctx, HEAD_SIZE))
    value_head = lax.dynamic_slice(
        values, (core * half_ctx, head * HEAD_SIZE), (half_ctx, HEAD_SIZE)
    )
    mine = spread(jnp.concatenate([key_head, value_head], axis=1), CTX, Y * Z)
    mine = mine.reshape(Y * Z * half_ctx, 2 * HEAD_SIZE)
    other = lax.ppermute(mine, "core", [(0, 1), (1, 0)])
    query_rows = queries.reshape(rows_ctx * heads, HEAD_SIZE)
    query_pos = ctx * rows_ctx + jnp.arange(rows_ctx * heads, dtype=jnp.int32) // heads
    index = jnp.arange(Y * Z * half_ctx, dtype=jnp.int32)
    base_pos = (index // half_ctx) * rows_ctx + index % half_ctx
    scored = []
    for both, part in ((mine, core), (other, 1 - core)):
        scores = (
            jnp.einsum(
                "qd,kd->qk", query_rows, both[:, :HEAD_SIZE], preferred_element_type=F32
            )
            * scale
        )
        visible = (base_pos + part * half_ctx)[None, :] <= query_pos[:, None]
        scored.append((jnp.where(visible, scores, -1e30), visible, both[:, HEAD_SIZE:]))
    peak = jnp.maximum(jnp.max(scored[0][0], axis=-1), jnp.max(scored[1][0], axis=-1))
    totals, accumulated = 0.0, 0.0
    for scores, visible, value_piece in scored:
        weights = jnp.where(visible, jnp.exp(scores - peak[:, None]), 0.0)
        totals = totals + jnp.sum(weights, axis=-1)
        accumulated = accumulated + jnp.dot(
            weights.astype(BF16), value_piece, preferred_element_type=F32
        )
    attention = (
        (accumulated / totals[:, None]).reshape(rows_ctx, heads * HEAD_SIZE).astype(BF16)
    )

    hidden_z = hidden.reshape(rows, Y, Z, HEAD_SIZE).transpose(2, 0, 1, 3).reshape(Z, rows, piece)
    routes_wide = jnp.pad(routes.astype(BF16), ((0, 0), (0, piece - TOPK)))
    parcel = jnp.concatenate(
        [
            jnp.broadcast_to(attention[None], (Z, rows_ctx, piece)),
            hidden_z,
            jnp.broadcast_to(routes_wide[None], (Z, rows, piece)),
        ],
        axis=1,
    )
    parcel = swap(parcel, "z")
    attention_z = parcel[:, :rows_ctx].reshape(Z, LANES, rows, piece)
    hidden_c = parcel[:, rows_ctx : rows_ctx + rows].astype(F32)
    routes_c = parcel[:, rows_ctx + rows :, :TOPK].astype(jnp.int32)

    partial = jnp.einsum("zerf,fc->ezrc", attention_z, weight_y, preferred_element_type=F32)
    projected_c = jnp.sum(swap(partial.astype(BF16), EXP).astype(F32), axis=0)
    residual_c = (hidden_c + projected_c).astype(BF16).reshape(Z * rows, piece)

    chosen, _ = slots_of(routes_c)
    same = jnp.eye(Z, dtype=bool)
    pick = chosen.transpose(2, 0, 3, 1)[:, :, :, None, :] & same[None, :, None, :, None]
    pick = pick.reshape(Z * LANES * Z * MOST, Z * rows).astype(BF16)
    outbox = jnp.dot(pick, residual_c, preferred_element_type=F32).astype(BF16)
    inbox = swap(outbox.reshape(Z * LANES, Z * MOST, piece), ("z",) + EXP)
    inbox, projected_c = lax.optimization_barrier((inbox, projected_c.astype(BF16)))
    slots = LANES * Z * MOST
    inbox = inbox.reshape(Z, slots, Y, HEAD_SIZE).transpose(1, 2, 0, 3).reshape(slots, D)
    inbox = inbox.astype(F32)
    mean_square = jnp.mean(inbox * inbox, axis=-1, keepdims=True)
    inbox = (inbox * lax.rsqrt(mean_square + 1e-06) * norm_gain).astype(BF16)

    half = slots // 2
    before = shift(inbox, 1)
    after = shift(inbox, -1)
    across_low = shift(after[:half], -1)
    across_high = shift(before[half:], 1)

    projected = swap(projected_c, "z").reshape(Z, rows, Y, HEAD_SIZE)
    projected = projected.transpose(1, 2, 0, 3).reshape(rows, D)
    residual = hidden.astype(F32) + projected.astype(F32)
    attended = residual.astype(BF16)

    def expert(block):
        block, gate_w, up_w, down_w = lax.optimization_barrier(
            (block, w_gate[0], w_up[0], w_down[0])
        )
        gate_h = jnp.dot(block, gate_w, preferred_element_type=F32)
        up_h = jnp.dot(block, up_w, preferred_element_type=F32)
        inner = (jax.nn.silu(gate_h) * up_h).astype(BF16)
        return jnp.dot(inner, down_w, preferred_element_type=F32).astype(BF16)

    out_own = expert(inbox)
    out_before = expert(before)
    out_after = expert(after)
    home_low = shift(out_before[:half], -1)
    home_high = shift(out_after[half:], 1)
    out_across = expert(jnp.concatenate([across_low, across_high], axis=0))
    far_after = shift(out_across[:half], 1)
    far_before = shift(out_across[half:], -1)
    sum_low = shift((out_after[:half].astype(F32) + far_after.astype(F32)).astype(BF16), 1)
    sum_high = shift((out_before[half:].astype(F32) + far_before.astype(F32)).astype(BF16), -1)
    low = out_own[:half].astype(F32) + home_low.astype(F32) + sum_low.astype(F32)
    high = out_own[half:].astype(F32) + home_high.astype(F32) + sum_high.astype(F32)
    returned = jnp.concatenate([low.astype(BF16), high.astype(BF16)], axis=0)

    back = swap(returned.reshape(LANES * Z, MOST, D), EXP + ("z",)).reshape(slots, D)
    chosen_own, named = slots_of(routes)
    gate = jnp.sum(jnp.where(named, gates[..., None], 0.0), axis=1)
    place = jnp.where(chosen_own, gate[..., None], 0.0).reshape(rows, Z, LANES, MOST)
    place = place.transpose(0, 2, 1, 3).reshape(rows, slots)
    place_high = place.astype(BF16)
    place_low = (place - place_high.astype(F32)).astype(BF16)
    moe = jnp.dot(place_high, back, preferred_element_type=F32) + jnp.dot(
        place_low, back, preferred_element_type=F32
    )
    mixed = (residual + moe).astype(BF16)
    return (attended, mixed)


def solution(mesh):
    fine = Mesh(mesh.devices.reshape(Y, Z, X, CORE), CTX + EXP)
    every = CTX + EXP
    return jax.shard_map(
        on_device,
        mesh=fine,
        in_specs=(
            P(every, None),
            P(CTX, EXP),
            P(CTX, None),
            P(CTX, None),
            P(EXP, CTX),
            P(),
            P(every, None, None),
            P(every, None, None),
            P(every, None, None),
            P(every, None),
            P(every, None),
        ),
        out_specs=(P(every, None), P(every, None)),
        check_vma=False,
    )
```

time: 298 us -> 290 us (0.973)
  waiting for transfers between devices: 133 us -> 103 us
  other arithmetic: 7.26 us -> 21.5 us
  between operations: 14.5 us -> 1.06 us
  local copies, waits for them, and re-layouts: 22.9 us -> 36.2 us
  matrix products: 32.7 us -> 42.2 us
  starting transfers between devices: 48.4 us -> 43.1 us
    all_to_all x4 -> x0, waiting for transfers between devices: 50.4 us -> none  [spread(): lax.all_to_all(jnp.broadcast_to(block[None], (count,) + block.shape), axe...]
    all_to_all x3 -> x5, waiting for transfers between devices: 22.5 us -> 62.6 us  [swap(): return lax.all_to_all(blocks, axes, 0, 0, tiled=True)]
    all_to_all x4 -> x0, starting transfers between devices: 23.7 us -> none  [spread(): lax.all_to_all(jnp.broadcast_to(block[None], (count,) + block.shape), axe...]
    all_to_all x3 -> x5, starting transfers between devices: 13.8 us -> 29.6 us  [swap(): return lax.all_to_all(blocks, axes, 0, 0, tiled=True)]
    ppermute x8 -> x10, waiting for transfers between devices: 53.6 us -> 40.1 us  [shift(): return lax.ppermute(block, 'y', [(i, (i + step) % Y) for i in range(Y)])]
    all_gather x0 -> x1, blocking collectives: none -> 12.8 us  [on_device(): weight_y = lax.all_gather(out_weight, 'y', axis=0, tiled=False)]
    dot_general x9 -> x14, matrix products: 26.5 us -> 38.5 us  [the longest x4 18.5 us: expert(): return jnp.dot(inner, down_w, preferred_element_type=F32).astype(BF16)]
    all_to_all x2 -> x1, blocking collectives: 38.5 us -> 28.3 us  [spread(): lax.all_to_all(jnp.broadcast_to(block[None], (count,) + block.shape), axe...]
  transfers between devices with their start and end apart: 16 -> 16, of which waited for: 13 -> 8; matrix products, arithmetic and copies ran while one was open for 9% -> 24% of each run, Pallas kernels for 0% -> 0%
where the time goes in v2:
time: 290 us; the launch traced here: 288 us
  waiting for transfers between devices  103 us (36%)
  starting transfers between devices  43.1 us (15%)
  matrix products  42.2 us (15%)
  blocking collectives  41.1 us (14%)
  local copies, waits for them, and re-layouts  36.2 us (12%)
  other arithmetic  21.5 us (7%)
    all_to_all x5, waiting for transfers between devices, swap(): return lax.all_to_all(blocks, axes, 0, 0, tiled=True)  62.6 us
    ppermute x10, waiting for transfers between devices, shift(): return lax.ppermute(block, 'y', [(i, (i + step) % Y) for i in range(Y)])  40.1 us
    all_to_all x5, starting transfers between devices, swap(): return lax.all_to_all(blocks, axes, 0, 0, tiled=True)  29.6 us
    all_to_all x1, blocking collectives, spread(): lax.all_to_all(jnp.broadcast_to(block[None], (count,) + block.shape), axe...  28.3 us
    dot_general x4, matrix products, expert(): return jnp.dot(inner, down_w, preferred_element_type=F32).astype(BF16)  18.5 us
    ppermute x10, starting transfers between devices, shift(): return lax.ppermute(block, 'y', [(i, (i + step) % Y) for i in range(Y)])  13.5 us
    all_gather x1, blocking collectives, on_device(): weight_y = lax.all_gather(out_weight, 'y', axis=0, tiled=False)  12.8 us
    dot_general x4, matrix products, expert(): gate_h = jnp.dot(block, gate_w, preferred_element_type=F32)  10.5 us
  transfers between devices with their start and end apart: 16, of which 8 were waited for; matrix products, arithmetic and copies ran while one was open for 24% of the time, Pallas kernels for 0%

profile of v2, /device:TPU:2, one launch (start us, length us, event | category | flops | bytes accessed | tf_op | source)
XLA Modules:
  0.0 287.7 jit_solution(8015466031472551273)
XLA Ops:
  2.4 28.3 %all_to_all.30 = bf16[32,32,256]{2,1,0:T(8,128)(2,1)} all-to-all(bf16[32,32,256]{2,1,0:T(8,128)(2,1)S(1)} %broadcast_in_dim.35), channel_id=1, replica_groups=mesh['y'=4,'z'=8,'x'=4,'core'=2] {'y','z'}, dimensions={0} | all-to-all | bytes 1048576 | tf_op jit(solution)/shard_map/all_to_all | solution.py:22
  40.5 4.4 %all-to-all-start.1 = ((bf16[8,80,512]{2,1,0:T(8,128)(2,1)}), bf16[8,80,512]{2,1,0:T(8,128)(2,1)}, u32[]{:S(2)}, u32[]{:S(2)}) async-start(bf16[8,80,512]{2,1,0:T(8,128)(2,1)} %pad_maximum_fusion.2), calls=%async_computation.1 | async-start | bytes 1310720 | tf_op jit(solution)/shard_map/all_to_all | solution.py:28
  45.0 12.8 %all-gather = bf16[2048,128]{1,0:T(8,128)(2,1)S(1)} all-gather(bf16[512,128]{1,0:T(8,128)(2,1)S(1)} %copy-done.4), channel_id=2, replica_groups=mesh['y'=4,'z'=8,'x'=4,'core'=2] {'y'}, dimensions={0}, use_global_device_ids=true | all-gather | bytes 655360 | tf_op jit(solution)/shard_map/all_gather | solution.py:57
  61.1 5.0 %all-to-all-done.1 = bf16[8,80,512]{2,1,0:T(8,128)(2,1)} async-done(((bf16[8,80,512]{2,1,0:T(8,128)(2,1)}), bf16[8,80,512]{2,1,0:T(8,128)(2,1)}, u32[]{:S(2)}, u32[]{:S(2)}) %all-to-all-start.1) | async-done | bytes 655392 | tf_op jit(solution)/shard_map/all_to_all | solution.py:28
  68.5 4.8 %all-to-all-start.2 = ((bf16[8,8,8,512]{3,2,1,0:T(8,128)(2,1)}), bf16[8,8,8,512]{3,2,1,0:T(8,128)(2,1)}, u32[]{:S(2)}, u32[]{:S(2)}) async-start(bf16[8,8,8,512]{3,2,1,0:T(8,128)(2,1)} %copy.45), calls=%async_computation.2 | async-start | bytes 1048576 | tf_op jit(solution)/shard_map/all_to_all | solution.py:28
  85.7 6.3 %all-to-all-start.3 = ((bf16[64,16,512]{2,1,0:T(8,128)(2,1)}), bf16[64,16,512]{2,1,0:T(8,128)(2,1)}, u32[]{:S(2)}, u32[]{:S(2)}) async-start(bf16[64,16,512]{2,1,0:T(8,128)(2,1)} %bitcast.100), calls=%async_computation.3 | async-start | bytes 2097152 | tf_op jit(solution)/shard_map/all_to_all | solution.py:28
  92.7 28.2 %all-to-all-done.3 = bf16[64,16,512]{2,1,0:T(8,128)(2,1)} async-done(((bf16[64,16,512]{2,1,0:T(8,128)(2,1)}), bf16[64,16,512]{2,1,0:T(8,128)(2,1)}, u32[]{:S(2)}, u32[]{:S(2)}) %all-to-all-start.3) | async-done | bytes 1048608 | tf_op jit(solution)/shard_map/all_to_all | solution.py:28
  120.9 2.7 reshape.260
  125.2 2.9 %copy.50 = f32[128,4,8,128]{0,3,2,1:T(8,128)} copy(f32[128,4,8,128]{3,1,0,2:T(4,128)} %bitcast.99) | data formatting | bytes 4194304 | tf_op jit(solution)/shard_map/convert_element_type | solution.py:123
  134.1 3.5 %all-to-all-start.4 = ((bf16[8,8,512]{2,1,0:T(8,128)(2,1)}), bf16[8,8,512]{2,1,0:T(8,128)(2,1)S(1)}, u32[]{:S(2)}, u32[]{:S(2)}) async-start(bf16[8,8,512]{2,1,0:T(8,128)(2,1)} %convert_element_type.234), calls=%async_computation.4 | async-start | bytes 131072 | tf_op jit(solution)/shard_map/all_to_all | solution.py:28
  137.7 18.6 %collective-permute-done.1 = bf16[128,4096]{0,1:T(8,128)(2,1)} collective-permute-done((bf16[128,4096]{0,1:T(8,128)(2,1)}, bf16[128,4096]{0,1:T(8,128)(2,1)}, u32[]{:S(2)}, u32[]{:S(2)}) %collective-permute-start.1) | collective-permute-done | bytes 1048608 | tf_op jit(solution)/shard_map/ppermute | solution.py:32
  163.6 3.2 %collective-permute-start.4 = (bf16[64,4096]{1,0:T(8,128)(2,1)}, bf16[64,4096]{1,0:T(8,128)(2,1)}, u32[]{:S(2)}, u32[]{:S(2)}) collective-permute-start(bf16[64,4096]{1,0:T(8,128)(2,1)} %copy.51), channel_id=1, source_target_pairs={{0,192},{64,0},{128,64},{192,128},{1,193},{65,1},{129,65},{193,129... | collective-permute-start | bytes 1572872 | tf_op jit(solution)/shard_map/ppermute | solution.py:32
  166.8 3.0 %fusion.80 = f32[128,384]{1,0:T(8,128)S(1)} fusion(bf16[128,4096]{0,1:T(8,128)(2,1)} %collective-permute-done.1, bf16[4096,384]{1,0:T(8,128)(2,1)} %bitcast.95), kind=kOutput, calls=%fused_computation.130 | convolution fusion | flops 402653184 | bytes 4390912 | tf_op jit(solution)/shard_map/dot_general | solution.py:142
  169.8 4.6 %convolution_convert_fusion.2 = bf16[128,4096]{1,0:T(8,128)(2,1)} fusion(bf16[384,4096]{1,0:T(8,128)(2,1)S(1)} %bitcast.88, f32[128,384]{1,0:T(8,128)S(1)} %fusion.80, bf16[128,4096]{0,1:T(8,128)(2,1)} %collective-permute-done.1, bf16[4096,384]{1,0:T(8,128)(2,1)} %bitcast.91), kind=kOutput, calls=%fused_computation.2 | convolution fusion | flops 806125568 | bytes 8585216 | tf_op jit(solution)/shard_map/dot_general | solution.py:145
  182.7 4.6 %convolution_convert_fusion = bf16[128,4096]{1,0:T(8,128)(2,1)} fusion(bf16[384,4096]{1,0:T(8,128)(2,1)S(1)} %bitcast.90, bf16[128,4096]{1,0:T(8,128)(2,1)} %copy-done.2, bf16[4096,384]{1,0:T(8,128)(2,1)} %bitcast.92, f32[128,384]{1,0:T(8,128)S(1)} %fusion.82), kind=kOutput, calls=%fused_computation | convolution fusion | flops 806125568 | bytes 8585216 | tf_op jit(solution)/shard_map/dot_general | solution.py:145
  189.5 3.7 %collective-permute-start.9 = (bf16[64,4096]{1,0:T(8,128)(2,1)}, bf16[64,4096]{1,0:T(8,128)(2,1)}, u32[]{:S(2)}, u32[]{:S(2)}) collective-permute-start(bf16[64,4096]{1,0:T(8,128)(2,1)} %get-tuple-element.43), channel_id=1, source_target_pairs={{0,192},{64,0},{128,64},{192,128},{1,193},{65,1},{129,65},{193,129... | collective-permute-start | bytes 1572872 | tf_op jit(solution)/shard_map/ppermute | solution.py:32
  193.3 3.0 %fusion.81 = f32[128,384]{1,0:T(8,128)S(1)} fusion(bf16[128,4096]{0,1:T(8,128)(2,1)} %collective-permute-done.3, bf16[4096,384]{1,0:T(8,128)(2,1)} %bitcast.97), kind=kOutput, calls=%fused_computation.131 | convolution fusion | flops 402653184 | bytes 4390912 | tf_op jit(solution)/shard_map/dot_general | solution.py:142
  196.2 4.6 %convolution_convert_fusion.1 = bf16[128,4096]{1,0:T(8,128)(2,1)} fusion(bf16[384,4096]{1,0:T(8,128)(2,1)S(1)} %bitcast.89, f32[128,384]{1,0:T(8,128)S(1)} %fusion.81, bf16[128,4096]{0,1:T(8,128)(2,1)} %collective-permute-done.3, bf16[4096,384]{1,0:T(8,128)(2,1)} %bitcast.93), kind=kOutput, calls=%fused_computation.1 | convolution fusion | flops 806125568 | bytes 8585216 | tf_op jit(solution)/shard_map/dot_general | solution.py:145
  205.1 3.3 %collective-permute-start.10 = (bf16[64,4096]{1,0:T(8,128)(2,1)}, bf16[64,4096]{1,0:T(8,128)(2,1)}, u32[]{:S(2)}, u32[]{:S(2)}) collective-permute-start(bf16[64,4096]{1,0:T(8,128)(2,1)} %add_convert_fusion.1), channel_id=1, source_target_pairs={{0,192},{64,0},{128,64},{192,128},{1,193},{65,1},{129,65},{193,129... | collective-permute-start | bytes 1572872 | tf_op jit(solution)/shard_map/ppermute | solution.py:32
  208.3 15.8 %collective-permute-done.6 = bf16[64,4096]{1,0:T(8,128)(2,1)S(1)} collective-permute-done((bf16[64,4096]{1,0:T(8,128)(2,1)}, bf16[64,4096]{1,0:T(8,128)(2,1)S(1)}, u32[]{:S(2)}, u32[]{:S(2)}) %collective-permute-start.6) | collective-permute-done | bytes 524320 | tf_op jit(solution)/shard_map/ppermute | solution.py:32
  228.1 4.6 %convolution_convert_fusion.3 = bf16[128,4096]{1,0:T(8,128)(2,1)} fusion(bf16[384,4096]{1,0:T(8,128)(2,1)S(1)} %bitcast.87, bf16[128,4096]{0,1:T(8,128)(2,1)} %fusion.3, bf16[4096,384]{1,0:T(8,128)(2,1)} %bitcast.94, f32[128,384]{1,0:T(8,128)S(1)} %fusion.79), kind=kOutput, calls=%fused_computation.3 | convolution fusion | flops 806125568 | bytes 8585216 | tf_op jit(solution)/shard_map/dot_general | solution.py:145
  232.7 4.1 %collective-permute-done.7 = bf16[64,4096]{1,0:T(8,128)(2,1)} collective-permute-done((bf16[64,4096]{1,0:T(8,128)(2,1)}, bf16[64,4096]{1,0:T(8,128)(2,1)}, u32[]{:S(2)}, u32[]{:S(2)}) %collective-permute-start.7) | collective-permute-done | bytes 524320 | tf_op jit(solution)/shard_map/ppermute | solution.py:32
  242.8 10.5 %all-to-all-start.5 = ((bf16[64,2,4096]{2,1,0:T(2,128)(2,1)}), bf16[64,2,4096]{2,1,0:T(2,128)(2,1)}, u32[]{:S(2)}, u32[]{:S(2)}) async-start(bf16[64,2,4096]{2,1,0:T(2,128)(2,1)} %reshape.255), calls=%async_computation.5 | async-start | bytes 2097152 | tf_op jit(solution)/shard_map/all_to_all | solution.py:28
  255.0 26.7 %all-to-all-done.5 = bf16[64,2,4096]{2,1,0:T(2,128)(2,1)} async-done(((bf16[64,2,4096]{2,1,0:T(2,128)(2,1)}), bf16[64,2,4096]{2,1,0:T(2,128)(2,1)}, u32[]{:S(2)}, u32[]{:S(2)}) %all-to-all-start.5) | async-done | bytes 1048608 | tf_op jit(solution)/shard_map/all_to_all | solution.py:28
  (108 shorter events, 77.3 us)
Async XLA Ops:
  0.6 133.5 %copy-start = (bf16[1,384,4096]{2,1,0:T(8,128)(2,1)S(1)}, bf16[1,384,4096]{2,1,0:T(8,128)(2,1)}, u32[]{:S(2)}) copy-start(bf16[1,384,4096]{2,1,0:T(8,128)(2,1)} %param.19) | copy-start | bytes 9437188
  30.6 3.8 %collective-permute-start = (bf16[1024,256]{1,0:T(8,128)(2,1)}, bf16[1024,256]{1,0:T(8,128)(2,1)}, u32[]{:S(2)}, u32[]{:S(2)}) collective-permute-start(bf16[1024,256]{1,0:T(8,128)(2,1)} %bitcast), channel_id=1, source_target_pairs={{0,1},{1,0},{2,3},{3,2},{4,5},{5,4},{6,7},{7,6},{8,9},{9,8},{10,11... | collective-permute-start | bytes 1572872 | tf_op jit(solution)/shard_map/ppermute | solution.py:68
  37.9 7.0 %copy-start.4 = (bf16[512,128]{1,0:T(8,128)(2,1)S(1)}, bf16[512,128]{1,0:T(8,128)(2,1)}, u32[]{:S(2)}) copy-start(bf16[512,128]{1,0:T(8,128)(2,1)} %param.15) | copy-start | bytes 393220
  40.5 25.5 %all-to-all-start.1 = ((bf16[8,80,512]{2,1,0:T(8,128)(2,1)}), bf16[8,80,512]{2,1,0:T(8,128)(2,1)}, u32[]{:S(2)}, u32[]{:S(2)}) async-start(bf16[8,80,512]{2,1,0:T(8,128)(2,1)} %pad_maximum_fusion.2), calls=%async_computation.1 | async-start | bytes 1310720 | tf_op jit(solution)/shard_map/all_to_all | solution.py:28
  68.5 13.8 %all-to-all-start.2 = ((bf16[8,8,8,512]{3,2,1,0:T(8,128)(2,1)}), bf16[8,8,8,512]{3,2,1,0:T(8,128)(2,1)}, u32[]{:S(2)}, u32[]{:S(2)}) async-start(bf16[8,8,8,512]{3,2,1,0:T(8,128)(2,1)} %copy.45), calls=%async_computation.2 | async-start | bytes 1048576 | tf_op jit(solution)/shard_map/all_to_all | solution.py:28
  85.7 35.2 %all-to-all-start.3 = ((bf16[64,16,512]{2,1,0:T(8,128)(2,1)}), bf16[64,16,512]{2,1,0:T(8,128)(2,1)}, u32[]{:S(2)}, u32[]{:S(2)}) async-start(bf16[64,16,512]{2,1,0:T(8,128)(2,1)} %bitcast.100), calls=%async_computation.3 | async-start | bytes 2097152 | tf_op jit(solution)/shard_map/all_to_all | solution.py:28
  123.6 4.5 %copy-start.6 = (f32[4096]{0:T(1024)S(1)}, f32[4096]{0:T(1024)}, u32[]{:S(2)}) copy-start(f32[4096]{0:T(1024)} %param.16) | copy-start | bytes 49156
  130.9 25.4 %collective-permute-start.1 = (bf16[128,4096]{0,1:T(8,128)(2,1)}, bf16[128,4096]{0,1:T(8,128)(2,1)}, u32[]{:S(2)}, u32[]{:S(2)}) collective-permute-start(bf16[128,4096]{0,1:T(8,128)(2,1)} %fusion.3), channel_id=1, source_target_pairs={{0,64},{64,128},{128,192},{192,0},{1,65},{65,129},{129,193},{193,1... | collective-permute-start | bytes 3145736 | tf_op jit(solution)/shard_map/ppermute | solution.py:32
  131.5 29.7 %collective-permute-start.3 = (bf16[128,4096]{0,1:T(8,128)(2,1)}, bf16[128,4096]{0,1:T(8,128)(2,1)}, u32[]{:S(2)}, u32[]{:S(2)}) collective-permute-start(bf16[128,4096]{0,1:T(8,128)(2,1)} %fusion.3), channel_id=1, source_target_pairs={{0,192},{64,0},{128,64},{192,128},{1,193},{65,1},{129,65},{193,129... | collective-permute-start | bytes 3145736 | tf_op jit(solution)/shard_map/ppermute | solution.py:32
  134.1 108.7 %all-to-all-start.4 = ((bf16[8,8,512]{2,1,0:T(8,128)(2,1)}), bf16[8,8,512]{2,1,0:T(8,128)(2,1)S(1)}, u32[]{:S(2)}, u32[]{:S(2)}) async-start(bf16[8,8,512]{2,1,0:T(8,128)(2,1)} %convert_element_type.234), calls=%async_computation.4 | async-start | bytes 131072 | tf_op jit(solution)/shard_map/all_to_all | solution.py:28
  161.2 15.1 %collective-permute-start.5 = (bf16[64,4096]{1,0:T(8,128)(2,1)}, bf16[64,4096]{1,0:T(8,128)(2,1)}, u32[]{:S(2)}, u32[]{:S(2)}) collective-permute-start(bf16[64,4096]{1,0:T(8,128)(2,1)} %copy.52), channel_id=1, source_target_pairs={{0,64},{64,128},{128,192},{192,0},{1,65},{65,129},{129,193},{193,1... | collective-permute-start | bytes 1572872 | tf_op jit(solution)/shard_map/ppermute | solution.py:32
  163.6 14.2 %collective-permute-start.4 = (bf16[64,4096]{1,0:T(8,128)(2,1)}, bf16[64,4096]{1,0:T(8,128)(2,1)}, u32[]{:S(2)}, u32[]{:S(2)}) collective-permute-start(bf16[64,4096]{1,0:T(8,128)(2,1)} %copy.51), channel_id=1, source_target_pairs={{0,192},{64,0},{128,64},{192,128},{1,193},{65,1},{129,65},{193,129... | collective-permute-start | bytes 1572872 | tf_op jit(solution)/shard_map/ppermute | solution.py:32
  176.3 56.5 %collective-permute-start.2 = (bf16[64,4096]{1,0:T(8,128)(2,1)}, bf16[64,4096]{1,0:T(8,128)(2,1)}, u32[]{:S(2)}, u32[]{:S(2)}) collective-permute-start(bf16[64,4096]{1,0:T(8,128)(2,1)} %slice.76), channel_id=1, source_target_pairs={{0,192},{64,0},{128,64},{192,128},{1,193},{65,1},{129,65},{193,129... | collective-permute-start | bytes 1572872 | tf_op jit(solution)/shard_map/ppermute | solution.py:32
  179.0 1.0 copy-start.2
  189.5 13.4 %collective-permute-start.9 = (bf16[64,4096]{1,0:T(8,128)(2,1)}, bf16[64,4096]{1,0:T(8,128)(2,1)}, u32[]{:S(2)}, u32[]{:S(2)}) collective-permute-start(bf16[64,4096]{1,0:T(8,128)(2,1)} %get-tuple-element.43), channel_id=1, source_target_pairs={{0,192},{64,0},{128,64},{192,128},{1,193},{65,1},{129,65},{193,129... | collective-permute-start | bytes 1572872 | tf_op jit(solution)/shard_map/ppermute | solution.py:32
  200.9 25.3 %copy-start.1 = (bf16[1,4096,384]{2,1,0:T(8,128)(2,1)S(1)}, bf16[1,4096,384]{2,1,0:T(8,128)(2,1)}, u32[]{:S(2)}) copy-start(bf16[1,4096,384]{2,1,0:T(8,128)(2,1)} %param.17) | copy-start | bytes 9437188
  202.9 29.8 %collective-permute-start.8 = (bf16[64,4096]{1,0:T(8,128)(2,1)}, bf16[64,4096]{1,0:T(8,128)(2,1)}, u32[]{:S(2)}, u32[]{:S(2)}) collective-permute-start(bf16[64,4096]{1,0:T(8,128)(2,1)} %slice.82), channel_id=1, source_target_pairs={{0,64},{64,128},{128,192},{192,0},{1,65},{65,129},{129,193},{193,1... | collective-permute-start | bytes 1572872 | tf_op jit(solution)/shard_map/ppermute | solution.py:32
  202.9 21.2 %collective-permute-start.6 = (bf16[64,4096]{1,0:T(8,128)(2,1)}, bf16[64,4096]{1,0:T(8,128)(2,1)S(1)}, u32[]{:S(2)}, u32[]{:S(2)}) collective-permute-start(bf16[64,4096]{1,0:T(8,128)(2,1)} %get-tuple-element.42), channel_id=1, source_target_pairs={{0,64},{64,128},{128,192},{192,0},{1,65},{65,129},{129,193},{193,1... | collective-permute-start | bytes 1572872 | tf_op jit(solution)/shard_map/ppermute | solution.py:32
  205.1 27.7 %collective-permute-start.10 = (bf16[64,4096]{1,0:T(8,128)(2,1)}, bf16[64,4096]{1,0:T(8,128)(2,1)}, u32[]{:S(2)}, u32[]{:S(2)}) collective-permute-start(bf16[64,4096]{1,0:T(8,128)(2,1)} %add_convert_fusion.1), channel_id=1, source_target_pairs={{0,192},{64,0},{128,64},{192,128},{1,193},{65,1},{129,65},{193,129... | collective-permute-start | bytes 1572872 | tf_op jit(solution)/shard_map/ppermute | solution.py:32
  226.1 10.7 %collective-permute-start.7 = (bf16[64,4096]{1,0:T(8,128)(2,1)}, bf16[64,4096]{1,0:T(8,128)(2,1)}, u32[]{:S(2)}, u32[]{:S(2)}) collective-permute-start(bf16[64,4096]{1,0:T(8,128)(2,1)} %add_convert_fusion.3), channel_id=1, source_target_pairs={{0,64},{64,128},{128,192},{192,0},{1,65},{65,129},{129,193},{193,1... | collective-permute-start | bytes 1572872 | tf_op jit(solution)/shard_map/ppermute | solution.py:32
  239.2 14.2 %copy-start.5 = (s32[8,8]{1,0:T(8,128)S(1)}, s32[8,8]{1,0:T(8,128)}, u32[]{:S(2)}) copy-start(s32[8,8]{1,0:T(8,128)} %param.20) | copy-start | bytes 772
  239.2 14.7 %copy-start.7 = (f32[8,8]{1,0:T(8,128)S(1)}, f32[8,8]{1,0:T(8,128)}, u32[]{:S(2)}) copy-start(f32[8,8]{1,0:T(8,128)} %param.21) | copy-start | bytes 772
  239.2 15.2 %copy-start.3 = (bf16[8,4096]{1,0:T(8,128)(2,1)S(1)}, bf16[8,4096]{1,0:T(8,128)(2,1)}, u32[]{:S(2)}) copy-start(bf16[8,4096]{1,0:T(8,128)(2,1)} %param.11) | copy-start | bytes 196612
  242.8 39.0 %all-to-all-start.5 = ((bf16[64,2,4096]{2,1,0:T(2,128)(2,1)}), bf16[64,2,4096]{2,1,0:T(2,128)(2,1)}, u32[]{:S(2)}, u32[]{:S(2)}) async-start(bf16[64,2,4096]{2,1,0:T(2,128)(2,1)} %reshape.255), calls=%async_computation.5 | async-start | bytes 2097152 | tf_op jit(solution)/shard_map/all_to_all | solution.py:28

commit v3 on v2

--- a/solution.py
+++ b/solution.py
@@ -1,6 +1,8 @@
 import jax
 import jax.numpy as jnp
 from jax import lax
+from jax.experimental import pallas as pl
+from jax.experimental.pallas import tpu as pltpu
 from jax.sharding import Mesh
 from jax.sharding import PartitionSpec as P
 
@@ -32,6 +34,110 @@
     return lax.ppermute(block, "y", [(i, (i + step) % Y) for i in range(Y)])
 
 
+def norm_kernel(x_ref, gain_ref, low_ref, high_ref):
+    lanes = LANES // 2
+    rows, piece = lanes * x_ref.shape[1], x_ref.shape[2]
+    for part, out_ref in enumerate((low_ref, high_ref)):
+
+        def piece_of(i):
+            x = x_ref[i * LANES + part * lanes : i * LANES + (part + 1) * lanes]
+            return x.reshape(rows, piece).astype(F32)
+
+        square = jnp.zeros((rows, 1), F32)
+        for i in range(Z):
+            x = piece_of(i)
+            square = square + jnp.sum(x * x, axis=-1, keepdims=True)
+        factor = lax.rsqrt(square * (1.0 / D) + 1e-06)
+        for i in range(Z):
+            x = piece_of(i) * factor
+            for j in range(Y):
+                at = (j * Z + i) * HEAD_SIZE
+                out_ref[:, at : at + HEAD_SIZE] = (
+                    x[:, j * HEAD_SIZE : (j + 1) * HEAD_SIZE] * gain_ref[:, at : at + HEAD_SIZE]
+                ).astype(BF16)
+
+
+def normalise(inbox, gain):
+    rows = inbox.shape[0] * inbox.shape[1] // Z // 2
+    return pl.pallas_call(
+        norm_kernel,
+        out_shape=[jax.ShapeDtypeStruct((rows, D), BF16)] * 2,
+        in_specs=[pl.BlockSpec(memory_space=pltpu.VMEM)] * 2,
+        out_specs=[pl.BlockSpec(memory_space=pltpu.VMEM)] * 2,
+        compiler_params=pltpu.CompilerParams(vmem_limit_bytes=32 * 1024 * 1024),
+        cost_estimate=pl.CostEstimate(flops=6 * rows * D, bytes_accessed=8 * rows * D, transcendentals=0),
+    )(inbox, gain.reshape(1, D))
+
+
+STEPS = 4
+
+
+def expert_kernel(
+    low_ref, high_ref, gate_ref, up_ref, down_ref, out_low_ref, out_high_ref, gate_sum, up_sum, inner
+):
+    step = pl.program_id(0)
+    depth = gate_ref.shape[0]
+    rows = low_ref.shape[0]
+
+    @pl.when(step < STEPS)
+    def _():
+        columns = pl.ds(pl.multiple_of(step * depth, depth), depth)
+        x = jnp.concatenate([low_ref[:, columns], high_ref[:, columns]], axis=0)
+        gate_h = jnp.dot(x, gate_ref[...], preferred_element_type=F32)
+        up_h = jnp.dot(x, up_ref[...], preferred_element_type=F32)
+
+        @pl.when(step == 0)
+        def _():
+            gate_sum[...] = gate_h
+            up_sum[...] = up_h
+
+        @pl.when(step > 0)
+        def _():
+            gate_sum[...] += gate_h
+            up_sum[...] += up_h
+
+    @pl.when(step == STEPS - 1)
+    def _():
+        v = gate_sum[...]
+        inner[...] = (v / (1.0 + jnp.exp(-v)) * up_sum[...]).astype(BF16)
+
+    @pl.when(step >= STEPS)
+    def _():
+        out = jnp.dot(inner[...], down_ref[...], preferred_element_type=F32).astype(BF16)
+        out_low_ref[...] = out[:rows]
+        out_high_ref[...] = out[rows:]
+
+
+def expert(low, high, w_gate, w_up, w_down):
+    rows = low.shape[0]
+    width = w_gate.shape[1]
+    piece = D // STEPS
+    whole = pl.BlockSpec((rows, D), lambda i: (0, 0))
+    into = pl.BlockSpec((piece, width), lambda i: (jnp.minimum(i, STEPS - 1), 0))
+    out_of = pl.BlockSpec((width, piece), lambda i: (0, jnp.maximum(i - STEPS, 0)))
+    result = pl.BlockSpec((rows, piece), lambda i: (0, jnp.maximum(i - STEPS, 0)))
+    return pl.pallas_call(
+        expert_kernel,
+        grid=(2 * STEPS,),
+        out_shape=[jax.ShapeDtypeStruct((rows, D), BF16)] * 2,
+        in_specs=[whole, whole, into, into, out_of],
+        out_specs=[result, result],
+        scratch_shapes=[
+            pltpu.VMEM((2 * rows, width), F32),
+            pltpu.VMEM((2 * rows, width), F32),
+            pltpu.VMEM((2 * rows, width), BF16),
+        ],
+        compiler_params=pltpu.CompilerParams(
+            dimension_semantics=("arbitrary",), vmem_limit_bytes=32 * 1024 * 1024
+        ),
+        cost_estimate=pl.CostEstimate(
+            flops=12 * rows * D * width,
+            bytes_accessed=6 * D * width + 8 * rows * D,
+            transcendentals=2 * rows * width,
+        ),
+    )(low, high, w_gate, w_up, w_down)
+
+
 def slots_of(routes):
     experts = jnp.arange(Z * LANES, dtype=jnp.int32)
     named = routes[..., None] == experts
@@ -54,7 +160,9 @@
     core = lax.axis_index("core")
     scale = HEAD_SIZE ** (-0.5)
 
-    weight_y = lax.all_gather(out_weight, "y", axis=0, tiled=False)
+    pieces = [out_weight] + [shift(out_weight, step) for step in range(1, Y)]
+    by_distance = jnp.stack(pieces[::-1] * 2)
+    weight_y = lax.dynamic_slice_in_dim(by_distance, Y - 1 - lax.axis_index("y"), Y, 0)
     weight_y = weight_y.transpose(1, 0, 2).reshape(out_weight.shape[0], piece)
 
     head = lane * heads // (QUERY_HEADS // KEY_VALUE_HEADS)
@@ -93,25 +201,32 @@
     )
 
     hidden_z = hidden.reshape(rows, Y, Z, HEAD_SIZE).transpose(2, 0, 1, 3).reshape(Z, rows, piece)
-    routes_wide = jnp.pad(routes.astype(BF16), ((0, 0), (0, piece - TOPK)))
+    gates_high = gates.astype(BF16)
+    gates_rest = gates - gates_high.astype(F32)
+    gates_mid = gates_rest.astype(BF16)
+    gates_low = (gates_rest - gates_mid.astype(F32)).astype(BF16)
+    table = jnp.concatenate([routes.astype(BF16), gates_high, gates_mid, gates_low], axis=1)
+    table = jnp.pad(table, ((0, 0), (0, piece - table.shape[1])))
     parcel = jnp.concatenate(
         [
             jnp.broadcast_to(attention[None], (Z, rows_ctx, piece)),
             hidden_z,
-            jnp.broadcast_to(routes_wide[None], (Z, rows, piece)),
+            jnp.broadcast_to(table[None], (Z, rows, piece)),
         ],
         axis=1,
     )
     parcel = swap(parcel, "z")
     attention_z = parcel[:, :rows_ctx].reshape(Z, LANES, rows, piece)
     hidden_c = parcel[:, rows_ctx : rows_ctx + rows].astype(F32)
-    routes_c = parcel[:, rows_ctx + rows :, :TOPK].astype(jnp.int32)
+    table_c = parcel[:, rows_ctx + rows :, : 4 * TOPK].astype(F32).reshape(Z, rows, 4, TOPK)
+    routes_c = table_c[:, :, 0].astype(jnp.int32)
+    gates_c = table_c[:, :, 1] + table_c[:, :, 2] + table_c[:, :, 3]
 
     partial = jnp.einsum("zerf,fc->ezrc", attention_z, weight_y, preferred_element_type=F32)
     projected_c = jnp.sum(swap(partial.astype(BF16), EXP).astype(F32), axis=0)
     residual_c = (hidden_c + projected_c).astype(BF16).reshape(Z * rows, piece)
 
-    chosen, _ = slots_of(routes_c)
+    chosen, named = slots_of(routes_c)
     same = jnp.eye(Z, dtype=bool)
     pick = chosen.transpose(2, 0, 3, 1)[:, :, :, None, :] & same[None, :, None, :, None]
     pick = pick.reshape(Z * LANES * Z * MOST, Z * rows).astype(BF16)
@@ -119,55 +234,47 @@
     inbox = swap(outbox.reshape(Z * LANES, Z * MOST, piece), ("z",) + EXP)
     inbox, projected_c = lax.optimization_barrier((inbox, projected_c.astype(BF16)))
     slots = LANES * Z * MOST
-    inbox = inbox.reshape(Z, slots, Y, HEAD_SIZE).transpose(1, 2, 0, 3).reshape(slots, D)
-    inbox = inbox.astype(F32)
-    mean_square = jnp.mean(inbox * inbox, axis=-1, keepdims=True)
-    inbox = (inbox * lax.rsqrt(mean_square + 1e-06) * norm_gain).astype(BF16)
-
-    half = slots // 2
-    before = shift(inbox, 1)
-    after = shift(inbox, -1)
-    across_low = shift(after[:half], -1)
-    across_high = shift(before[half:], 1)
+    low, high = normalise(inbox, norm_gain)
+
+    after_low = shift(low, -1)
+    before_high = shift(high, 1)
+    before_low = shift(low, 1)
+    after_high = shift(high, -1)
+    across_low = shift(after_low, -1)
+    across_high = shift(before_high, 1)
 
     projected = swap(projected_c, "z").reshape(Z, rows, Y, HEAD_SIZE)
     projected = projected.transpose(1, 2, 0, 3).reshape(rows, D)
     residual = hidden.astype(F32) + projected.astype(F32)
     attended = residual.astype(BF16)
 
-    def expert(block):
-        block, gate_w, up_w, down_w = lax.optimization_barrier(
-            (block, w_gate[0], w_up[0], w_down[0])
-        )
-        gate_h = jnp.dot(block, gate_w, preferred_element_type=F32)
-        up_h = jnp.dot(block, up_w, preferred_element_type=F32)
-        inner = (jax.nn.silu(gate_h) * up_h).astype(BF16)
-        return jnp.dot(inner, down_w, preferred_element_type=F32).astype(BF16)
-
-    out_own = expert(inbox)
-    out_before = expert(before)
-    out_after = expert(after)
-    home_low = shift(out_before[:half], -1)
-    home_high = shift(out_after[half:], 1)
-    out_across = expert(jnp.concatenate([across_low, across_high], axis=0))
-    far_after = shift(out_across[:half], 1)
-    far_before = shift(out_across[half:], -1)
-    sum_low = shift((out_after[:half].astype(F32) + far_after.astype(F32)).astype(BF16), 1)
-    sum_high = shift((out_before[half:].astype(F32) + far_before.astype(F32)).astype(BF16), -1)
-    low = out_own[:half].astype(F32) + home_low.astype(F32) + sum_low.astype(F32)
-    high = out_own[half:].astype(F32) + home_high.astype(F32) + sum_high.astype(F32)
-    returned = jnp.concatenate([low.astype(BF16), high.astype(BF16)], axis=0)
-
-    back = swap(returned.reshape(LANES * Z, MOST, D), EXP + ("z",)).reshape(slots, D)
-    chosen_own, named = slots_of(routes)
-    gate = jnp.sum(jnp.where(named, gates[..., None], 0.0), axis=1)
-    place = jnp.where(chosen_own, gate[..., None], 0.0).reshape(rows, Z, LANES, MOST)
-    place = place.transpose(0, 2, 1, 3).reshape(rows, slots)
+    weights = (w_gate[0], w_up[0], w_down[0])
+    own_low, own_high = expert(low, high, *weights)
+    out_after_low, out_before_high = expert(after_low, before_high, *weights)
+    out_before_low, out_after_high = expert(before_low, after_high, *weights)
+    home_low = shift(out_before_low, -1)
+    home_high = shift(out_after_high, 1)
+    out_across_low, out_across_high = expert(across_low, across_high, *weights)
+    far_low = shift(out_across_low, 1)
+    far_high = shift(out_across_high, -1)
+    sum_low = shift((out_after_low.astype(F32) + far_low.astype(F32)).astype(BF16), 1)
+    sum_high = shift((out_before_high.astype(F32) + far_high.astype(F32)).astype(BF16), -1)
+    home_low = own_low.astype(F32) + home_low.astype(F32) + sum_low.astype(F32)
+    home_high = own_high.astype(F32) + home_high.astype(F32) + sum_high.astype(F32)
+    returned = jnp.concatenate([home_low.astype(BF16), home_high.astype(BF16)], axis=0)
+
+    back = swap(returned.reshape(LANES, Z * MOST, D), EXP).reshape(slots, D)
+    gate = jnp.sum(jnp.where(named, gates_c[..., None], 0.0), axis=2)
+    place = jnp.where(chosen, gate[..., None], 0.0).reshape(Z, rows, Z, LANES, MOST)
+    place = lax.dynamic_index_in_dim(place, lax.axis_index("z"), 2, keepdims=False)
+    place = jnp.where(same[:, None, None, :, None], place[:, :, :, None, :], 0.0)
+    place = place.reshape(Z * rows, slots)
     place_high = place.astype(BF16)
     place_low = (place - place_high.astype(F32)).astype(BF16)
-    moe = jnp.dot(place_high, back, preferred_element_type=F32) + jnp.dot(
+    moe_z = jnp.dot(place_high, back, preferred_element_type=F32) + jnp.dot(
         place_low, back, preferred_element_type=F32
     )
+    moe = jnp.sum(swap(moe_z.astype(BF16).reshape(Z, rows, D), "z").astype(F32), axis=0)
     mixed = (residual + moe).astype(BF16)
     return (attended, mixed)
 

time: 290 us -> 268 us (0.924)
  blocking collectives: 41.1 us -> 0 us
  matrix products: 42.2 us -> 5.11 us
  waiting for transfers between devices: 103 us -> 140 us
  Pallas kernels: 0 us -> 21.2 us
  starting transfers between devices: 43.1 us -> 62.7 us
  local copies, waits for them, and re-layouts: 36.2 us -> 25 us
  other arithmetic: 21.5 us -> 11.1 us
    dot_general x8 -> x0, matrix products: 29 us -> none  [the longest x4 18.5 us: expert(): return jnp.dot(inner, down_w, preferred_element_type=F32).astype(BF16)]
    all_to_all x1 -> x0, blocking collectives: 28.3 us -> none  [spread(): lax.all_to_all(jnp.broadcast_to(block[None], (count,) + block.shape), axe...]
    all_to_all x5 -> x6, waiting for transfers between devices: 62.6 us -> 89.4 us  [swap(): return lax.all_to_all(blocks, axes, 0, 0, tiled=True)]
    pallas_call x0 -> x5, Pallas kernels: none -> 21.2 us  [the longest x4 19.4 us: expert(): pl.pallas_call(expert_kernel, grid=(2 * STEPS,), out_shape=[jax.ShapeDtyp...]
    all_gather x1 -> x0, blocking collectives: 12.8 us -> none  [on_device(): weight_y = lax.all_gather(out_weight, 'y', axis=0, tiled=False)]
    slice x6 -> x1, local copies, waits for them, and re-layouts: 13.5 us -> 0.71 us  [on_device(): gates_c = table_c[:, :, 1] + table_c[:, :, 2] + table_c[:, :, 3]]
    all_to_all x0 -> x1, starting transfers between devices: none -> 11.5 us  [spread(): lax.all_to_all(jnp.broadcast_to(block[None], (count,) + block.shape), axe...]
    unnamed x16 -> x35, local copies, waits for them, and re-layouts: 1.01 us -> 10.6 us
  transfers between devices with their start and end apart: 16 -> 23, of which waited for: 8 -> 14; matrix products, arithmetic and copies ran while one was open for 24% -> 7% of each run, Pallas kernels for 0% -> 7%
where the time goes in v3:
time: 268 us; the launch traced here: 266 us
  waiting for transfers between devices  140 us (52%)
  starting transfers between devices  62.7 us (23%)
  local copies, waits for them, and re-layouts  25 us (9%)
  Pallas kernels  21.2 us (8%)
  other arithmetic  11.1 us (4%)
  matrix products  5.11 us (2%)
    all_to_all x6, waiting for transfers between devices, swap(): return lax.all_to_all(blocks, axes, 0, 0, tiled=True)  89.4 us
    ppermute x15, waiting for transfers between devices, shift(): return lax.ppermute(block, 'y', [(i, (i + step) % Y) for i in range(Y)])  44.7 us
    all_to_all x6, starting transfers between devices, swap(): return lax.all_to_all(blocks, axes, 0, 0, tiled=True)  30.6 us
    ppermute x15, starting transfers between devices, shift(): return lax.ppermute(block, 'y', [(i, (i + step) % Y) for i in range(Y)])  20.6 us
    pallas_call x4, Pallas kernels, expert(): pl.pallas_call(expert_kernel, grid=(2 * STEPS,), out_shape=[jax.ShapeDtyp...  19.4 us
    all_to_all x1, starting transfers between devices, spread(): lax.all_to_all(jnp.broadcast_to(block[None], (count,) + block.shape), axe...  11.5 us
    unnamed x35, local copies, waits for them, and re-layouts  10.6 us
  transfers between devices with their start and end apart: 23, of which 14 were waited for; matrix products, arithmetic and copies ran while one was open for 7% of the time, Pallas kernels for 7%

profile of v3, /device:TPU:2, one launch (start us, length us, event | category | flops | bytes accessed | tf_op | source)
XLA Modules:
  0.0 266.1 jit_solution(2584954930001434820)
XLA Ops:
  2.9 11.5 %all-to-all-start = ((bf16[32,32,256]{2,1,0:T(8,128)(2,1)}), bf16[32,32,256]{2,1,0:T(8,128)(2,1)S(1)}, u32[]{:S(2)}, u32[]{:S(2)}) async-start(bf16[32,32,256]{2,1,0:T(8,128)(2,1)} %broadcast_in_dim.54), calls=%async_computation | async-start | bytes 1048576 | tf_op jit(solution)/shard_map/all_to_all | solution.py:24
  22.6 4.5 %collective-permute-done.1 = bf16[512,128]{1,0:T(8,128)(2,1)S(1)} collective-permute-done((bf16[512,128]{1,0:T(8,128)(2,1)}, bf16[512,128]{1,0:T(8,128)(2,1)S(1)}, u32[]{:S(2)}, u32[]{:S(2)}) %collective-permute-start.1) | collective-permute-done | bytes 131104 | tf_op jit(solution)/shard_map/ppermute | solution.py:34
  27.1 4.1 %all-to-all-done = bf16[32,32,256]{2,1,0:T(8,128)(2,1)S(1)} async-done(((bf16[32,32,256]{2,1,0:T(8,128)(2,1)}), bf16[32,32,256]{2,1,0:T(8,128)(2,1)S(1)}, u32[]{:S(2)}, u32[]{:S(2)}) %all-to-all-start) | async-done | bytes 524320 | tf_op jit(solution)/shard_map/all_to_all | solution.py:24
  36.4 4.4 %all-to-all-start.1 = ((bf16[8,80,512]{2,1,0:T(8,128)(2,1)}), bf16[8,80,512]{2,1,0:T(8,128)(2,1)S(1)}, u32[]{:S(2)}, u32[]{:S(2)}) async-start(bf16[8,80,512]{2,1,0:T(8,128)(2,1)} %pad_maximum_fusion.1), calls=%async_computation.1 | async-start | bytes 1310720 | tf_op jit(solution)/shard_map/all_to_all | solution.py:30
  41.7 19.8 %all-to-all-done.1 = bf16[8,80,512]{2,1,0:T(8,128)(2,1)S(1)} async-done(((bf16[8,80,512]{2,1,0:T(8,128)(2,1)}), bf16[8,80,512]{2,1,0:T(8,128)(2,1)S(1)}, u32[]{:S(2)}, u32[]{:S(2)}) %all-to-all-start.1) | async-done | bytes 655392 | tf_op jit(solution)/shard_map/all_to_all | solution.py:30
  64.2 4.8 %all-to-all-start.2 = ((bf16[8,8,8,512]{3,2,1,0:T(8,128)(2,1)}), bf16[8,8,8,512]{3,2,1,0:T(8,128)(2,1)S(1)}, u32[]{:S(2)}, u32[]{:S(2)}) async-start(bf16[8,8,8,512]{3,2,1,0:T(8,128)(2,1)} %copy.33), calls=%async_computation.2 | async-start | bytes 1048576 | tf_op jit(solution)/shard_map/all_to_all | solution.py:30
  71.8 6.1 %all-to-all-done.2 = bf16[8,8,8,512]{3,2,1,0:T(8,128)(2,1)S(1)} async-done(((bf16[8,8,8,512]{3,2,1,0:T(8,128)(2,1)}), bf16[8,8,8,512]{3,2,1,0:T(8,128)(2,1)S(1)}, u32[]{:S(2)}, u32[]{:S(2)}) %all-to-all-start.2) | async-done | bytes 524320 | tf_op jit(solution)/shard_map/all_to_all | solution.py:30
  79.4 6.6 %all-to-all-start.3 = ((bf16[64,16,512]{2,1,0:T(8,128)(2,1)}), bf16[64,16,512]{2,1,0:T(8,128)(2,1)}, u32[]{:S(2)}, u32[]{:S(2)}) async-start(bf16[64,16,512]{2,1,0:T(8,128)(2,1)} %bitcast.109), calls=%async_computation.3 | async-start | bytes 2097152 | tf_op jit(solution)/shard_map/all_to_all | solution.py:30
  86.6 28.2 %all-to-all-done.3.x_ref = bf16[64,16,512]{2,1,0:T(8,128)(2,1)} async-done(((bf16[64,16,512]{2,1,0:T(8,128)(2,1)}), bf16[64,16,512]{2,1,0:T(8,128)(2,1)}, u32[]{:S(2)}, u32[]{:S(2)}) %all-to-all-start.3) | async-done | bytes 1048608 | tf_op jit(solution)/shard_map/all_to_all | solution.py:30
  118.8 10.7 %collective-permute-done.7.low_ref = bf16[64,4096]{1,0:T(8,128)(2,1)} collective-permute-done((bf16[64,4096]{1,0:T(8,128)(2,1)S(1)}, bf16[64,4096]{1,0:T(8,128)(2,1)}, u32[]{:S(2)}, u32[]{:S(2)}) %collective-permute-start.7) | collective-permute-done | bytes 524320 | tf_op jit(solution)/shard_map/ppermute | solution.py:34
  139.7 5.7 %collective-permute-done.9.low_ref = bf16[64,4096]{1,0:T(8,128)(2,1)} collective-permute-done((bf16[64,4096]{1,0:T(8,128)(2,1)}, bf16[64,4096]{1,0:T(8,128)(2,1)}, u32[]{:S(2)}, u32[]{:S(2)}) %collective-permute-start.9) | collective-permute-done | bytes 524320 | tf_op jit(solution)/shard_map/ppermute | solution.py:34
  145.4 3.7 %collective-permute-done.10.high_ref = bf16[64,4096]{1,0:T(8,128)(2,1)} collective-permute-done((bf16[64,4096]{1,0:T(8,128)(2,1)}, bf16[64,4096]{1,0:T(8,128)(2,1)}, u32[]{:S(2)}, u32[]{:S(2)}) %collective-permute-start.10) | collective-permute-done | bytes 524320 | tf_op jit(solution)/shard_map/ppermute | solution.py:34
  152.8 5.8 %shard_map.126 = (bf16[64,4096]{1,0:T(8,128)(2,1)S(1)}, bf16[64,4096]{1,0:T(8,128)(2,1)}) custom-call(bf16[64,4096]{1,0:T(8,128)(2,1)} %collective-permute-done.9.low_ref, bf16[64,4096]{1,0:T(8,128)(2,1)} %collective-permute-done.10.high_ref, bf16[4096,384]{1,0:T(8,128)(2,1)S(1)} %bitcast.94, bf16[4096,384]{1,0:T(8,128)(2,1)S(1)} %bitcast.98, ...), custom_call_target="tpu_custom_call" | custom-call | flops 1207959552 | bytes 11534336 | tf_op jit(solution)/shard_map/pallas_call | solution.py:119
  168.0 3.7 %shard_map.123 = (bf16[64,4096]{1,0:T(8,128)(2,1)S(1)}, bf16[64,4096]{1,0:T(8,128)(2,1)S(1)}) custom-call(bf16[64,4096]{1,0:T(8,128)(2,1)S(1)} %copy-done.8, bf16[64,4096]{1,0:T(8,128)(2,1)S(1)} %copy-done.6, bf16[4096,384]{1,0:T(8,128)(2,1)S(1)} %bitcast.95, bf16[4096,384]{1,0:T(8,128)(2,1)S(1)} %bitcast.99, bf16[384,4096]{1,0:T(8,128)(2,1)S(1)} %bitcast.103), custom_call_target="tpu_custom_call" | custom-call | flops 1207959552 | bytes 11534336 | tf_op jit(solution)/shard_map/pallas_call | solution.py:119
  171.8 4.9 %shard_map.124 = (bf16[64,4096]{1,0:T(8,128)(2,1)S(1)}, bf16[64,4096]{1,0:T(8,128)(2,1)S(1)}) custom-call(bf16[64,4096]{1,0:T(8,128)(2,1)} %collective-permute-done.4.low_ref, bf16[64,4096]{1,0:T(8,128)(2,1)} %collective-permute-done.5.high_ref, bf16[4096,384]{1,0:T(8,128)(2,1)S(1)} %bitcast.96, bf16[4096,384]{1,0:T(8,128)(2,1)S(1)} %bitcast.100, ...), custom_call_target="tpu_custom_call" | custom-call | flops 1207959552 | bytes 11534336 | tf_op jit(solution)/shard_map/pallas_call | solution.py:119
  180.1 4.9 %shard_map.125 = (bf16[64,4096]{1,0:T(8,128)(2,1)S(1)}, bf16[64,4096]{1,0:T(8,128)(2,1)S(1)}) custom-call(bf16[64,4096]{1,0:T(8,128)(2,1)} %collective-permute-done.7.low_ref, bf16[64,4096]{1,0:T(8,128)(2,1)} %collective-permute-done.8.high_ref, bf16[4096,384]{1,0:T(8,128)(2,1)S(1)} %bitcast.97, bf16[4096,384]{1,0:T(8,128)(2,1)S(1)} %bitcast.101, ...), custom_call_target="tpu_custom_call" | custom-call | flops 1207959552 | bytes 11534336 | tf_op jit(solution)/shard_map/pallas_call | solution.py:119
  189.6 9.9 %collective-permute-done.11 = bf16[64,4096]{1,0:T(8,128)(2,1)S(1)} collective-permute-done((bf16[64,4096]{1,0:T(8,128)(2,1)S(1)}, bf16[64,4096]{1,0:T(8,128)(2,1)S(1)}, u32[]{:S(2)}, u32[]{:S(2)}) %collective-permute-start.11) | collective-permute-done | bytes 524320 | tf_op jit(solution)/shard_map/ppermute | solution.py:34
  200.1 10.1 %collective-permute-done.12 = bf16[64,4096]{1,0:T(8,128)(2,1)S(1)} collective-permute-done((bf16[64,4096]{1,0:T(8,128)(2,1)S(1)}, bf16[64,4096]{1,0:T(8,128)(2,1)S(1)}, u32[]{:S(2)}, u32[]{:S(2)}) %collective-permute-start.12) | collective-permute-done | bytes 524320 | tf_op jit(solution)/shard_map/ppermute | solution.py:34
  211.6 4.9 %all-to-all-start.5 = ((bf16[8,16,4096]{2,1,0:T(8,128)(2,1)}), bf16[8,16,4096]{2,1,0:T(8,128)(2,1)S(1)}, u32[]{:S(2)}, u32[]{:S(2)}) async-start(bf16[8,16,4096]{2,1,0:T(8,128)(2,1)} %bitcast.31), calls=%async_computation.5 | async-start | bytes 2097152 | tf_op jit(solution)/shard_map/all_to_all | solution.py:30
  218.5 12.4 %all-to-all-done.5 = bf16[8,16,4096]{2,1,0:T(8,128)(2,1)S(1)} async-done(((bf16[8,16,4096]{2,1,0:T(8,128)(2,1)}), bf16[8,16,4096]{2,1,0:T(8,128)(2,1)S(1)}, u32[]{:S(2)}, u32[]{:S(2)}) %all-to-all-start.5) | async-done | bytes 1048608 | tf_op jit(solution)/shard_map/all_to_all | solution.py:30
  230.9 6.4 %all-to-all-start.4 = ((bf16[8,8,512]{2,1,0:T(8,128)(2,1)}), bf16[8,8,512]{2,1,0:T(8,128)(2,1)S(1)}, u32[]{:S(2)}, u32[]{:S(2)}) async-start(bf16[8,8,512]{2,1,0:T(8,128)(2,1)} %convert_element_type.221), calls=%async_computation.4 | async-start | bytes 131072 | tf_op jit(solution)/shard_map/all_to_all | solution.py:30
  238.9 6.9 %all-to-all-done.4 = bf16[8,8,512]{2,1,0:T(8,128)(2,1)S(1)} async-done(((bf16[8,8,512]{2,1,0:T(8,128)(2,1)}), bf16[8,8,512]{2,1,0:T(8,128)(2,1)S(1)}, u32[]{:S(2)}, u32[]{:S(2)}) %all-to-all-start.4) | async-done | bytes 65568 | tf_op jit(solution)/shard_map/all_to_all | solution.py:30
  245.7 3.5 %all-to-all-start.6 = ((bf16[8,8,4096]{2,1,0:T(8,128)(2,1)}), bf16[8,8,4096]{2,1,0:T(8,128)(2,1)S(1)}, u32[]{:S(2)}, u32[]{:S(2)}) async-start(bf16[8,8,4096]{2,1,0:T(8,128)(2,1)} %fusion.1), calls=%async_computation.6 | async-start | bytes 1048576 | tf_op jit(solution)/shard_map/all_to_all | solution.py:30
  249.3 16.0 %all-to-all-done.6 = bf16[8,8,4096]{2,1,0:T(8,128)(2,1)S(1)} async-done(((bf16[8,8,4096]{2,1,0:T(8,128)(2,1)}), bf16[8,8,4096]{2,1,0:T(8,128)(2,1)S(1)}, u32[]{:S(2)}, u32[]{:S(2)}) %all-to-all-start.6) | async-done | bytes 524320 | tf_op jit(solution)/shard_map/all_to_all | solution.py:30
  (135 shorter events, 65.1 us)
Async XLA Ops:
  2.9 28.4 %all-to-all-start = ((bf16[32,32,256]{2,1,0:T(8,128)(2,1)}), bf16[32,32,256]{2,1,0:T(8,128)(2,1)S(1)}, u32[]{:S(2)}, u32[]{:S(2)}) async-start(bf16[32,32,256]{2,1,0:T(8,128)(2,1)} %broadcast_in_dim.54), calls=%async_computation | async-start | bytes 1048576 | tf_op jit(solution)/shard_map/all_to_all | solution.py:24
  14.4 12.7 %collective-permute-start.1 = (bf16[512,128]{1,0:T(8,128)(2,1)}, bf16[512,128]{1,0:T(8,128)(2,1)S(1)}, u32[]{:S(2)}, u32[]{:S(2)}) collective-permute-start(bf16[512,128]{1,0:T(8,128)(2,1)} %param.15), channel_id=1, source_target_pairs={{0,192},{64,0},{128,64},{192,128},{1,193},{65,1},{129,65},{193,129... | collective-permute-start | bytes 393224 | tf_op jit(solution)/shard_map/ppermute | solution.py:34
  17.6 13.7 %collective-permute-start.2 = (bf16[512,128]{1,0:T(8,128)(2,1)}, bf16[512,128]{1,0:T(8,128)(2,1)S(1)}, u32[]{:S(2)}, u32[]{:S(2)}) collective-permute-start(bf16[512,128]{1,0:T(8,128)(2,1)} %param.15), channel_id=1, source_target_pairs={{0,128},{64,192},{128,0},{192,64},{1,129},{65,193},{129,1},{193,65... | collective-permute-start | bytes 393224 | tf_op jit(solution)/shard_map/ppermute | solution.py:34
  18.4 13.0 %collective-permute-start.3 = (bf16[512,128]{1,0:T(8,128)(2,1)}, bf16[512,128]{1,0:T(8,128)(2,1)S(1)}, u32[]{:S(2)}, u32[]{:S(2)}) collective-permute-start(bf16[512,128]{1,0:T(8,128)(2,1)} %param.15), channel_id=1, source_target_pairs={{0,64},{64,128},{128,192},{192,0},{1,65},{65,129},{129,193},{193,1... | collective-permute-start | bytes 393224 | tf_op jit(solution)/shard_map/ppermute | solution.py:34
  31.3 1.9 collective-permute-start
  36.4 25.0 %all-to-all-start.1 = ((bf16[8,80,512]{2,1,0:T(8,128)(2,1)}), bf16[8,80,512]{2,1,0:T(8,128)(2,1)S(1)}, u32[]{:S(2)}, u32[]{:S(2)}) async-start(bf16[8,80,512]{2,1,0:T(8,128)(2,1)} %pad_maximum_fusion.1), calls=%async_computation.1 | async-start | bytes 1310720 | tf_op jit(solution)/shard_map/all_to_all | solution.py:30
  64.2 13.7 %all-to-all-start.2 = ((bf16[8,8,8,512]{3,2,1,0:T(8,128)(2,1)}), bf16[8,8,8,512]{3,2,1,0:T(8,128)(2,1)S(1)}, u32[]{:S(2)}, u32[]{:S(2)}) async-start(bf16[8,8,8,512]{3,2,1,0:T(8,128)(2,1)} %copy.33), calls=%async_computation.2 | async-start | bytes 1048576 | tf_op jit(solution)/shard_map/all_to_all | solution.py:30
  79.4 69.7 %copy-start = (bf16[1,4096,384]{2,1,0:T(8,128)(2,1)S(1)}, bf16[1,4096,384]{2,1,0:T(8,128)(2,1)}, u32[]{:S(2)}) copy-start(bf16[1,4096,384]{2,1,0:T(8,128)(2,1)} %param.17) | copy-start | bytes 9437188
  79.4 35.4 %all-to-all-start.3 = ((bf16[64,16,512]{2,1,0:T(8,128)(2,1)}), bf16[64,16,512]{2,1,0:T(8,128)(2,1)}, u32[]{:S(2)}, u32[]{:S(2)}) async-start(bf16[64,16,512]{2,1,0:T(8,128)(2,1)} %bitcast.109), calls=%async_computation.3 | async-start | bytes 2097152 | tf_op jit(solution)/shard_map/all_to_all | solution.py:30
  116.6 13.0 %collective-permute-start.7 = (bf16[64,4096]{1,0:T(8,128)(2,1)S(1)}, bf16[64,4096]{1,0:T(8,128)(2,1)}, u32[]{:S(2)}, u32[]{:S(2)}) collective-permute-start(bf16[64,4096]{1,0:T(8,128)(2,1)S(1)} %get-tuple-element.16.low_ref), channel_id=1, source_target_pairs={{0,192},{64,0},{128,64},{192,128},{1,193},{65,1},{129,65},{193,129... | collective-permute-start | bytes 1572872 | tf_op jit(solution)/shard_map/ppermute | solution.py:34
  118.7 13.9 %collective-permute-start.8 = (bf16[64,4096]{1,0:T(8,128)(2,1)S(1)}, bf16[64,4096]{1,0:T(8,128)(2,1)}, u32[]{:S(2)}, u32[]{:S(2)}) collective-permute-start(bf16[64,4096]{1,0:T(8,128)(2,1)S(1)} %get-tuple-element.17.high_ref), channel_id=1, source_target_pairs={{0,64},{64,128},{128,192},{192,0},{1,65},{65,129},{129,193},{193,1... | collective-permute-start | bytes 1572872 | tf_op jit(solution)/shard_map/ppermute | solution.py:34
  129.5 15.8 %collective-permute-start.9 = (bf16[64,4096]{1,0:T(8,128)(2,1)}, bf16[64,4096]{1,0:T(8,128)(2,1)}, u32[]{:S(2)}, u32[]{:S(2)}) collective-permute-start(bf16[64,4096]{1,0:T(8,128)(2,1)} %collective-permute-done.7.low_ref), channel_id=1, source_target_pairs={{0,192},{64,0},{128,64},{192,128},{1,193},{65,1},{129,65},{193,129... | collective-permute-start | bytes 1572872 | tf_op jit(solution)/shard_map/ppermute | solution.py:34
  132.7 16.4 %collective-permute-start.10 = (bf16[64,4096]{1,0:T(8,128)(2,1)}, bf16[64,4096]{1,0:T(8,128)(2,1)}, u32[]{:S(2)}, u32[]{:S(2)}) collective-permute-start(bf16[64,4096]{1,0:T(8,128)(2,1)} %collective-permute-done.8.high_ref), channel_id=1, source_target_pairs={{0,64},{64,128},{128,192},{192,0},{1,65},{65,129},{129,193},{193,1... | collective-permute-start | bytes 1572872 | tf_op jit(solution)/shard_map/ppermute | solution.py:34
  134.6 37.2 %collective-permute-start.4 = (bf16[64,4096]{1,0:T(8,128)(2,1)}, bf16[64,4096]{1,0:T(8,128)(2,1)}, u32[]{:S(2)}, u32[]{:S(2)}) collective-permute-start(bf16[64,4096]{1,0:T(8,128)(2,1)} %copy-done.7), channel_id=1, source_target_pairs={{0,64},{64,128},{128,192},{192,0},{1,65},{65,129},{129,193},{193,1... | collective-permute-start | bytes 1572872 | tf_op jit(solution)/shard_map/ppermute | solution.py:34
  134.7 37.1 %collective-permute-start.5 = (bf16[64,4096]{1,0:T(8,128)(2,1)}, bf16[64,4096]{1,0:T(8,128)(2,1)}, u32[]{:S(2)}, u32[]{:S(2)}) collective-permute-start(bf16[64,4096]{1,0:T(8,128)(2,1)} %copy-done.5), channel_id=1, source_target_pairs={{0,192},{64,0},{128,64},{192,128},{1,193},{65,1},{129,65},{193,129... | collective-permute-start | bytes 1572872 | tf_op jit(solution)/shard_map/ppermute | solution.py:34
  159.5 26.4 %collective-permute-start.14 = (bf16[64,4096]{1,0:T(8,128)(2,1)}, bf16[64,4096]{1,0:T(8,128)(2,1)}, u32[]{:S(2)}, u32[]{:S(2)}) collective-permute-start(bf16[64,4096]{1,0:T(8,128)(2,1)} %get-tuple-element.25), channel_id=1, source_target_pairs={{0,192},{64,0},{128,64},{192,128},{1,193},{65,1},{129,65},{193,129... | collective-permute-start | bytes 1572872 | tf_op jit(solution)/shard_map/ppermute | solution.py:34
  176.8 23.1 %collective-permute-start.13 = (bf16[64,4096]{1,0:T(8,128)(2,1)S(1)}, bf16[64,4096]{1,0:T(8,128)(2,1)S(1)}, u32[]{:S(2)}, u32[]{:S(2)}) collective-permute-start(bf16[64,4096]{1,0:T(8,128)(2,1)S(1)} %get-tuple-element.23), channel_id=1, source_target_pairs={{0,64},{64,128},{128,192},{192,0},{1,65},{65,129},{129,193},{193,1... | collective-permute-start | bytes 1572872 | tf_op jit(solution)/shard_map/ppermute | solution.py:34
  178.9 21.3 %collective-permute-start.6 = (bf16[64,4096]{1,0:T(8,128)(2,1)S(1)}, bf16[64,4096]{1,0:T(8,128)(2,1)S(1)}, u32[]{:S(2)}, u32[]{:S(2)}) collective-permute-start(bf16[64,4096]{1,0:T(8,128)(2,1)S(1)} %get-tuple-element.19), channel_id=1, source_target_pairs={{0,192},{64,0},{128,64},{192,128},{1,193},{65,1},{129,65},{193,129... | collective-permute-start | bytes 1572872 | tf_op jit(solution)/shard_map/ppermute | solution.py:34
  185.0 14.4 %collective-permute-start.11 = (bf16[64,4096]{1,0:T(8,128)(2,1)S(1)}, bf16[64,4096]{1,0:T(8,128)(2,1)S(1)}, u32[]{:S(2)}, u32[]{:S(2)}) collective-permute-start(bf16[64,4096]{1,0:T(8,128)(2,1)S(1)} %copy-done.11), channel_id=1, source_target_pairs={{0,64},{64,128},{128,192},{192,0},{1,65},{65,129},{129,193},{193,1... | collective-permute-start | bytes 1572872 | tf_op jit(solution)/shard_map/ppermute | solution.py:34
  187.1 12.8 %collective-permute-start.15 = (bf16[64,4096]{1,0:T(8,128)(2,1)S(1)}, bf16[64,4096]{1,0:T(8,128)(2,1)S(1)}, u32[]{:S(2)}, u32[]{:S(2)}) collective-permute-start(bf16[64,4096]{1,0:T(8,128)(2,1)S(1)} %add_convert_fusion.1), channel_id=1, source_target_pairs={{0,192},{64,0},{128,64},{192,128},{1,193},{65,1},{129,65},{193,129... | collective-permute-start | bytes 1572872 | tf_op jit(solution)/shard_map/ppermute | solution.py:34
  199.6 10.7 %collective-permute-start.12 = (bf16[64,4096]{1,0:T(8,128)(2,1)S(1)}, bf16[64,4096]{1,0:T(8,128)(2,1)S(1)}, u32[]{:S(2)}, u32[]{:S(2)}) collective-permute-start(bf16[64,4096]{1,0:T(8,128)(2,1)S(1)} %add_convert_fusion.3), channel_id=1, source_target_pairs={{0,64},{64,128},{128,192},{192,0},{1,65},{65,129},{129,193},{193,1... | collective-permute-start | bytes 1572872 | tf_op jit(solution)/shard_map/ppermute | solution.py:34
  211.6 19.4 %all-to-all-start.5 = ((bf16[8,16,4096]{2,1,0:T(8,128)(2,1)}), bf16[8,16,4096]{2,1,0:T(8,128)(2,1)S(1)}, u32[]{:S(2)}, u32[]{:S(2)}) async-start(bf16[8,16,4096]{2,1,0:T(8,128)(2,1)} %bitcast.31), calls=%async_computation.5 | async-start | bytes 2097152 | tf_op jit(solution)/shard_map/all_to_all | solution.py:30
  230.9 14.8 %all-to-all-start.4 = ((bf16[8,8,512]{2,1,0:T(8,128)(2,1)}), bf16[8,8,512]{2,1,0:T(8,128)(2,1)S(1)}, u32[]{:S(2)}, u32[]{:S(2)}) async-start(bf16[8,8,512]{2,1,0:T(8,128)(2,1)} %convert_element_type.221), calls=%async_computation.4 | async-start | bytes 131072 | tf_op jit(solution)/shard_map/all_to_all | solution.py:30
  245.7 19.6 %all-to-all-start.6 = ((bf16[8,8,4096]{2,1,0:T(8,128)(2,1)}), bf16[8,8,4096]{2,1,0:T(8,128)(2,1)S(1)}, u32[]{:S(2)}, u32[]{:S(2)}) async-start(bf16[8,8,4096]{2,1,0:T(8,128)(2,1)} %fusion.1), calls=%async_computation.6 | async-start | bytes 1048576 | tf_op jit(solution)/shard_map/all_to_all | solution.py:30
  (13 other events, 111.0 us)

commit v4 on v3

--- a/solution.py
+++ b/solution.py
@@ -16,6 +16,7 @@
 CTX = ("y", "z")
 EXP = ("x", "core")
 LANES = X * CORE
+VMEM_LIMIT = 65024 * 1024
 BF16 = jnp.bfloat16
 F32 = jnp.float32
 
@@ -64,7 +65,7 @@
         out_shape=[jax.ShapeDtypeStruct((rows, D), BF16)] * 2,
         in_specs=[pl.BlockSpec(memory_space=pltpu.VMEM)] * 2,
         out_specs=[pl.BlockSpec(memory_space=pltpu.VMEM)] * 2,
-        compiler_params=pltpu.CompilerParams(vmem_limit_bytes=32 * 1024 * 1024),
+        compiler_params=pltpu.CompilerParams(vmem_limit_bytes=VMEM_LIMIT),
         cost_estimate=pl.CostEstimate(flops=6 * rows * D, bytes_accessed=8 * rows * D, transcendentals=0),
     )(inbox, gain.reshape(1, D))
 
@@ -72,9 +73,8 @@
 STEPS = 4
 
 
-def expert_kernel(
-    low_ref, high_ref, gate_ref, up_ref, down_ref, out_low_ref, out_high_ref, gate_sum, up_sum, inner
-):
+def expert_kernel(low_ref, high_ref, gate_ref, up_ref, down_ref, *refs):
+    out_low_ref, out_high_ref, gate_sum, up_sum, inner = refs[-5:]
     step = pl.program_id(0)
     depth = gate_ref.shape[0]
     rows = low_ref.shape[0]
@@ -108,7 +108,7 @@
         out_high_ref[...] = out[rows:]
 
 
-def expert(low, high, w_gate, w_up, w_down):
+def expert(low, high, w_gate, w_up, w_down, after=()):
     rows = low.shape[0]
     width = w_gate.shape[1]
     piece = D // STEPS
@@ -120,7 +120,8 @@
         expert_kernel,
         grid=(2 * STEPS,),
         out_shape=[jax.ShapeDtypeStruct((rows, D), BF16)] * 2,
-        in_specs=[whole, whole, into, into, out_of],
+        in_specs=[whole, whole, into, into, out_of]
+        + [pl.BlockSpec((rows // 4, HEAD_SIZE), lambda i: (0, 0)) for _ in after],
         out_specs=[result, result],
         scratch_shapes=[
             pltpu.VMEM((2 * rows, width), F32),
@@ -128,14 +129,14 @@
             pltpu.VMEM((2 * rows, width), BF16),
         ],
         compiler_params=pltpu.CompilerParams(
-            dimension_semantics=("arbitrary",), vmem_limit_bytes=32 * 1024 * 1024
+            dimension_semantics=("arbitrary",), vmem_limit_bytes=VMEM_LIMIT
         ),
         cost_estimate=pl.CostEstimate(
             flops=12 * rows * D * width,
             bytes_accessed=6 * D * width + 8 * rows * D,
             transcendentals=2 * rows * width,
         ),
-    )(low, high, w_gate, w_up, w_down)
+    )(low, high, w_gate, w_up, w_down, *after)
 
 
 def slots_of(routes):
@@ -164,6 +165,30 @@
     by_distance = jnp.stack(pieces[::-1] * 2)
     weight_y = lax.dynamic_slice_in_dim(by_distance, Y - 1 - lax.axis_index("y"), Y, 0)
     weight_y = weight_y.transpose(1, 0, 2).reshape(out_weight.shape[0], piece)
+
+    group = lax.axis_index("z")
+    hidden_z = hidden.reshape(rows, Y, Z, HEAD_SIZE).transpose(2, 0, 1, 3).reshape(Z, rows, piece)
+    gates_high = gates.astype(BF16)
+    gates_rest = gates - gates_high.astype(F32)
+    gates_mid = gates_rest.astype(BF16)
+    gates_low = (gates_rest - gates_mid.astype(F32)).astype(BF16)
+    table = jnp.concatenate([routes.astype(BF16), gates_high, gates_mid, gates_low], axis=1)
+    table = jnp.pad(table, ((0, 0), (0, HEAD_SIZE - table.shape[1])))
+    parcels = jnp.concatenate(
+        [hidden_z, jnp.broadcast_to(table[None], (Z, rows, HEAD_SIZE))], axis=2
+    )
+    parcels = jnp.concatenate([parcels, parcels], axis=0)
+    parcels = lax.dynamic_slice_in_dim(parcels, group, Z, 0)
+    pieces = [parcels[0]] + [
+        lax.ppermute(parcels[step], "z", [(i, (i + step) % Z) for i in range(Z)])
+        for step in range(1, Z)
+    ]
+    by_distance = jnp.stack(pieces[::-1] * 2)
+    parcels = lax.dynamic_slice_in_dim(by_distance, Z - 1 - group, Z, 0)
+    hidden_c = parcels[:, :, :piece].astype(F32)
+    table_c = parcels[:, :, piece : piece + 4 * TOPK].astype(F32).reshape(Z, rows, 4, TOPK)
+    routes_c = table_c[:, :, 0].astype(jnp.int32)
+    gates_c = table_c[:, :, 1] + table_c[:, :, 2] + table_c[:, :, 3]
 
     head = lane * heads // (QUERY_HEADS // KEY_VALUE_HEADS)
     half_ctx = rows_ctx // CORE
@@ -200,27 +225,7 @@
         (accumulated / totals[:, None]).reshape(rows_ctx, heads * HEAD_SIZE).astype(BF16)
     )
 
-    hidden_z = hidden.reshape(rows, Y, Z, HEAD_SIZE).transpose(2, 0, 1, 3).reshape(Z, rows, piece)
-    gates_high = gates.astype(BF16)
-    gates_rest = gates - gates_high.astype(F32)
-    gates_mid = gates_rest.astype(BF16)
-    gates_low = (gates_rest - gates_mid.astype(F32)).astype(BF16)
-    table = jnp.concatenate([routes.astype(BF16), gates_high, gates_mid, gates_low], axis=1)
-    table = jnp.pad(table, ((0, 0), (0, piece - table.shape[1])))
-    parcel = jnp.concatenate(
-        [
-            jnp.broadcast_to(attention[None], (Z, rows_ctx, piece)),
-            hidden_z,
-            jnp.broadcast_to(table[None], (Z, rows, piece)),
-        ],
-        axis=1,
-    )
-    parcel = swap(parcel, "z")
-    attention_z = parcel[:, :rows_ctx].reshape(Z, LANES, rows, piece)
-    hidden_c = parcel[:, rows_ctx : rows_ctx + rows].astype(F32)
-    table_c = parcel[:, rows_ctx + rows :, : 4 * TOPK].astype(F32).reshape(Z, rows, 4, TOPK)
-    routes_c = table_c[:, :, 0].astype(jnp.int32)
-    gates_c = table_c[:, :, 1] + table_c[:, :, 2] + table_c[:, :, 3]
+    attention_z = spread(attention, "z", Z).reshape(Z, LANES, rows, piece)
 
     partial = jnp.einsum("zerf,fc->ezrc", attention_z, weight_y, preferred_element_type=F32)
     projected_c = jnp.sum(swap(partial.astype(BF16), EXP).astype(F32), axis=0)
@@ -250,11 +255,17 @@
 
     weights = (w_gate[0], w_up[0], w_down[0])
     own_low, own_high = expert(low, high, *weights)
-    out_after_low, out_before_high = expert(after_low, before_high, *weights)
-    out_before_low, out_after_high = expert(before_low, after_high, *weights)
+    out_after_low, out_before_high = expert(
+        after_low, before_high, *weights, after=(own_low, jnp.tile(projected, (2, 1)))
+    )
+    out_across_low, out_across_high = expert(
+        across_low, across_high, *weights, after=(out_after_low,)
+    )
+    out_before_low, out_after_high = expert(
+        before_low, after_high, *weights, after=(out_across_low,)
+    )
     home_low = shift(out_before_low, -1)
     home_high = shift(out_after_high, 1)
-    out_across_low, out_across_high = expert(across_low, across_high, *weights)
     far_low = shift(out_across_low, 1)
     far_high = shift(out_across_high, -1)
     sum_low = shift((out_after_low.astype(F32) + far_low.astype(F32)).astype(BF16), 1)

time: 268 us -> 277 us (1.034)
  waiting for transfers between devices: 140 us -> 105 us
  blocking collectives: 0 us -> 24.3 us
  Pallas kernels: 21.2 us -> 38.8 us
  starting transfers between devices: 62.7 us -> 77.6 us
  local copies, waits for them, and re-layouts: 25 us -> 12 us
    all_to_all x6 -> x4, waiting for transfers between devices: 89.4 us -> 47.5 us  [swap(): return lax.all_to_all(blocks, axes, 0, 0, tiled=True)]
    all_to_all x0 -> x1, blocking collectives: none -> 24.3 us  [swap(): return lax.all_to_all(blocks, axes, 0, 0, tiled=True)]
    ppermute x0 -> x7, starting transfers between devices: none -> 17.8 us  [on_device(): lax.ppermute(parcels[step], 'z', [(i, (i + step) % Z) for i in range(Z)])]
    pallas_call x4, Pallas kernels: 19.4 us -> 36.2 us  [expert(): pl.pallas_call(expert_kernel, grid=(2 * STEPS,), out_shape=[jax.ShapeDtyp...]
    ppermute x15, waiting for transfers between devices: 44.7 us -> 29.3 us  [shift(): return lax.ppermute(block, 'y', [(i, (i + step) % Y) for i in range(Y)])]
    all_to_all x1 -> x2, waiting for transfers between devices: 4.14 us -> 17 us  [spread(): lax.all_to_all(jnp.broadcast_to(block[None], (count,) + block.shape), axe...]
    all_to_all x6 -> x4, starting transfers between devices: 30.6 us -> 20.3 us  [swap(): return lax.all_to_all(blocks, axes, 0, 0, tiled=True)]
    ppermute x0 -> x7, waiting for transfers between devices: none -> 10.1 us  [on_device(): lax.ppermute(parcels[step], 'z', [(i, (i + step) % Z) for i in range(Z)])]
  transfers between devices with their start and end apart: 23 -> 29, of which waited for: 14 -> 14; matrix products, arithmetic and copies ran while one was open for 7% -> 6% of each run, Pallas kernels for 7% -> 13%
where the time goes in v4:
time: 277 us; the launch traced here: 274 us
  waiting for transfers between devices  105 us (38%)
  starting transfers between devices  77.6 us (28%)
  Pallas kernels  38.8 us (14%)
  blocking collectives  24.3 us (9%)
  local copies, waits for them, and re-layouts  12 us (4%)
  other arithmetic  9.88 us (4%)
  matrix products  4.29 us (2%)
    all_to_all x4, waiting for transfers between devices, swap(): return lax.all_to_all(blocks, axes, 0, 0, tiled=True)  47.5 us
    pallas_call x4, Pallas kernels, expert(): pl.pallas_call(expert_kernel, grid=(2 * STEPS,), out_shape=[jax.ShapeDtyp...  36.2 us
    ppermute x15, waiting for transfers between devices, shift(): return lax.ppermute(block, 'y', [(i, (i + step) % Y) for i in range(Y)])  29.3 us
    all_to_all x1, blocking collectives, swap(): return lax.all_to_all(blocks, axes, 0, 0, tiled=True)  24.3 us
    ppermute x15, starting transfers between devices, shift(): return lax.ppermute(block, 'y', [(i, (i + step) % Y) for i in range(Y)])  23 us
    all_to_all x4, starting transfers between devices, swap(): return lax.all_to_all(blocks, axes, 0, 0, tiled=True)  20.3 us
    ppermute x7, starting transfers between devices, on_device(): lax.ppermute(parcels[step], 'z', [(i, (i + step) % Z) for i in range(Z)])  17.8 us
    all_to_all x2, waiting for transfers between devices, spread(): lax.all_to_all(jnp.broadcast_to(block[None], (count,) + block.shape), axe...  17 us
  transfers between devices with their start and end apart: 29, of which 14 were waited for; matrix products, arithmetic and copies ran while one was open for 6% of the time, Pallas kernels for 13%

profile of v4, /device:TPU:2, one launch (start us, length us, event | category | flops | bytes accessed | tf_op | source)
XLA Modules:
  0.0 273.6 jit_solution(11982494977305668317)
XLA Ops:
  7.6 10.7 %all-to-all-start = ((bf16[32,32,256]{2,1,0:T(8,128)(2,1)}), bf16[32,32,256]{2,1,0:T(8,128)(2,1)S(1)}, u32[]{:S(2)}, u32[]{:S(2)}) async-start(bf16[32,32,256]{2,1,0:T(8,128)(2,1)} %broadcast_in_dim.92), calls=%async_computation | async-start | bytes 1048576 | tf_op jit(solution)/shard_map/all_to_all | solution.py:25
  26.5 4.7 %collective-permute-done = bf16[8,640]{1,0:T(8,128)(2,1)S(1)} collective-permute-done((bf16[8,640]{1,0:T(8,128)(2,1)S(1)}, bf16[8,640]{1,0:T(8,128)(2,1)S(1)}, u32[]{:S(2)}, u32[]{:S(2)}) %collective-permute-start) | collective-permute-done | bytes 10272 | tf_op jit(solution)/shard_map/ppermute | solution.py:183
  31.2 3.5 %collective-permute-start.2 = (bf16[8,640]{1,0:T(8,128)(2,1)S(1)}, bf16[8,640]{1,0:T(8,128)(2,1)S(1)}, u32[]{:S(2)}, u32[]{:S(2)}) collective-permute-start(bf16[8,640]{1,0:T(8,128)(2,1)S(1)} %get-tuple-element.36), channel_id=1, source_target_pairs={{0,40},{8,48},{16,56},{24,0},{32,8},{40,16},{48,24},{56,32},{1,41}... | collective-permute-start | bytes 30728 | tf_op jit(solution)/shard_map/ppermute | solution.py:183
  37.5 5.0 %collective-permute-start.4 = (bf16[8,640]{1,0:T(8,128)(2,1)S(1)}, bf16[8,640]{1,0:T(8,128)(2,1)S(1)}, u32[]{:S(2)}, u32[]{:S(2)}) collective-permute-start(bf16[8,640]{1,0:T(8,128)(2,1)S(1)} %get-tuple-element.34), channel_id=1, source_target_pairs={{0,24},{8,32},{16,40},{24,48},{32,56},{40,0},{48,8},{56,16},{1,25}... | collective-permute-start | bytes 30728 | tf_op jit(solution)/shard_map/ppermute | solution.py:183
  55.2 5.7 %all-to-all-start.1 = ((bf16[8,64,512]{2,1,0:T(8,128)(2,1)}), bf16[8,64,512]{2,1,0:T(8,128)(2,1)S(1)}, u32[]{:S(2)}, u32[]{:S(2)}) async-start(bf16[8,64,512]{2,1,0:T(8,128)(2,1)} %broadcast_in_dim.95), calls=%async_computation.1 | async-start | bytes 1048576 | tf_op jit(solution)/shard_map/all_to_all | solution.py:25
  61.6 17.0 %all-to-all-done.1 = bf16[8,64,512]{2,1,0:T(8,128)(2,1)S(1)} async-done(((bf16[8,64,512]{2,1,0:T(8,128)(2,1)}), bf16[8,64,512]{2,1,0:T(8,128)(2,1)S(1)}, u32[]{:S(2)}, u32[]{:S(2)}) %all-to-all-start.1) | async-done | bytes 524320 | tf_op jit(solution)/shard_map/all_to_all | solution.py:25
  80.0 4.8 %all-to-all-start.2 = ((bf16[8,8,8,512]{3,2,1,0:T(8,128)(2,1)}), bf16[8,8,8,512]{3,2,1,0:T(8,128)(2,1)S(1)}, u32[]{:S(2)}, u32[]{:S(2)}) async-start(bf16[8,8,8,512]{3,2,1,0:T(8,128)(2,1)} %copy.32), calls=%async_computation.2 | async-start | bytes 1048576 | tf_op jit(solution)/shard_map/all_to_all | solution.py:31
  87.5 6.1 %all-to-all-done.2 = bf16[8,8,8,512]{3,2,1,0:T(8,128)(2,1)S(1)} async-done(((bf16[8,8,8,512]{3,2,1,0:T(8,128)(2,1)}), bf16[8,8,8,512]{3,2,1,0:T(8,128)(2,1)S(1)}, u32[]{:S(2)}, u32[]{:S(2)}) %all-to-all-start.2) | async-done | bytes 524320 | tf_op jit(solution)/shard_map/all_to_all | solution.py:31
  95.1 6.3 %all-to-all-start.3 = ((bf16[64,16,512]{2,1,0:T(8,128)(2,1)}), bf16[64,16,512]{2,1,0:T(8,128)(2,1)}, u32[]{:S(2)}, u32[]{:S(2)}) async-start(bf16[64,16,512]{2,1,0:T(8,128)(2,1)} %bitcast.33), calls=%async_computation.3 | async-start | bytes 2097152 | tf_op jit(solution)/shard_map/all_to_all | solution.py:31
  102.1 28.2 %all-to-all-done.3.x_ref = bf16[64,16,512]{2,1,0:T(8,128)(2,1)} async-done(((bf16[64,16,512]{2,1,0:T(8,128)(2,1)}), bf16[64,16,512]{2,1,0:T(8,128)(2,1)}, u32[]{:S(2)}, u32[]{:S(2)}) %all-to-all-start.3) | async-done | bytes 1048608 | tf_op jit(solution)/shard_map/all_to_all | solution.py:31
  135.6 4.0 %all-to-all-start.4 = ((bf16[8,8,512]{2,1,0:T(8,128)(2,1)}), bf16[8,8,512]{2,1,0:T(8,128)(2,1)}, u32[]{:S(2)}, u32[]{:S(2)}) async-start(bf16[8,8,512]{2,1,0:T(8,128)(2,1)} %convert_element_type.212), calls=%async_computation.4 | async-start | bytes 131072 | tf_op jit(solution)/shard_map/all_to_all | solution.py:31
  144.0 9.0 %shard_map.123 = (bf16[64,4096]{1,0:T(8,128)(2,1)}, bf16[64,4096]{1,0:T(8,128)(2,1)}) custom-call(bf16[64,4096]{1,0:T(8,128)(2,1)} %get-tuple-element.16.low_ref, bf16[64,4096]{1,0:T(8,128)(2,1)} %get-tuple-element.17.high_ref, bf16[4096,384]{1,0:T(8,128)(2,1)} %bitcast.138, bf16[4096,384]{1,0:T(8,128)(2,1)} %bitcast.142, bf16[384,4096]{1,0:T(8,128)(2,1)} %bitcast.146), custom_call_target="tpu_custom_call" | custom-call | flops 1207959552 | bytes 11534336 | tf_op jit(solution)/shard_map/pallas_call | solution.py:119
  156.7 9.1 %shard_map.124 = (bf16[64,4096]{1,0:T(8,128)(2,1)}, bf16[64,4096]{1,0:T(8,128)(2,1)}) custom-call(bf16[64,4096]{1,0:T(8,128)(2,1)} %collective-permute-done.13.low_ref, bf16[64,4096]{1,0:T(8,128)(2,1)} %collective-permute-done.15.high_ref, bf16[4096,384]{1,0:T(8,128)(2,1)} %bitcast.139, bf16[4096,384]{1,0:T(8,128)(2,1)} %bitcast.143, ...), custom_call_target="tpu_custom_call" | custom-call | flops 1207959552 | bytes 11534336 | tf_op jit(solution)/shard_map/pallas_call | solution.py:119
  168.6 3.4 %collective-permute-done.16.high_ref = bf16[64,4096]{1,0:T(8,128)(2,1)} collective-permute-done((bf16[64,4096]{1,0:T(8,128)(2,1)}, bf16[64,4096]{1,0:T(8,128)(2,1)}, u32[]{:S(2)}, u32[]{:S(2)}) %collective-permute-start.16) | collective-permute-done | bytes 524320 | tf_op jit(solution)/shard_map/ppermute | solution.py:35
  172.0 9.0 %shard_map.125 = (bf16[64,4096]{1,0:T(8,128)(2,1)}, bf16[64,4096]{1,0:T(8,128)(2,1)}) custom-call(bf16[64,4096]{1,0:T(8,128)(2,1)} %collective-permute-done.14.low_ref, bf16[64,4096]{1,0:T(8,128)(2,1)} %collective-permute-done.16.high_ref, bf16[4096,384]{1,0:T(8,128)(2,1)} %bitcast.140, bf16[4096,384]{1,0:T(8,128)(2,1)} %bitcast.144, ...), custom_call_target="tpu_custom_call" | custom-call | flops 1207959552 | bytes 11534336 | tf_op jit(solution)/shard_map/pallas_call | solution.py:119
  181.6 9.1 %shard_map.126 = (bf16[64,4096]{1,0:T(8,128)(2,1)}, bf16[64,4096]{1,0:T(8,128)(2,1)}) custom-call(bf16[64,4096]{1,0:T(8,128)(2,1)} %collective-permute-done.11.low_ref, bf16[64,4096]{1,0:T(8,128)(2,1)} %collective-permute-done.12.high_ref, bf16[4096,384]{1,0:T(8,128)(2,1)} %bitcast.141, bf16[4096,384]{1,0:T(8,128)(2,1)} %bitcast.145, ...), custom_call_target="tpu_custom_call" | custom-call | flops 1207959552 | bytes 11534336 | tf_op jit(solution)/shard_map/pallas_call | solution.py:119
  190.7 3.3 %collective-permute-start.17 = (bf16[64,4096]{1,0:T(8,128)(2,1)}, bf16[64,4096]{1,0:T(8,128)(2,1)S(1)}, u32[]{:S(2)}, u32[]{:S(2)}) collective-permute-start(bf16[64,4096]{1,0:T(8,128)(2,1)} %get-tuple-element.21), channel_id=1, source_target_pairs={{0,192},{64,0},{128,64},{192,128},{1,193},{65,1},{129,65},{193,129... | collective-permute-start | bytes 1572872 | tf_op jit(solution)/shard_map/ppermute | solution.py:35
  194.0 3.2 %collective-permute-start.21 = (bf16[64,4096]{1,0:T(8,128)(2,1)}, bf16[64,4096]{1,0:T(8,128)(2,1)S(1)}, u32[]{:S(2)}, u32[]{:S(2)}) collective-permute-start(bf16[64,4096]{1,0:T(8,128)(2,1)} %get-tuple-element.25), channel_id=1, source_target_pairs={{0,192},{64,0},{128,64},{192,128},{1,193},{65,1},{129,65},{193,129... | collective-permute-start | bytes 1572872 | tf_op jit(solution)/shard_map/ppermute | solution.py:35
  198.7 15.6 %collective-permute-done.21 = bf16[64,4096]{1,0:T(8,128)(2,1)S(1)} collective-permute-done((bf16[64,4096]{1,0:T(8,128)(2,1)}, bf16[64,4096]{1,0:T(8,128)(2,1)S(1)}, u32[]{:S(2)}, u32[]{:S(2)}) %collective-permute-start.21) | collective-permute-done | bytes 524320 | tf_op jit(solution)/shard_map/ppermute | solution.py:35
  215.4 3.7 %collective-permute-start.22 = (bf16[64,4096]{1,0:T(8,128)(2,1)S(1)}, bf16[64,4096]{1,0:T(8,128)(2,1)S(1)}, u32[]{:S(2)}, u32[]{:S(2)}) collective-permute-start(bf16[64,4096]{1,0:T(8,128)(2,1)S(1)} %add_convert_fusion.1), channel_id=1, source_target_pairs={{0,192},{64,0},{128,64},{192,128},{1,193},{65,1},{129,65},{193,129... | collective-permute-start | bytes 1572872 | tf_op jit(solution)/shard_map/ppermute | solution.py:35
  219.3 7.5 %collective-permute-done.22 = bf16[64,4096]{1,0:T(8,128)(2,1)S(1)} collective-permute-done((bf16[64,4096]{1,0:T(8,128)(2,1)S(1)}, bf16[64,4096]{1,0:T(8,128)(2,1)S(1)}, u32[]{:S(2)}, u32[]{:S(2)}) %collective-permute-start.22) | collective-permute-done | bytes 524320 | tf_op jit(solution)/shard_map/ppermute | solution.py:35
  228.1 5.2 %all-to-all-start.5 = ((bf16[8,16,4096]{2,1,0:T(8,128)(2,1)}), bf16[8,16,4096]{2,1,0:T(8,128)(2,1)S(1)}, u32[]{:S(2)}, u32[]{:S(2)}) async-start(bf16[8,16,4096]{2,1,0:T(8,128)(2,1)} %bitcast.44), calls=%async_computation.5 | async-start | bytes 2097152 | tf_op jit(solution)/shard_map/all_to_all | solution.py:31
  234.6 13.2 %all-to-all-done.5 = bf16[8,16,4096]{2,1,0:T(8,128)(2,1)S(1)} async-done(((bf16[8,16,4096]{2,1,0:T(8,128)(2,1)}), bf16[8,16,4096]{2,1,0:T(8,128)(2,1)S(1)}, u32[]{:S(2)}, u32[]{:S(2)}) %all-to-all-start.5) | async-done | bytes 1048608 | tf_op jit(solution)/shard_map/all_to_all | solution.py:31
  248.5 24.3 %all_to_all.35 = bf16[8,8,4096]{2,1,0:T(8,128)(2,1)S(1)} all-to-all(bf16[8,8,4096]{2,1,0:T(8,128)(2,1)S(1)} %fusion.1), channel_id=1, replica_groups=mesh['y'=4,'z'=8,'x'=4,'core'=2] {'z'}, dimensions={0} | all-to-all | bytes 1048576 | tf_op jit(solution)/shard_map/all_to_all | solution.py:31
  (151 shorter events, 60.7 us)
Async XLA Ops:
  0.6 49.4 %collective-permute-start.7 = (bf16[512,128]{1,0:T(8,128)(2,1)}, bf16[512,128]{1,0:T(8,128)(2,1)S(1)}, u32[]{:S(2)}, u32[]{:S(2)}) collective-permute-start(bf16[512,128]{1,0:T(8,128)(2,1)} %param.15), channel_id=1, source_target_pairs={{0,192},{64,0},{128,64},{192,128},{1,193},{65,1},{129,65},{193,129... | collective-permute-start | bytes 393224 | tf_op jit(solution)/shard_map/ppermute | solution.py:35
  3.7 46.3 %collective-permute-start.8 = (bf16[512,128]{1,0:T(8,128)(2,1)}, bf16[512,128]{1,0:T(8,128)(2,1)S(1)}, u32[]{:S(2)}, u32[]{:S(2)}) collective-permute-start(bf16[512,128]{1,0:T(8,128)(2,1)} %param.15), channel_id=1, source_target_pairs={{0,128},{64,192},{128,0},{192,64},{1,129},{65,193},{129,1},{193,65... | collective-permute-start | bytes 393224 | tf_op jit(solution)/shard_map/ppermute | solution.py:35
  4.4 45.8 %collective-permute-start.9 = (bf16[512,128]{1,0:T(8,128)(2,1)}, bf16[512,128]{1,0:T(8,128)(2,1)S(1)}, u32[]{:S(2)}, u32[]{:S(2)}) collective-permute-start(bf16[512,128]{1,0:T(8,128)(2,1)} %param.15), channel_id=1, source_target_pairs={{0,64},{64,128},{128,192},{192,0},{1,65},{65,129},{129,193},{193,1... | collective-permute-start | bytes 393224 | tf_op jit(solution)/shard_map/ppermute | solution.py:35
  7.6 42.5 %all-to-all-start = ((bf16[32,32,256]{2,1,0:T(8,128)(2,1)}), bf16[32,32,256]{2,1,0:T(8,128)(2,1)S(1)}, u32[]{:S(2)}, u32[]{:S(2)}) async-start(bf16[32,32,256]{2,1,0:T(8,128)(2,1)} %broadcast_in_dim.92), calls=%async_computation | async-start | bytes 1048576 | tf_op jit(solution)/shard_map/all_to_all | solution.py:25
  20.9 10.3 %collective-permute-start = (bf16[8,640]{1,0:T(8,128)(2,1)S(1)}, bf16[8,640]{1,0:T(8,128)(2,1)S(1)}, u32[]{:S(2)}, u32[]{:S(2)}) collective-permute-start(bf16[8,640]{1,0:T(8,128)(2,1)S(1)} %get-tuple-element.38), channel_id=1, source_target_pairs={{0,56},{8,0},{16,8},{24,16},{32,24},{40,32},{48,40},{56,48},{1,57}... | collective-permute-start | bytes 30728 | tf_op jit(solution)/shard_map/ppermute | solution.py:183
  23.9 10.8 %collective-permute-start.1 = (bf16[8,640]{1,0:T(8,128)(2,1)S(1)}, bf16[8,640]{1,0:T(8,128)(2,1)S(1)}, u32[]{:S(2)}, u32[]{:S(2)}) collective-permute-start(bf16[8,640]{1,0:T(8,128)(2,1)S(1)} %get-tuple-element.37), channel_id=1, source_target_pairs={{0,48},{8,56},{16,0},{24,8},{32,16},{40,24},{48,32},{56,40},{1,49}... | collective-permute-start | bytes 30728 | tf_op jit(solution)/shard_map/ppermute | solution.py:183
  34.7 7.8 %collective-permute-start.3 = (bf16[8,640]{1,0:T(8,128)(2,1)S(1)}, bf16[8,640]{1,0:T(8,128)(2,1)S(1)}, u32[]{:S(2)}, u32[]{:S(2)}) collective-permute-start(bf16[8,640]{1,0:T(8,128)(2,1)S(1)} %get-tuple-element.35), channel_id=1, source_target_pairs={{0,32},{8,40},{16,48},{24,56},{32,0},{40,8},{48,16},{56,24},{1,33}... | collective-permute-start | bytes 30728 | tf_op jit(solution)/shard_map/ppermute | solution.py:183
  55.2 23.5 %all-to-all-start.1 = ((bf16[8,64,512]{2,1,0:T(8,128)(2,1)}), bf16[8,64,512]{2,1,0:T(8,128)(2,1)S(1)}, u32[]{:S(2)}, u32[]{:S(2)}) async-start(bf16[8,64,512]{2,1,0:T(8,128)(2,1)} %broadcast_in_dim.95), calls=%async_computation.1 | async-start | bytes 1048576 | tf_op jit(solution)/shard_map/all_to_all | solution.py:25
  80.0 13.7 %all-to-all-start.2 = ((bf16[8,8,8,512]{3,2,1,0:T(8,128)(2,1)}), bf16[8,8,8,512]{3,2,1,0:T(8,128)(2,1)S(1)}, u32[]{:S(2)}, u32[]{:S(2)}) async-start(bf16[8,8,8,512]{3,2,1,0:T(8,128)(2,1)} %copy.32), calls=%async_computation.2 | async-start | bytes 1048576 | tf_op jit(solution)/shard_map/all_to_all | solution.py:31
  95.1 35.2 %all-to-all-start.3 = ((bf16[64,16,512]{2,1,0:T(8,128)(2,1)}), bf16[64,16,512]{2,1,0:T(8,128)(2,1)}, u32[]{:S(2)}, u32[]{:S(2)}) async-start(bf16[64,16,512]{2,1,0:T(8,128)(2,1)} %bitcast.33), calls=%async_computation.3 | async-start | bytes 2097152 | tf_op jit(solution)/shard_map/all_to_all | solution.py:31
  132.9 21.0 %collective-permute-start.13 = (bf16[64,4096]{1,0:T(8,128)(2,1)}, bf16[64,4096]{1,0:T(8,128)(2,1)}, u32[]{:S(2)}, u32[]{:S(2)}) collective-permute-start(bf16[64,4096]{1,0:T(8,128)(2,1)} %get-tuple-element.16.low_ref), channel_id=1, source_target_pairs={{0,192},{64,0},{128,64},{192,128},{1,193},{65,1},{129,65},{193,129... | collective-permute-start | bytes 1572872 | tf_op jit(solution)/shard_map/ppermute | solution.py:35
  135.6 20.4 %collective-permute-start.15 = (bf16[64,4096]{1,0:T(8,128)(2,1)}, bf16[64,4096]{1,0:T(8,128)(2,1)}, u32[]{:S(2)}, u32[]{:S(2)}) collective-permute-start(bf16[64,4096]{1,0:T(8,128)(2,1)} %get-tuple-element.17.high_ref), channel_id=1, source_target_pairs={{0,64},{64,128},{128,192},{192,0},{1,65},{65,129},{129,193},{193,1... | collective-permute-start | bytes 1572872 | tf_op jit(solution)/shard_map/ppermute | solution.py:35
  135.6 17.3 %all-to-all-start.4 = ((bf16[8,8,512]{2,1,0:T(8,128)(2,1)}), bf16[8,8,512]{2,1,0:T(8,128)(2,1)}, u32[]{:S(2)}, u32[]{:S(2)}) async-start(bf16[8,8,512]{2,1,0:T(8,128)(2,1)} %convert_element_type.212), calls=%async_computation.4 | async-start | bytes 131072 | tf_op jit(solution)/shard_map/all_to_all | solution.py:31
  140.7 40.9 %collective-permute-start.11 = (bf16[64,4096]{1,0:T(8,128)(2,1)}, bf16[64,4096]{1,0:T(8,128)(2,1)}, u32[]{:S(2)}, u32[]{:S(2)}) collective-permute-start(bf16[64,4096]{1,0:T(8,128)(2,1)} %get-tuple-element.16.low_ref), channel_id=1, source_target_pairs={{0,64},{64,128},{128,192},{192,0},{1,65},{65,129},{129,193},{193,1... | collective-permute-start | bytes 1572872 | tf_op jit(solution)/shard_map/ppermute | solution.py:35
  141.5 40.2 %collective-permute-start.12 = (bf16[64,4096]{1,0:T(8,128)(2,1)}, bf16[64,4096]{1,0:T(8,128)(2,1)}, u32[]{:S(2)}, u32[]{:S(2)}) collective-permute-start(bf16[64,4096]{1,0:T(8,128)(2,1)} %get-tuple-element.17.high_ref), channel_id=1, source_target_pairs={{0,192},{64,0},{128,64},{192,128},{1,193},{65,1},{129,65},{193,129... | collective-permute-start | bytes 1572872 | tf_op jit(solution)/shard_map/ppermute | solution.py:35
  153.9 14.7 %collective-permute-start.14 = (bf16[64,4096]{1,0:T(8,128)(2,1)}, bf16[64,4096]{1,0:T(8,128)(2,1)}, u32[]{:S(2)}, u32[]{:S(2)}) collective-permute-start(bf16[64,4096]{1,0:T(8,128)(2,1)} %collective-permute-done.13.low_ref), channel_id=1, source_target_pairs={{0,192},{64,0},{128,64},{192,128},{1,193},{65,1},{129,65},{193,129... | collective-permute-start | bytes 1572872 | tf_op jit(solution)/shard_map/ppermute | solution.py:35
  156.0 16.0 %collective-permute-start.16 = (bf16[64,4096]{1,0:T(8,128)(2,1)}, bf16[64,4096]{1,0:T(8,128)(2,1)}, u32[]{:S(2)}, u32[]{:S(2)}) collective-permute-start(bf16[64,4096]{1,0:T(8,128)(2,1)} %collective-permute-done.15.high_ref), channel_id=1, source_target_pairs={{0,64},{64,128},{128,192},{192,0},{1,65},{65,129},{129,193},{193,1... | collective-permute-start | bytes 1572872 | tf_op jit(solution)/shard_map/ppermute | solution.py:35
  181.0 16.2 %collective-permute-start.18 = (bf16[64,4096]{1,0:T(8,128)(2,1)}, bf16[64,4096]{1,0:T(8,128)(2,1)}, u32[]{:S(2)}, u32[]{:S(2)}) collective-permute-start(bf16[64,4096]{1,0:T(8,128)(2,1)} %get-tuple-element.20.refs_0_), channel_id=1, source_target_pairs={{0,64},{64,128},{128,192},{192,0},{1,65},{65,129},{129,193},{193,1... | collective-permute-start | bytes 1572872 | tf_op jit(solution)/shard_map/ppermute | solution.py:35
  190.7 28.3 %collective-permute-start.17 = (bf16[64,4096]{1,0:T(8,128)(2,1)}, bf16[64,4096]{1,0:T(8,128)(2,1)S(1)}, u32[]{:S(2)}, u32[]{:S(2)}) collective-permute-start(bf16[64,4096]{1,0:T(8,128)(2,1)} %get-tuple-element.21), channel_id=1, source_target_pairs={{0,192},{64,0},{128,64},{192,128},{1,193},{65,1},{129,65},{193,129... | collective-permute-start | bytes 1572872 | tf_op jit(solution)/shard_map/ppermute | solution.py:35
  194.0 25.3 %collective-permute-start.20 = (bf16[64,4096]{1,0:T(8,128)(2,1)}, bf16[64,4096]{1,0:T(8,128)(2,1)S(1)}, u32[]{:S(2)}, u32[]{:S(2)}) collective-permute-start(bf16[64,4096]{1,0:T(8,128)(2,1)} %get-tuple-element.23), channel_id=1, source_target_pairs={{0,64},{64,128},{128,192},{192,0},{1,65},{65,129},{129,193},{193,1... | collective-permute-start | bytes 1572872 | tf_op jit(solution)/shard_map/ppermute | solution.py:35
  194.0 20.2 %collective-permute-start.21 = (bf16[64,4096]{1,0:T(8,128)(2,1)}, bf16[64,4096]{1,0:T(8,128)(2,1)S(1)}, u32[]{:S(2)}, u32[]{:S(2)}) collective-permute-start(bf16[64,4096]{1,0:T(8,128)(2,1)} %get-tuple-element.25), channel_id=1, source_target_pairs={{0,192},{64,0},{128,64},{192,128},{1,193},{65,1},{129,65},{193,129... | collective-permute-start | bytes 1572872 | tf_op jit(solution)/shard_map/ppermute | solution.py:35
  198.6 20.5 %collective-permute-start.19 = (bf16[64,4096]{1,0:T(8,128)(2,1)S(1)}, bf16[64,4096]{1,0:T(8,128)(2,1)S(1)}, u32[]{:S(2)}, u32[]{:S(2)}) collective-permute-start(bf16[64,4096]{1,0:T(8,128)(2,1)S(1)} %add_convert_fusion.3), channel_id=1, source_target_pairs={{0,64},{64,128},{128,192},{192,0},{1,65},{65,129},{129,193},{193,1... | collective-permute-start | bytes 1572872 | tf_op jit(solution)/shard_map/ppermute | solution.py:35
  215.4 11.4 %collective-permute-start.22 = (bf16[64,4096]{1,0:T(8,128)(2,1)S(1)}, bf16[64,4096]{1,0:T(8,128)(2,1)S(1)}, u32[]{:S(2)}, u32[]{:S(2)}) collective-permute-start(bf16[64,4096]{1,0:T(8,128)(2,1)S(1)} %add_convert_fusion.1), channel_id=1, source_target_pairs={{0,192},{64,0},{128,64},{192,128},{1,193},{65,1},{129,65},{193,129... | collective-permute-start | bytes 1572872 | tf_op jit(solution)/shard_map/ppermute | solution.py:35
  228.1 19.7 %all-to-all-start.5 = ((bf16[8,16,4096]{2,1,0:T(8,128)(2,1)}), bf16[8,16,4096]{2,1,0:T(8,128)(2,1)S(1)}, u32[]{:S(2)}, u32[]{:S(2)}) async-start(bf16[8,16,4096]{2,1,0:T(8,128)(2,1)} %bitcast.44), calls=%async_computation.5 | async-start | bytes 2097152 | tf_op jit(solution)/shard_map/all_to_all | solution.py:31
  (12 other events, 205.2 us)

commit v5 on v3

--- a/solution.py
+++ b/solution.py
@@ -1,3 +1,5 @@
+import functools
+
 import jax
 import jax.numpy as jnp
 from jax import lax
@@ -16,6 +18,7 @@
 CTX = ("y", "z")
 EXP = ("x", "core")
 LANES = X * CORE
+VMEM_LIMIT = 65024 * 1024
 BF16 = jnp.bfloat16
 F32 = jnp.float32
 
@@ -64,7 +67,7 @@
         out_shape=[jax.ShapeDtypeStruct((rows, D), BF16)] * 2,
         in_specs=[pl.BlockSpec(memory_space=pltpu.VMEM)] * 2,
         out_specs=[pl.BlockSpec(memory_space=pltpu.VMEM)] * 2,
-        compiler_params=pltpu.CompilerParams(vmem_limit_bytes=32 * 1024 * 1024),
+        compiler_params=pltpu.CompilerParams(vmem_limit_bytes=VMEM_LIMIT),
         cost_estimate=pl.CostEstimate(flops=6 * rows * D, bytes_accessed=8 * rows * D, transcendentals=0),
     )(inbox, gain.reshape(1, D))
 
@@ -72,70 +75,129 @@
 STEPS = 4
 
 
-def expert_kernel(
-    low_ref, high_ref, gate_ref, up_ref, down_ref, out_low_ref, out_high_ref, gate_sum, up_sum, inner
-):
-    step = pl.program_id(0)
-    depth = gate_ref.shape[0]
-    rows = low_ref.shape[0]
-
-    @pl.when(step < STEPS)
-    def _():
-        columns = pl.ds(pl.multiple_of(step * depth, depth), depth)
-        x = jnp.concatenate([low_ref[:, columns], high_ref[:, columns]], axis=0)
-        gate_h = jnp.dot(x, gate_ref[...], preferred_element_type=F32)
-        up_h = jnp.dot(x, up_ref[...], preferred_element_type=F32)
-
-        @pl.when(step == 0)
-        def _():
-            gate_sum[...] = gate_h
-            up_sum[...] = up_h
-
-        @pl.when(step > 0)
-        def _():
-            gate_sum[...] += gate_h
-            up_sum[...] += up_h
-
-    @pl.when(step == STEPS - 1)
-    def _():
-        v = gate_sum[...]
-        inner[...] = (v / (1.0 + jnp.exp(-v)) * up_sum[...]).astype(BF16)
-
-    @pl.when(step >= STEPS)
-    def _():
-        out = jnp.dot(inner[...], down_ref[...], preferred_element_type=F32).astype(BF16)
-        out_low_ref[...] = out[:rows]
-        out_high_ref[...] = out[rows:]
-
-
-def expert(low, high, w_gate, w_up, w_down):
-    rows = low.shape[0]
-    width = w_gate.shape[1]
+def expert_kernel(count, *refs):
+    blocks, (gate_ref, up_ref, down_ref) = refs[:count], refs[count : count + 3]
+    x, gate_w, up_w, down_w, out, in_sems, weight_sems, out_sems = refs[-8:]
+    outs = refs[-8 - count : -8]
+    rows = blocks[0].shape[0]
     piece = D // STEPS
-    whole = pl.BlockSpec((rows, D), lambda i: (0, 0))
-    into = pl.BlockSpec((piece, width), lambda i: (jnp.minimum(i, STEPS - 1), 0))
-    out_of = pl.BlockSpec((width, piece), lambda i: (0, jnp.maximum(i - STEPS, 0)))
-    result = pl.BlockSpec((rows, piece), lambda i: (0, jnp.maximum(i - STEPS, 0)))
+    parts = [slice(i * piece, (i + 1) * piece) for i in range(STEPS)]
+    own_rows = [slice(j * rows, (j + 1) * rows) for j in range(count)]
+    row_copies, weight_copies, down_copies, out_copies = [], [], [], []
+    for i, part in enumerate(parts):
+        row_copies.append(
+            [
+                pltpu.make_async_copy(block.at[:, part], x.at[own, part], in_sems.at[i, j])
+                for j, (block, own) in enumerate(zip(blocks, own_rows))
+            ]
+        )
+        weight_copies.append(
+            [
+                pltpu.make_async_copy(gate_ref.at[part], gate_w.at[part], weight_sems.at[0, i]),
+                pltpu.make_async_copy(up_ref.at[part], up_w.at[part], weight_sems.at[1, i]),
+            ]
+        )
+        down_copies.append(
+            pltpu.make_async_copy(down_ref.at[:, part], down_w.at[:, part], weight_sems.at[2, i])
+        )
+        out_copies.append(
+            [
+                pltpu.make_async_copy(out.at[own, part], out_ref.at[:, part], out_sems.at[i, j])
+                for j, (out_ref, own) in enumerate(zip(outs, own_rows))
+            ]
+        )
+    for i in range(STEPS):
+        for copy in row_copies[i] + weight_copies[i]:
+            copy.start()
+    for copy in down_copies:
+        copy.start()
+    gate_h, up_h = 0.0, 0.0
+    for i, part in enumerate(parts):
+        for copy in row_copies[i] + weight_copies[i]:
+            copy.wait()
+        gate_h = gate_h + jnp.dot(x[:, part], gate_w[part], preferred_element_type=F32)
+        up_h = up_h + jnp.dot(x[:, part], up_w[part], preferred_element_type=F32)
+    inner = (gate_h / (1.0 + jnp.exp(-gate_h)) * up_h).astype(BF16)
+    for i, part in enumerate(parts):
+        down_copies[i].wait()
+        out[:, part] = jnp.dot(inner, down_w[:, part], preferred_element_type=F32).astype(BF16)
+        for copy in out_copies[i]:
+            copy.start()
+    for copies in out_copies:
+        for copy in copies:
+            copy.wait()
+
+
+def expert(blocks, weights, after=()):
+    rows = blocks[0].shape[0]
+    count = len(blocks)
+    width = weights[0].shape[1]
     return pl.pallas_call(
-        expert_kernel,
-        grid=(2 * STEPS,),
-        out_shape=[jax.ShapeDtypeStruct((rows, D), BF16)] * 2,
-        in_specs=[whole, whole, into, into, out_of],
-        out_specs=[result, result],
+        functools.partial(expert_kernel, count),
+        out_shape=[jax.ShapeDtypeStruct((rows, D), BF16)] * count,
+        in_specs=[pl.BlockSpec(memory_space=pl.ANY)] * (count + 3 + len(after)),
+        out_specs=[pl.BlockSpec(memory_space=pl.ANY)] * count,
         scratch_shapes=[
-            pltpu.VMEM((2 * rows, width), F32),
-            pltpu.VMEM((2 * rows, width), F32),
-            pltpu.VMEM((2 * rows, width), BF16),
+            pltpu.VMEM((count * rows, D), BF16),
+            pltpu.VMEM((D, width), BF16),
+            pltpu.VMEM((D, width), BF16),
+            pltpu.VMEM((width, D), BF16),
+            pltpu.VMEM((count * rows, D), BF16),
+            pltpu.SemaphoreType.DMA((STEPS, count)),
+            pltpu.SemaphoreType.DMA((3, STEPS)),
+            pltpu.SemaphoreType.DMA((STEPS, count)),
         ],
+        compiler_params=pltpu.CompilerParams(vmem_limit_bytes=VMEM_LIMIT),
+        cost_estimate=pl.CostEstimate(
+            flops=6 * count * rows * D * width,
+            bytes_accessed=6 * D * width + 4 * count * rows * D,
+            transcendentals=count * rows * width,
+        ),
+    )(*blocks, *weights, *after)
+
+
+def add_kernel(count, *refs):
+    out_ref = refs[-1]
+    rows = refs[0].shape[0]
+    for i in range(2):
+        total = refs[i * count][...].astype(F32)
+        for ref in refs[i * count + 1 : (i + 1) * count]:
+            total = total + ref[...].astype(F32)
+        out_ref[i * rows : (i + 1) * rows] = total.astype(BF16)
+
+
+def pair_kernel(count, *refs):
+    for i, out_ref in enumerate(refs[-2:]):
+        total = refs[i * count][...].astype(F32)
+        for ref in refs[i * count + 1 : (i + 1) * count]:
+            total = total + ref[...].astype(F32)
+        out_ref[...] = total.astype(BF16)
+
+
+def add_up(terms, after, joined):
+    rows = terms[0][0].shape[0]
+    count = len(terms[0])
+    piece = D // 2
+    block = pl.BlockSpec((rows, piece), lambda i: (0, i))
+    if joined:
+        kernel, blocks, results = add_kernel, pl.BlockSpec((2 * rows, piece), lambda i: (0, i)), 1
+    else:
+        kernel, blocks, results = pair_kernel, block, 2
+    return pl.pallas_call(
+        functools.partial(kernel, count),
+        grid=(D // piece,),
+        out_shape=[jax.ShapeDtypeStruct((2 * rows // results, D), BF16)] * results,
+        in_specs=[block] * (2 * count) + [pl.BlockSpec(memory_space=pl.ANY) for _ in after],
+        out_specs=[blocks] * results,
         compiler_params=pltpu.CompilerParams(
-            dimension_semantics=("arbitrary",), vmem_limit_bytes=32 * 1024 * 1024
+            dimension_semantics=("arbitrary",), vmem_limit_bytes=VMEM_LIMIT
         ),
         cost_estimate=pl.CostEstimate(
-            flops=12 * rows * D * width,
-            bytes_accessed=6 * D * width + 8 * rows * D,
-            transcendentals=2 * rows * width,
+            flops=2 * count * rows * D,
+            bytes_accessed=4 * (count + 1) * rows * D,
+            transcendentals=0,
         ),
-    )(low, high, w_gate, w_up, w_down)
+    )(*terms[0], *terms[1], *after)
 
 
 def slots_of(routes):
@@ -232,7 +294,6 @@
     pick = pick.reshape(Z * LANES * Z * MOST, Z * rows).astype(BF16)
     outbox = jnp.dot(pick, residual_c, preferred_element_type=F32).astype(BF16)
     inbox = swap(outbox.reshape(Z * LANES, Z * MOST, piece), ("z",) + EXP)
-    inbox, projected_c = lax.optimization_barrier((inbox, projected_c.astype(BF16)))
     slots = LANES * Z * MOST
     low, high = normalise(inbox, norm_gain)
 
@@ -243,25 +304,34 @@
     across_low = shift(after_low, -1)
     across_high = shift(before_high, 1)
 
-    projected = swap(projected_c, "z").reshape(Z, rows, Y, HEAD_SIZE)
+    projected = swap(projected_c.astype(BF16), "z").reshape(Z, rows, Y, HEAD_SIZE)
     projected = projected.transpose(1, 2, 0, 3).reshape(rows, D)
-    residual = hidden.astype(F32) + projected.astype(F32)
-    attended = residual.astype(BF16)
 
     weights = (w_gate[0], w_up[0], w_down[0])
-    own_low, own_high = expert(low, high, *weights)
-    out_after_low, out_before_high = expert(after_low, before_high, *weights)
-    out_before_low, out_after_high = expert(before_low, after_high, *weights)
+    (
+        own_low,
+        own_high,
+        out_after_low,
+        out_before_high,
+        out_before_low,
+        out_after_high,
+    ) = expert(
+        (low, high, after_low, before_high, before_low, after_high), weights, after=(projected,)
+    )
+    out_across_low, out_across_high = expert(
+        (across_low, across_high), weights, after=(own_low,)
+    )
     home_low = shift(out_before_low, -1)
     home_high = shift(out_after_high, 1)
-    out_across_low, out_across_high = expert(across_low, across_high, *weights)
     far_low = shift(out_across_low, 1)
     far_high = shift(out_across_high, -1)
-    sum_low = shift((out_after_low.astype(F32) + far_low.astype(F32)).astype(BF16), 1)
-    sum_high = shift((out_before_high.astype(F32) + far_high.astype(F32)).astype(BF16), -1)
-    home_low = own_low.astype(F32) + home_low.astype(F32) + sum_low.astype(F32)
-    home_high = own_high.astype(F32) + home_high.astype(F32) + sum_high.astype(F32)
-    returned = jnp.concatenate([home_low.astype(BF16), home_high.astype(BF16)], axis=0)
+    sum_low, sum_high = add_up(
+        ((out_after_low, far_low), (out_before_high, far_high)), (home_low, home_high), False
+    )
+    sum_low, sum_high = shift(sum_low, 1), shift(sum_high, -1)
+    (returned,) = add_up(
+        ((own_low, home_low, sum_low), (own_high, home_high, sum_high)), (), True
+    )
 
     back = swap(returned.reshape(LANES, Z * MOST, D), EXP).reshape(slots, D)
     gate = jnp.sum(jnp.where(named, gates_c[..., None], 0.0), axis=2)
@@ -275,6 +345,8 @@
         place_low, back, preferred_element_type=F32
     )
     moe = jnp.sum(swap(moe_z.astype(BF16).reshape(Z, rows, D), "z").astype(F32), axis=0)
+    residual = hidden.astype(F32) + projected.astype(F32)
+    attended = residual.astype(BF16)
     mixed = (residual + moe).astype(BF16)
     return (attended, mixed)
 

time: 268 us -> 240 us (0.90)
  blocking collectives: 0 us -> 65.5 us
  waiting for transfers between devices: 140 us -> 82.1 us
  local copies, waits for them, and re-layouts: 25 us -> 7.94 us
  starting transfers between devices: 62.7 us -> 49.5 us
  other arithmetic: 11.1 us -> 4.61 us
  Pallas kernels: 21.2 us -> 24.3 us
    all_to_all x0 -> x3, blocking collectives: none -> 65.5 us  [swap(): return lax.all_to_all(blocks, axes, 0, 0, tiled=True)]
    all_to_all x6 -> x3, waiting for transfers between devices: 89.4 us -> 39.8 us  [swap(): return lax.all_to_all(blocks, axes, 0, 0, tiled=True)]
    all_to_all x6 -> x3, starting transfers between devices: 30.6 us -> 14.8 us  [swap(): return lax.all_to_all(blocks, axes, 0, 0, tiled=True)]
    unnamed x35 -> x19, local copies, waits for them, and re-layouts: 10.6 us -> 0.15 us
    ppermute x15, waiting for transfers between devices: 44.7 us -> 36.5 us  [shift(): return lax.ppermute(block, 'y', [(i, (i + step) % Y) for i in range(Y)])]
  transfers between devices with their start and end apart: 23 -> 20, of which waited for: 14 -> 10; matrix products, arithmetic and copies ran while one was open for 7% -> 3% of each run, Pallas kernels for 7% -> 7%
where the time goes in v5:
time: 240 us; the launch traced here: 238 us
  waiting for transfers between devices  82.1 us (34%)
  blocking collectives  65.5 us (27%)
  starting transfers between devices  49.5 us (21%)
  Pallas kernels  24.3 us (10%)
  local copies, waits for them, and re-layouts  7.94 us (3%)
  other arithmetic  4.61 us (2%)
  matrix products  3.35 us (1%)
    all_to_all x3, blocking collectives, swap(): return lax.all_to_all(blocks, axes, 0, 0, tiled=True)  65.5 us
    all_to_all x3, waiting for transfers between devices, swap(): return lax.all_to_all(blocks, axes, 0, 0, tiled=True)  39.8 us
    ppermute x15, waiting for transfers between devices, shift(): return lax.ppermute(block, 'y', [(i, (i + step) % Y) for i in range(Y)])  36.5 us
    ppermute x15, starting transfers between devices, shift(): return lax.ppermute(block, 'y', [(i, (i + step) % Y) for i in range(Y)])  23.2 us
    pallas_call x2, Pallas kernels, expert(): pl.pallas_call(functools.partial(expert_kernel, count), out_shape=[jax.Sh...  16.4 us
    all_to_all x3, starting transfers between devices, swap(): return lax.all_to_all(blocks, axes, 0, 0, tiled=True)  14.8 us
    all_to_all x1, starting transfers between devices, spread(): lax.all_to_all(jnp.broadcast_to(block[None], (count,) + block.shape), axe...  11.5 us
    pallas_call x2, Pallas kernels, add_up(): pl.pallas_call(functools.partial(kernel, count), grid=(D // piece,), out_...  5.3 us
  transfers between devices with their start and end apart: 20, of which 10 were waited for; matrix products, arithmetic and copies ran while one was open for 3% of the time, Pallas kernels for 7%

profile of v5, /device:TPU:2, one launch (start us, length us, event | category | flops | bytes accessed | tf_op | source)
XLA Modules:
  0.0 238.4 jit_solution(3564092067450071778)
XLA Ops:
  3.0 11.5 %all-to-all-start = ((bf16[32,32,256]{2,1,0:T(8,128)(2,1)}), bf16[32,32,256]{2,1,0:T(8,128)(2,1)S(1)}, u32[]{:S(2)}, u32[]{:S(2)}) async-start(bf16[32,32,256]{2,1,0:T(8,128)(2,1)} %broadcast_in_dim.54), calls=%async_computation | async-start | bytes 1048576 | tf_op jit(solution)/shard_map/all_to_all | solution.py:27
  14.6 3.1 %collective-permute-start = (bf16[512,128]{1,0:T(8,128)(2,1)S(1)}, bf16[512,128]{1,0:T(8,128)(2,1)S(1)}, u32[]{:S(2)}, u32[]{:S(2)}) collective-permute-start(bf16[512,128]{1,0:T(8,128)(2,1)S(1)} %copy-done), channel_id=1, source_target_pairs={{0,192},{64,0},{128,64},{192,128},{1,193},{65,1},{129,65},{193,129... | collective-permute-start | bytes 393224 | tf_op jit(solution)/shard_map/ppermute | solution.py:37
  19.7 7.4 %collective-permute-done = bf16[512,128]{1,0:T(8,128)(2,1)S(1)} collective-permute-done((bf16[512,128]{1,0:T(8,128)(2,1)S(1)}, bf16[512,128]{1,0:T(8,128)(2,1)S(1)}, u32[]{:S(2)}, u32[]{:S(2)}) %collective-permute-start) | collective-permute-done | bytes 131104 | tf_op jit(solution)/shard_map/ppermute | solution.py:37
  27.1 4.3 %all-to-all-done = bf16[32,32,256]{2,1,0:T(8,128)(2,1)S(1)} async-done(((bf16[32,32,256]{2,1,0:T(8,128)(2,1)}), bf16[32,32,256]{2,1,0:T(8,128)(2,1)S(1)}, u32[]{:S(2)}, u32[]{:S(2)}) %all-to-all-start) | async-done | bytes 524320 | tf_op jit(solution)/shard_map/all_to_all | solution.py:27
  36.5 4.4 %all-to-all-start.1 = ((bf16[8,80,512]{2,1,0:T(8,128)(2,1)}), bf16[8,80,512]{2,1,0:T(8,128)(2,1)S(1)}, u32[]{:S(2)}, u32[]{:S(2)}) async-start(bf16[8,80,512]{2,1,0:T(8,128)(2,1)} %pad_maximum_fusion), calls=%async_computation.1 | async-start | bytes 1310720 | tf_op jit(solution)/shard_map/all_to_all | solution.py:33
  41.8 19.8 %all-to-all-done.1 = bf16[8,80,512]{2,1,0:T(8,128)(2,1)S(1)} async-done(((bf16[8,80,512]{2,1,0:T(8,128)(2,1)}), bf16[8,80,512]{2,1,0:T(8,128)(2,1)S(1)}, u32[]{:S(2)}, u32[]{:S(2)}) %all-to-all-start.1) | async-done | bytes 655392 | tf_op jit(solution)/shard_map/all_to_all | solution.py:33
  63.6 4.8 %all-to-all-start.2 = ((bf16[8,8,8,512]{3,2,1,0:T(8,128)(2,1)}), bf16[8,8,8,512]{3,2,1,0:T(8,128)(2,1)S(1)}, u32[]{:S(2)}, u32[]{:S(2)}) async-start(bf16[8,8,8,512]{3,2,1,0:T(8,128)(2,1)} %copy.28), calls=%async_computation.2 | async-start | bytes 1048576 | tf_op jit(solution)/shard_map/all_to_all | solution.py:33
  71.2 6.1 %all-to-all-done.2 = bf16[8,8,8,512]{3,2,1,0:T(8,128)(2,1)S(1)} async-done(((bf16[8,8,8,512]{3,2,1,0:T(8,128)(2,1)}), bf16[8,8,8,512]{3,2,1,0:T(8,128)(2,1)S(1)}, u32[]{:S(2)}, u32[]{:S(2)}) %all-to-all-start.2) | async-done | bytes 524320 | tf_op jit(solution)/shard_map/all_to_all | solution.py:33
  77.9 34.3 %all_to_all.35.x_ref = bf16[64,16,512]{2,1,0:T(8,128)(2,1)} all-to-all(bf16[64,16,512]{2,1,0:T(8,128)(2,1)S(1)} %bitcast.88), channel_id=1, replica_groups=mesh['y'=4,'z'=8,'x'=4,'core'=2] {'z','x','core'}, dimensions={0} | all-to-all | bytes 2097152 | tf_op jit(solution)/shard_map/all_to_all | solution.py:33
  120.0 9.9 %collective-permute-done.4.refs_2_ = bf16[64,4096]{1,0:T(8,128)(2,1)} collective-permute-done((bf16[64,4096]{1,0:T(8,128)(2,1)}, bf16[64,4096]{1,0:T(8,128)(2,1)}, u32[]{:S(2)}, u32[]{:S(2)}) %collective-permute-start.4) | collective-permute-done | bytes 524320 | tf_op jit(solution)/shard_map/ppermute | solution.py:37
  129.9 2.9 %collective-permute-start.9 = (bf16[64,4096]{1,0:T(8,128)(2,1)}, bf16[64,4096]{1,0:T(8,128)(2,1)}, u32[]{:S(2)}, u32[]{:S(2)}) collective-permute-start(bf16[64,4096]{1,0:T(8,128)(2,1)} %collective-permute-done.4.refs_2_), channel_id=1, source_target_pairs={{0,192},{64,0},{128,64},{192,128},{1,193},{65,1},{129,65},{193,129... | collective-permute-start | bytes 1572872 | tf_op jit(solution)/shard_map/ppermute | solution.py:37
  132.9 11.1 %all_to_all.36 = bf16[8,8,512]{2,1,0:T(8,128)(2,1)S(1)} all-to-all(bf16[8,8,512]{2,1,0:T(8,128)(2,1)S(1)} %convert_element_type.162), channel_id=1, replica_groups=mesh['y'=4,'z'=8,'x'=4,'core'=2] {'z'}, dimensions={0} | all-to-all | bytes 131072 | tf_op jit(solution)/shard_map/all_to_all | solution.py:33
  144.7 9.8 %shard_map.123 = (bf16[64,4096]{1,0:T(8,128)(2,1)}, bf16[64,4096]{1,0:T(8,128)(2,1)}, bf16[64,4096]{1,0:T(8,128)(2,1)}, bf16[64,4096]{1,0:T(8,128)(2,1)}, bf16[6...) custom-call(bf16[64,4096]{1,0:T(8,128)(2,1)} %get-tuple-element.14.refs_0_, bf16[64,4096]{1,0:T(8,128)(2,1)} %get-tuple-element.15.refs_1_, ...), custom_call_target="tpu_custom_call" | custom-call | flops 3623878656 | bytes 15728640 | tf_op jit(solution)/shard_map/pallas_call | solution.py:135
  154.5 3.3 %collective-permute-start.8 = (bf16[64,4096]{1,0:T(8,128)(2,1)}, bf16[64,4096]{1,0:T(8,128)(2,1)}, u32[]{:S(2)}, u32[]{:S(2)}) collective-permute-start(bf16[64,4096]{1,0:T(8,128)(2,1)} %get-tuple-element.17), channel_id=1, source_target_pairs={{0,192},{64,0},{128,64},{192,128},{1,193},{65,1},{129,65},{193,129... | collective-permute-start | bytes 1572872 | tf_op jit(solution)/shard_map/ppermute | solution.py:37
  157.8 6.6 %shard_map.124 = (bf16[64,4096]{1,0:T(8,128)(2,1)}, bf16[64,4096]{1,0:T(8,128)(2,1)}) custom-call(bf16[64,4096]{1,0:T(8,128)(2,1)} %collective-permute-done.9.refs_0_, bf16[64,4096]{1,0:T(8,128)(2,1)} %collective-permute-done.10.refs_1_, bf16[4096,384]{1,0:T(8,128)(2,1)} %bitcast.91, bf16[4096,384]{1,0:T(8,128)(2,1)} %bitcast.93, ...), custom_call_target="tpu_custom_call" | custom-call | flops 1207959552 | bytes 11534336 | tf_op jit(solution)/shard_map/pallas_call | solution.py:135
  164.7 3.3 %collective-permute-start.12 = (bf16[64,4096]{1,0:T(8,128)(2,1)}, bf16[64,4096]{1,0:T(8,128)(2,1)}, u32[]{:S(2)}, u32[]{:S(2)}) collective-permute-start(bf16[64,4096]{1,0:T(8,128)(2,1)} %get-tuple-element.21), channel_id=1, source_target_pairs={{0,192},{64,0},{128,64},{192,128},{1,193},{65,1},{129,65},{193,129... | collective-permute-start | bytes 1572872 | tf_op jit(solution)/shard_map/ppermute | solution.py:37
  168.0 5.3 %collective-permute-done.13.refs_5_.refs_4_ = bf16[64,4096]{1,0:T(8,128)(2,1)} collective-permute-done((bf16[64,4096]{1,0:T(8,128)(2,1)}, bf16[64,4096]{1,0:T(8,128)(2,1)}, u32[]{:S(2)}, u32[]{:S(2)}) %collective-permute-start.13) | collective-permute-done | bytes 524320 | tf_op jit(solution)/shard_map/ppermute | solution.py:37
  173.3 6.9 %collective-permute-done.11.refs_1_ = bf16[64,4096]{1,0:T(8,128)(2,1)} collective-permute-done((bf16[64,4096]{1,0:T(8,128)(2,1)}, bf16[64,4096]{1,0:T(8,128)(2,1)}, u32[]{:S(2)}, u32[]{:S(2)}) %collective-permute-start.11) | collective-permute-done | bytes 524320 | tf_op jit(solution)/shard_map/ppermute | solution.py:37
  182.7 3.2 %collective-permute-start.15 = (bf16[64,4096]{1,0:T(8,128)(2,1)}, bf16[64,4096]{1,0:T(8,128)(2,1)}, u32[]{:S(2)}, u32[]{:S(2)}) collective-permute-start(bf16[64,4096]{1,0:T(8,128)(2,1)} %get-tuple-element.25), channel_id=1, source_target_pairs={{0,192},{64,0},{128,64},{192,128},{1,193},{65,1},{129,65},{193,129... | collective-permute-start | bytes 1572872 | tf_op jit(solution)/shard_map/ppermute | solution.py:37
  187.0 6.9 %collective-permute-done.14.refs_2_ = bf16[64,4096]{1,0:T(8,128)(2,1)} collective-permute-done((bf16[64,4096]{1,0:T(8,128)(2,1)}, bf16[64,4096]{1,0:T(8,128)(2,1)}, u32[]{:S(2)}, u32[]{:S(2)}) %collective-permute-start.14) | collective-permute-done | bytes 524320 | tf_op jit(solution)/shard_map/ppermute | solution.py:37
  193.9 2.8 %shard_map.126 = bf16[128,4096]{1,0:T(8,128)(2,1)} custom-call(bf16[64,4096]{1,0:T(8,128)(2,1)} %get-tuple-element.16.refs_5_.refs_0_, bf16[64,4096]{1,0:T(8,128)(2,1)} %collective-permute-done.8.refs_4_.refs_1_, bf16[64,4096]{1,0:T(8,128)(2,1)} %collective-permute-done.14.refs_2_, bf16[64,4096]{1,0:T(8,128)(2,1)} %get-tuple-element.24.refs_3_, ...), custom_call_target="tpu_custom_call" | custom-call | flops 1572864 | bytes 4194304 | tf_op jit(solution)/shard_map/pallas_call | solution.py:186
  196.7 5.6 %all-to-all-start.5 = ((bf16[8,16,4096]{2,1,0:T(8,128)(2,1)}), bf16[8,16,4096]{2,1,0:T(8,128)(2,1)S(1)}, u32[]{:S(2)}, u32[]{:S(2)}) async-start(bf16[8,16,4096]{2,1,0:T(8,128)(2,1)} %bitcast.89), calls=%async_computation.5 | async-start | bytes 2097152 | tf_op jit(solution)/shard_map/all_to_all | solution.py:33
  203.0 13.9 %all-to-all-done.5 = bf16[8,16,4096]{2,1,0:T(8,128)(2,1)S(1)} async-done(((bf16[8,16,4096]{2,1,0:T(8,128)(2,1)}), bf16[8,16,4096]{2,1,0:T(8,128)(2,1)S(1)}, u32[]{:S(2)}, u32[]{:S(2)}) %all-to-all-start.5) | async-done | bytes 1048608 | tf_op jit(solution)/shard_map/all_to_all | solution.py:33
  217.5 20.1 %all_to_all.37 = bf16[8,8,4096]{2,1,0:T(8,128)(2,1)S(1)} all-to-all(bf16[8,8,4096]{2,1,0:T(8,128)(2,1)S(1)} %fusion.1), channel_id=1, replica_groups=mesh['y'=4,'z'=8,'x'=4,'core'=2] {'z'}, dimensions={0} | all-to-all | bytes 1048576 | tf_op jit(solution)/shard_map/all_to_all | solution.py:33
  (108 shorter events, 29.7 us)
Async XLA Ops:
  0.7 18.8 %copy-start.4 = (s32[8,8]{1,0:T(8,128)S(1)}, s32[8,8]{1,0:T(8,128)}, u32[]{:S(2)}) copy-start(s32[8,8]{1,0:T(8,128)} %param.20) | copy-start | bytes 772
  0.7 18.8 %copy-start.1 = (bf16[8,4096]{1,0:T(8,128)(2,1)S(1)}, bf16[8,4096]{1,0:T(8,128)(2,1)}, u32[]{:S(2)}) copy-start(bf16[8,4096]{1,0:T(8,128)(2,1)} %param.11) | copy-start | bytes 196612
  0.7 18.8 %copy-start.3 = (bf16[64,512]{1,0:T(8,128)(2,1)S(1)}, bf16[64,512]{1,0:T(8,128)(2,1)}, u32[]{:S(2)}) copy-start(bf16[64,512]{1,0:T(8,128)(2,1)} %param.12) | copy-start | bytes 196612
  3.0 28.4 %all-to-all-start = ((bf16[32,32,256]{2,1,0:T(8,128)(2,1)}), bf16[32,32,256]{2,1,0:T(8,128)(2,1)S(1)}, u32[]{:S(2)}, u32[]{:S(2)}) async-start(bf16[32,32,256]{2,1,0:T(8,128)(2,1)} %broadcast_in_dim.54), calls=%async_computation | async-start | bytes 1048576 | tf_op jit(solution)/shard_map/all_to_all | solution.py:27
  14.6 12.5 %collective-permute-start = (bf16[512,128]{1,0:T(8,128)(2,1)S(1)}, bf16[512,128]{1,0:T(8,128)(2,1)S(1)}, u32[]{:S(2)}, u32[]{:S(2)}) collective-permute-start(bf16[512,128]{1,0:T(8,128)(2,1)S(1)} %copy-done), channel_id=1, source_target_pairs={{0,192},{64,0},{128,64},{192,128},{1,193},{65,1},{129,65},{193,129... | collective-permute-start | bytes 393224 | tf_op jit(solution)/shard_map/ppermute | solution.py:37
  17.7 13.7 %collective-permute-start.1 = (bf16[512,128]{1,0:T(8,128)(2,1)S(1)}, bf16[512,128]{1,0:T(8,128)(2,1)S(1)}, u32[]{:S(2)}, u32[]{:S(2)}) collective-permute-start(bf16[512,128]{1,0:T(8,128)(2,1)S(1)} %copy-done), channel_id=1, source_target_pairs={{0,128},{64,192},{128,0},{192,64},{1,129},{65,193},{129,1},{193,65... | collective-permute-start | bytes 393224 | tf_op jit(solution)/shard_map/ppermute | solution.py:37
  18.5 12.9 %collective-permute-start.2 = (bf16[512,128]{1,0:T(8,128)(2,1)S(1)}, bf16[512,128]{1,0:T(8,128)(2,1)S(1)}, u32[]{:S(2)}, u32[]{:S(2)}) collective-permute-start(bf16[512,128]{1,0:T(8,128)(2,1)S(1)} %copy-done), channel_id=1, source_target_pairs={{0,64},{64,128},{128,192},{192,0},{1,65},{65,129},{129,193},{193,1... | collective-permute-start | bytes 393224 | tf_op jit(solution)/shard_map/ppermute | solution.py:37
  31.4 1.9 collective-permute-start.3
  36.5 25.0 %all-to-all-start.1 = ((bf16[8,80,512]{2,1,0:T(8,128)(2,1)}), bf16[8,80,512]{2,1,0:T(8,128)(2,1)S(1)}, u32[]{:S(2)}, u32[]{:S(2)}) async-start(bf16[8,80,512]{2,1,0:T(8,128)(2,1)} %pad_maximum_fusion), calls=%async_computation.1 | async-start | bytes 1310720 | tf_op jit(solution)/shard_map/all_to_all | solution.py:33
  63.6 13.7 %all-to-all-start.2 = ((bf16[8,8,8,512]{3,2,1,0:T(8,128)(2,1)}), bf16[8,8,8,512]{3,2,1,0:T(8,128)(2,1)S(1)}, u32[]{:S(2)}, u32[]{:S(2)}) async-start(bf16[8,8,8,512]{3,2,1,0:T(8,128)(2,1)} %copy.28), calls=%async_computation.2 | async-start | bytes 1048576 | tf_op jit(solution)/shard_map/all_to_all | solution.py:33
  114.8 15.2 %collective-permute-start.4 = (bf16[64,4096]{1,0:T(8,128)(2,1)}, bf16[64,4096]{1,0:T(8,128)(2,1)}, u32[]{:S(2)}, u32[]{:S(2)}) collective-permute-start(bf16[64,4096]{1,0:T(8,128)(2,1)} %get-tuple-element.14.refs_0_), channel_id=1, source_target_pairs={{0,192},{64,0},{128,64},{192,128},{1,193},{65,1},{129,65},{193,129... | collective-permute-start | bytes 1572872 | tf_op jit(solution)/shard_map/ppermute | solution.py:37
  116.5 16.4 %collective-permute-start.5 = (bf16[64,4096]{1,0:T(8,128)(2,1)}, bf16[64,4096]{1,0:T(8,128)(2,1)}, u32[]{:S(2)}, u32[]{:S(2)}) collective-permute-start(bf16[64,4096]{1,0:T(8,128)(2,1)} %get-tuple-element.15.refs_1_), channel_id=1, source_target_pairs={{0,64},{64,128},{128,192},{192,0},{1,65},{65,129},{129,193},{193,1... | collective-permute-start | bytes 1572872 | tf_op jit(solution)/shard_map/ppermute | solution.py:37
  116.8 27.9 %collective-permute-start.6 = (bf16[64,4096]{1,0:T(8,128)(2,1)}, bf16[64,4096]{1,0:T(8,128)(2,1)}, u32[]{:S(2)}, u32[]{:S(2)}) collective-permute-start(bf16[64,4096]{1,0:T(8,128)(2,1)} %get-tuple-element.14.refs_0_), channel_id=1, source_target_pairs={{0,64},{64,128},{128,192},{192,0},{1,65},{65,129},{129,193},{193,1... | collective-permute-start | bytes 1572872 | tf_op jit(solution)/shard_map/ppermute | solution.py:37
  117.4 27.3 %collective-permute-start.7 = (bf16[64,4096]{1,0:T(8,128)(2,1)}, bf16[64,4096]{1,0:T(8,128)(2,1)}, u32[]{:S(2)}, u32[]{:S(2)}) collective-permute-start(bf16[64,4096]{1,0:T(8,128)(2,1)} %get-tuple-element.15.refs_1_), channel_id=1, source_target_pairs={{0,192},{64,0},{128,64},{192,128},{1,193},{65,1},{129,65},{193,129... | collective-permute-start | bytes 1572872 | tf_op jit(solution)/shard_map/ppermute | solution.py:37
  129.9 27.9 %collective-permute-start.9 = (bf16[64,4096]{1,0:T(8,128)(2,1)}, bf16[64,4096]{1,0:T(8,128)(2,1)}, u32[]{:S(2)}, u32[]{:S(2)}) collective-permute-start(bf16[64,4096]{1,0:T(8,128)(2,1)} %collective-permute-done.4.refs_2_), channel_id=1, source_target_pairs={{0,192},{64,0},{128,64},{192,128},{1,193},{65,1},{129,65},{193,129... | collective-permute-start | bytes 1572872 | tf_op jit(solution)/shard_map/ppermute | solution.py:37
  132.9 24.9 %collective-permute-start.10 = (bf16[64,4096]{1,0:T(8,128)(2,1)}, bf16[64,4096]{1,0:T(8,128)(2,1)}, u32[]{:S(2)}, u32[]{:S(2)}) collective-permute-start(bf16[64,4096]{1,0:T(8,128)(2,1)} %collective-permute-done.5.refs_3_), channel_id=1, source_target_pairs={{0,64},{64,128},{128,192},{192,0},{1,65},{65,129},{129,193},{193,1... | collective-permute-start | bytes 1572872 | tf_op jit(solution)/shard_map/ppermute | solution.py:37
  154.5 13.5 %collective-permute-start.8 = (bf16[64,4096]{1,0:T(8,128)(2,1)}, bf16[64,4096]{1,0:T(8,128)(2,1)}, u32[]{:S(2)}, u32[]{:S(2)}) collective-permute-start(bf16[64,4096]{1,0:T(8,128)(2,1)} %get-tuple-element.17), channel_id=1, source_target_pairs={{0,192},{64,0},{128,64},{192,128},{1,193},{65,1},{129,65},{193,129... | collective-permute-start | bytes 1572872 | tf_op jit(solution)/shard_map/ppermute | solution.py:37
  157.8 15.5 %collective-permute-start.13 = (bf16[64,4096]{1,0:T(8,128)(2,1)}, bf16[64,4096]{1,0:T(8,128)(2,1)}, u32[]{:S(2)}, u32[]{:S(2)}) collective-permute-start(bf16[64,4096]{1,0:T(8,128)(2,1)} %get-tuple-element.22), channel_id=1, source_target_pairs={{0,64},{64,128},{128,192},{192,0},{1,65},{65,129},{129,193},{193,1... | collective-permute-start | bytes 1572872 | tf_op jit(solution)/shard_map/ppermute | solution.py:37
  164.4 15.9 %collective-permute-start.11 = (bf16[64,4096]{1,0:T(8,128)(2,1)}, bf16[64,4096]{1,0:T(8,128)(2,1)}, u32[]{:S(2)}, u32[]{:S(2)}) collective-permute-start(bf16[64,4096]{1,0:T(8,128)(2,1)} %get-tuple-element.19), channel_id=1, source_target_pairs={{0,64},{64,128},{128,192},{192,0},{1,65},{65,129},{129,193},{193,1... | collective-permute-start | bytes 1572872 | tf_op jit(solution)/shard_map/ppermute | solution.py:37
  164.7 15.6 %collective-permute-start.12 = (bf16[64,4096]{1,0:T(8,128)(2,1)}, bf16[64,4096]{1,0:T(8,128)(2,1)}, u32[]{:S(2)}, u32[]{:S(2)}) collective-permute-start(bf16[64,4096]{1,0:T(8,128)(2,1)} %get-tuple-element.21), channel_id=1, source_target_pairs={{0,192},{64,0},{128,64},{192,128},{1,193},{65,1},{129,65},{193,129... | collective-permute-start | bytes 1572872 | tf_op jit(solution)/shard_map/ppermute | solution.py:37
  182.7 11.2 %collective-permute-start.14 = (bf16[64,4096]{1,0:T(8,128)(2,1)}, bf16[64,4096]{1,0:T(8,128)(2,1)}, u32[]{:S(2)}, u32[]{:S(2)}) collective-permute-start(bf16[64,4096]{1,0:T(8,128)(2,1)} %get-tuple-element.23), channel_id=1, source_target_pairs={{0,64},{64,128},{128,192},{192,0},{1,65},{65,129},{129,193},{193,1... | collective-permute-start | bytes 1572872 | tf_op jit(solution)/shard_map/ppermute | solution.py:37
  182.7 11.2 %collective-permute-start.15 = (bf16[64,4096]{1,0:T(8,128)(2,1)}, bf16[64,4096]{1,0:T(8,128)(2,1)}, u32[]{:S(2)}, u32[]{:S(2)}) collective-permute-start(bf16[64,4096]{1,0:T(8,128)(2,1)} %get-tuple-element.25), channel_id=1, source_target_pairs={{0,192},{64,0},{128,64},{192,128},{1,193},{65,1},{129,65},{193,129... | collective-permute-start | bytes 1572872 | tf_op jit(solution)/shard_map/ppermute | solution.py:37
  196.7 20.1 %all-to-all-start.5 = ((bf16[8,16,4096]{2,1,0:T(8,128)(2,1)}), bf16[8,16,4096]{2,1,0:T(8,128)(2,1)S(1)}, u32[]{:S(2)}, u32[]{:S(2)}) async-start(bf16[8,16,4096]{2,1,0:T(8,128)(2,1)} %bitcast.89), calls=%async_computation.5 | async-start | bytes 2097152 | tf_op jit(solution)/shard_map/all_to_all | solution.py:33
  217.5 20.2 %copy-start.2 = (bf16[8,4,8,128]{3,0,2,1:T(8,128)(2,1)S(1)}, bf16[8,4,8,128]{3,0,2,1:T(8,128)(2,1)}, u32[]{:S(2)}) copy-start(bf16[8,4,8,128]{3,0,2,1:T(8,128)(2,1)} %copy.29) | copy-start | bytes 196612
  (2 other events, 32.6 us)

commit v6 on v5

--- a/solution.py
+++ b/solution.py
@@ -18,7 +18,7 @@
 CTX = ("y", "z")
 EXP = ("x", "core")
 LANES = X * CORE
-VMEM_LIMIT = 65024 * 1024
+VMEM_LIMIT = 20 * 1024 * 1024
 BF16 = jnp.bfloat16
 F32 = jnp.float32
 
@@ -75,15 +75,38 @@
 STEPS = 4
 
 
+def load_kernel(*refs):
+    sources, targets, sems = refs[:3], refs[-4:-1], refs[-1]
+    copies = [
+        pltpu.make_async_copy(source, target, sems.at[i])
+        for i, (source, target) in enumerate(zip(sources, targets))
+    ]
+    for copy in copies:
+        copy.start()
+    for copy in copies:
+        copy.wait()
+
+
+def load(arrays, after):
+    return pl.pallas_call(
+        load_kernel,
+        out_shape=[pltpu.VMEM(array.shape, array.dtype) for array in arrays],
+        in_specs=[pl.BlockSpec(memory_space=pl.ANY)] * (len(arrays) + len(after)),
+        out_specs=[pl.BlockSpec(memory_space=pltpu.VMEM)] * len(arrays),
+        scratch_shapes=[pltpu.SemaphoreType.DMA((len(arrays),))],
+        compiler_params=pltpu.CompilerParams(vmem_limit_bytes=16 * 1024 * 1024),
+    )(*arrays, *after)
+
+
 def expert_kernel(count, *refs):
-    blocks, (gate_ref, up_ref, down_ref) = refs[:count], refs[count : count + 3]
-    x, gate_w, up_w, down_w, out, in_sems, weight_sems, out_sems = refs[-8:]
-    outs = refs[-8 - count : -8]
+    blocks, (gate_w, up_w, down_w) = refs[:count], refs[count : count + 3]
+    x, out, in_sems, out_sems = refs[-4:]
+    outs = refs[-4 - count : -4]
     rows = blocks[0].shape[0]
     piece = D // STEPS
     parts = [slice(i * piece, (i + 1) * piece) for i in range(STEPS)]
     own_rows = [slice(j * rows, (j + 1) * rows) for j in range(count)]
-    row_copies, weight_copies, down_copies, out_copies = [], [], [], []
+    row_copies, out_copies = [], []
     for i, part in enumerate(parts):
         row_copies.append(
             [
@@ -91,35 +114,23 @@
                 for j, (block, own) in enumerate(zip(blocks, own_rows))
             ]
         )
-        weight_copies.append(
-            [
-                pltpu.make_async_copy(gate_ref.at[part], gate_w.at[part], weight_sems.at[0, i]),
-                pltpu.make_async_copy(up_ref.at[part], up_w.at[part], weight_sems.at[1, i]),
-            ]
-        )
-        down_copies.append(
-            pltpu.make_async_copy(down_ref.at[:, part], down_w.at[:, part], weight_sems.at[2, i])
-        )
         out_copies.append(
             [
                 pltpu.make_async_copy(out.at[own, part], out_ref.at[:, part], out_sems.at[i, j])
                 for j, (out_ref, own) in enumerate(zip(outs, own_rows))
             ]
         )
-    for i in range(STEPS):
-        for copy in row_copies[i] + weight_copies[i]:
+    for copies in row_copies:
+        for copy in copies:
             copy.start()
-    for copy in down_copies:
-        copy.start()
     gate_h, up_h = 0.0, 0.0
     for i, part in enumerate(parts):
-        for copy in row_copies[i] + weight_copies[i]:
+        for copy in row_copies[i]:
             copy.wait()
         gate_h = gate_h + jnp.dot(x[:, part], gate_w[part], preferred_element_type=F32)
         up_h = up_h + jnp.dot(x[:, part], up_w[part], preferred_element_type=F32)
     inner = (gate_h / (1.0 + jnp.exp(-gate_h)) * up_h).astype(BF16)
     for i, part in enumerate(parts):
-        down_copies[i].wait()
         out[:, part] = jnp.dot(inner, down_w[:, part], preferred_element_type=F32).astype(BF16)
         for copy in out_copies[i]:
             copy.start()
@@ -135,16 +146,14 @@
     return pl.pallas_call(
         functools.partial(expert_kernel, count),
         out_shape=[jax.ShapeDtypeStruct((rows, D), BF16)] * count,
-        in_specs=[pl.BlockSpec(memory_space=pl.ANY)] * (count + 3 + len(after)),
+        in_specs=[pl.BlockSpec(memory_space=pl.ANY)] * count
+        + [pl.BlockSpec(memory_space=pltpu.VMEM)] * 3
+        + [pl.BlockSpec(memory_space=pl.ANY)] * len(after),
         out_specs=[pl.BlockSpec(memory_space=pl.ANY)] * count,
         scratch_shapes=[
             pltpu.VMEM((count * rows, D), BF16),
-            pltpu.VMEM((D, width), BF16),
-            pltpu.VMEM((D, width), BF16),
-            pltpu.VMEM((width, D), BF16),
             pltpu.VMEM((count * rows, D), BF16),
             pltpu.SemaphoreType.DMA((STEPS, count)),
-            pltpu.SemaphoreType.DMA((3, STEPS)),
             pltpu.SemaphoreType.DMA((STEPS, count)),
         ],
         compiler_params=pltpu.CompilerParams(vmem_limit_bytes=VMEM_LIMIT),
@@ -156,48 +165,43 @@
     )(*blocks, *weights, *after)
 
 
-def add_kernel(count, *refs):
-    out_ref = refs[-1]
-    rows = refs[0].shape[0]
-    for i in range(2):
-        total = refs[i * count][...].astype(F32)
-        for ref in refs[i * count + 1 : (i + 1) * count]:
-            total = total + ref[...].astype(F32)
-        out_ref[i * rows : (i + 1) * rows] = total.astype(BF16)
-
-
-def pair_kernel(count, *refs):
+def hand_on_kernel(*refs):
+    pass
+
+
+def hand_on(blocks, after):
+    count = len(blocks)
+    return pl.pallas_call(
+        hand_on_kernel,
+        out_shape=[jax.ShapeDtypeStruct(block.shape, block.dtype) for block in blocks],
+        in_specs=[pl.BlockSpec(memory_space=pl.ANY)] * (count + len(after)),
+        out_specs=[pl.BlockSpec(memory_space=pl.ANY)] * count,
+        input_output_aliases={i: i for i in range(count)},
+    )(*blocks, *after)
+
+
+def pair_kernel(*refs):
     for i, out_ref in enumerate(refs[-2:]):
-        total = refs[i * count][...].astype(F32)
-        for ref in refs[i * count + 1 : (i + 1) * count]:
-            total = total + ref[...].astype(F32)
-        out_ref[...] = total.astype(BF16)
-
-
-def add_up(terms, after, joined):
-    rows = terms[0][0].shape[0]
-    count = len(terms[0])
+        out_ref[...] = (refs[2 * i][...].astype(F32) + refs[2 * i + 1][...].astype(F32)).astype(BF16)
+
+
+def add_pairs(low, high, after):
+    rows = low[0].shape[0]
     piece = D // 2
     block = pl.BlockSpec((rows, piece), lambda i: (0, i))
-    if joined:
-        kernel, blocks, results = add_kernel, pl.BlockSpec((2 * rows, piece), lambda i: (0, i)), 1
-    else:
-        kernel, blocks, results = pair_kernel, block, 2
-    return pl.pallas_call(
-        functools.partial(kernel, count),
+    return pl.pallas_call(
+        pair_kernel,
         grid=(D // piece,),
-        out_shape=[jax.ShapeDtypeStruct((2 * rows // results, D), BF16)] * results,
-        in_specs=[block] * (2 * count) + [pl.BlockSpec(memory_space=pl.ANY) for _ in after],
-        out_specs=[blocks] * results,
+        out_shape=[jax.ShapeDtypeStruct((rows, D), BF16)] * 2,
+        in_specs=[block] * 4 + [pl.BlockSpec(memory_space=pl.ANY) for _ in after],
+        out_specs=[block] * 2,
         compiler_params=pltpu.CompilerParams(
-            dimension_semantics=("arbitrary",), vmem_limit_bytes=VMEM_LIMIT
+            dimension_semantics=("arbitrary",), vmem_limit_bytes=16 * 1024 * 1024
         ),
         cost_estimate=pl.CostEstimate(
-            flops=2 * count * rows * D,
-            bytes_accessed=4 * (count + 1) * rows * D,
-            transcendentals=0,
+            flops=2 * rows * D, bytes_accessed=12 * rows * D, transcendentals=0
         ),
-    )(*terms[0], *terms[1], *after)
+    )(*low, *high, *after)
 
 
 def slots_of(routes):
@@ -301,39 +305,14 @@
     before_high = shift(high, 1)
     before_low = shift(low, 1)
     after_high = shift(high, -1)
+
+    projected = swap(projected_c.astype(BF16), "z").reshape(Z, rows, Y, HEAD_SIZE)
+    projected = projected.transpose(1, 2, 0, 3).reshape(rows, D)
+
+    after_low, before_high = hand_on((after_low, before_high), (projected,))
     across_low = shift(after_low, -1)
     across_high = shift(before_high, 1)
 
-    projected = swap(projected_c.astype(BF16), "z").reshape(Z, rows, Y, HEAD_SIZE)
-    projected = projected.transpose(1, 2, 0, 3).reshape(rows, D)
-
-    weights = (w_gate[0], w_up[0], w_down[0])
-    (
-        own_low,
-        own_high,
-        out_after_low,
-        out_before_high,
-        out_before_low,
-        out_after_high,
-    ) = expert(
-        (low, high, after_low, before_high, before_low, after_high), weights, after=(projected,)
-    )
-    out_across_low, out_across_high = expert(
-        (across_low, across_high), weights, after=(own_low,)
-    )
-    home_low = shift(out_before_low, -1)
-    home_high = shift(out_after_high, 1)
-    far_low = shift(out_across_low, 1)
-    far_high = shift(out_across_high, -1)
-    sum_low, sum_high = add_up(
-        ((out_after_low, far_low), (out_before_high, far_high)), (home_low, home_high), False
-    )
-    sum_low, sum_high = shift(sum_low, 1), shift(sum_high, -1)
-    (returned,) = add_up(
-        ((own_low, home_low, sum_low), (own_high, home_high, sum_high)), (), True
-    )
-
-    back = swap(returned.reshape(LANES, Z * MOST, D), EXP).reshape(slots, D)
     gate = jnp.sum(jnp.where(named, gates_c[..., None], 0.0), axis=2)
     place = jnp.where(chosen, gate[..., None], 0.0).reshape(Z, rows, Z, LANES, MOST)
     place = lax.dynamic_index_in_dim(place, lax.axis_index("z"), 2, keepdims=False)
@@ -341,6 +320,30 @@
     place = place.reshape(Z * rows, slots)
     place_high = place.astype(BF16)
     place_low = (place - place_high.astype(F32)).astype(BF16)
+
+    weights = load((w_gate[0], w_up[0], w_down[0]), (place_high, place_low))
+    own_low, own_high, out_after_low, out_before_high = expert(
+        (low, high, after_low, before_high), weights
+    )
+    out_before_low, out_after_high = expert(
+        (before_low, after_high), weights, after=(own_low,)
+    )
+    out_across_low, out_across_high = expert(
+        (across_low, across_high), weights, after=(out_before_low,)
+    )
+    home_low = shift(out_before_low, -1)
+    home_high = shift(out_after_high, 1)
+    far_low = shift(out_across_low, 1)
+    far_high = shift(out_across_high, -1)
+    sum_low, sum_high = add_pairs(
+        (out_after_low, far_low), (out_before_high, far_high), (home_low, home_high)
+    )
+    sum_low, sum_high = shift(sum_low, 1), shift(sum_high, -1)
+    home_low = own_low.astype(F32) + home_low.astype(F32) + sum_low.astype(F32)
+    home_high = own_high.astype(F32) + home_high.astype(F32) + sum_high.astype(F32)
+    returned = jnp.concatenate([home_low.astype(BF16), home_high.astype(BF16)], axis=0)
+
+    back = swap(returned.reshape(LANES, Z * MOST, D), EXP).reshape(slots, D)
     moe_z = jnp.dot(place_high, back, preferred_element_type=F32) + jnp.dot(
         place_low, back, preferred_element_type=F32
     )

time: 240 us -> 234 us (0.975)
  blocking collectives: 65.5 us -> 21.9 us
  waiting for transfers between devices: 82.1 us -> 105 us
  local copies, waits for them, and re-layouts: 7.94 us -> 16.1 us
  starting transfers between devices: 49.5 us -> 57.5 us
  Pallas kernels: 24.3 us -> 16.6 us
  other arithmetic: 4.61 us -> 9.85 us
    all_to_all x3 -> x1, blocking collectives: 65.5 us -> 21.9 us  [swap(): return lax.all_to_all(blocks, axes, 0, 0, tiled=True)]
    all_to_all x3 -> x5, waiting for transfers between devices: 39.8 us -> 70 us  [swap(): return lax.all_to_all(blocks, axes, 0, 0, tiled=True)]
    all_to_all x3 -> x5, starting transfers between devices: 14.8 us -> 24.2 us  [swap(): return lax.all_to_all(blocks, axes, 0, 0, tiled=True)]
    ppermute x15, waiting for transfers between devices: 36.5 us -> 29.2 us  [shift(): return lax.ppermute(block, 'y', [(i, (i + step) % Y) for i in range(Y)])]
    pallas_call x2 -> x3, Pallas kernels: 5.3 us -> 1.17 us  [the longest x1 0.66 us: load(): pl.pallas_call(load_kernel, out_shape=[pltpu.VMEM(array.shape, array.dtyp...]
    unnamed x19 -> x21, local copies, waits for them, and re-layouts: 0.15 us -> 3.92 us
    pallas_call x2 -> x3, Pallas kernels: 16.4 us -> 14 us  [expert(): pl.pallas_call(functools.partial(expert_kernel, count), out_shape=[jax.Sh...]
  transfers between devices with their start and end apart: 20 -> 22, of which waited for: 10 -> 13; matrix products, arithmetic and copies ran while one was open for 3% -> 6% of each run, Pallas kernels for 7% -> 6%
where the time goes in v6:
time: 234 us; the launch traced here: 232 us
  waiting for transfers between devices  105 us (45%)
  starting transfers between devices  57.5 us (25%)
  blocking collectives  21.9 us (9%)
  Pallas kernels  16.6 us (7%)
  local copies, waits for them, and re-layouts  16.1 us (7%)
  other arithmetic  9.85 us (4%)
  matrix products  4.33 us (2%)
    all_to_all x5, waiting for transfers between devices, swap(): return lax.all_to_all(blocks, axes, 0, 0, tiled=True)  70 us
    ppermute x15, waiting for transfers between devices, shift(): return lax.ppermute(block, 'y', [(i, (i + step) % Y) for i in range(Y)])  29.2 us
    all_to_all x5, starting transfers between devices, swap(): return lax.all_to_all(blocks, axes, 0, 0, tiled=True)  24.2 us
    all_to_all x1, blocking collectives, swap(): return lax.all_to_all(blocks, axes, 0, 0, tiled=True)  21.9 us
    ppermute x15, starting transfers between devices, shift(): return lax.ppermute(block, 'y', [(i, (i + step) % Y) for i in range(Y)])  21.8 us
    pallas_call x3, Pallas kernels, expert(): pl.pallas_call(functools.partial(expert_kernel, count), out_shape=[jax.Sh...  14 us
    all_to_all x1, starting transfers between devices, spread(): lax.all_to_all(jnp.broadcast_to(block[None], (count,) + block.shape), axe...  11.5 us
  transfers between devices with their start and end apart: 22, of which 13 were waited for; matrix products, arithmetic and copies ran while one was open for 6% of the time, Pallas kernels for 6%

profile of v6, /device:TPU:2, one launch (start us, length us, event | category | flops | bytes accessed | tf_op | source)
XLA Modules:
  0.0 232.2 jit_solution(11065671990748785421)
XLA Ops:
  2.9 11.5 %all-to-all-start = ((bf16[32,32,256]{2,1,0:T(8,128)(2,1)}), bf16[32,32,256]{2,1,0:T(8,128)(2,1)S(1)}, u32[]{:S(2)}, u32[]{:S(2)}) async-start(bf16[32,32,256]{2,1,0:T(8,128)(2,1)} %broadcast_in_dim.54), calls=%async_computation | async-start | bytes 1048576 | tf_op jit(solution)/shard_map/all_to_all | solution.py:27
  14.4 3.1 %collective-permute-start = (bf16[512,128]{1,0:T(8,128)(2,1)}, bf16[512,128]{1,0:T(8,128)(2,1)S(1)}, u32[]{:S(2)}, u32[]{:S(2)}) collective-permute-start(bf16[512,128]{1,0:T(8,128)(2,1)} %param.15), channel_id=1, source_target_pairs={{0,192},{64,0},{128,64},{192,128},{1,193},{65,1},{129,65},{193,129... | collective-permute-start | bytes 393224 | tf_op jit(solution)/shard_map/ppermute | solution.py:37
  22.6 4.5 %collective-permute-done = bf16[512,128]{1,0:T(8,128)(2,1)S(1)} collective-permute-done((bf16[512,128]{1,0:T(8,128)(2,1)}, bf16[512,128]{1,0:T(8,128)(2,1)S(1)}, u32[]{:S(2)}, u32[]{:S(2)}) %collective-permute-start) | collective-permute-done | bytes 131104 | tf_op jit(solution)/shard_map/ppermute | solution.py:37
  27.1 4.1 %all-to-all-done = bf16[32,32,256]{2,1,0:T(8,128)(2,1)S(1)} async-done(((bf16[32,32,256]{2,1,0:T(8,128)(2,1)}), bf16[32,32,256]{2,1,0:T(8,128)(2,1)S(1)}, u32[]{:S(2)}, u32[]{:S(2)}) %all-to-all-start) | async-done | bytes 524320 | tf_op jit(solution)/shard_map/all_to_all | solution.py:27
  36.5 4.4 %all-to-all-start.1 = ((bf16[8,80,512]{2,1,0:T(8,128)(2,1)}), bf16[8,80,512]{2,1,0:T(8,128)(2,1)S(1)}, u32[]{:S(2)}, u32[]{:S(2)}) async-start(bf16[8,80,512]{2,1,0:T(8,128)(2,1)} %pad_maximum_fusion.1), calls=%async_computation.1 | async-start | bytes 1310720 | tf_op jit(solution)/shard_map/all_to_all | solution.py:33
  41.7 19.8 %all-to-all-done.1 = bf16[8,80,512]{2,1,0:T(8,128)(2,1)S(1)} async-done(((bf16[8,80,512]{2,1,0:T(8,128)(2,1)}), bf16[8,80,512]{2,1,0:T(8,128)(2,1)S(1)}, u32[]{:S(2)}, u32[]{:S(2)}) %all-to-all-start.1) | async-done | bytes 655392 | tf_op jit(solution)/shard_map/all_to_all | solution.py:33
  63.6 4.8 %all-to-all-start.2 = ((bf16[8,8,8,512]{3,2,1,0:T(8,128)(2,1)}), bf16[8,8,8,512]{3,2,1,0:T(8,128)(2,1)S(1)}, u32[]{:S(2)}, u32[]{:S(2)}) async-start(bf16[8,8,8,512]{3,2,1,0:T(8,128)(2,1)} %copy.34), calls=%async_computation.2 | async-start | bytes 1048576 | tf_op jit(solution)/shard_map/all_to_all | solution.py:33
  71.2 6.1 %all-to-all-done.2 = bf16[8,8,8,512]{3,2,1,0:T(8,128)(2,1)S(1)} async-done(((bf16[8,8,8,512]{3,2,1,0:T(8,128)(2,1)}), bf16[8,8,8,512]{3,2,1,0:T(8,128)(2,1)S(1)}, u32[]{:S(2)}, u32[]{:S(2)}) %all-to-all-start.2) | async-done | bytes 524320 | tf_op jit(solution)/shard_map/all_to_all | solution.py:33
  78.8 5.7 %all-to-all-start.4 = ((bf16[64,16,512]{2,1,0:T(8,128)(2,1)}), bf16[64,16,512]{2,1,0:T(8,128)(2,1)S(1)}, u32[]{:S(2)}, u32[]{:S(2)}) async-start(bf16[64,16,512]{2,1,0:T(8,128)(2,1)} %bitcast.26), calls=%async_computation.4 | async-start | bytes 2097152 | tf_op jit(solution)/shard_map/all_to_all | solution.py:33
  85.6 27.8 %all-to-all-done.4.x_ref = bf16[64,16,512]{2,1,0:T(8,128)(2,1)S(1)} async-done(((bf16[64,16,512]{2,1,0:T(8,128)(2,1)}), bf16[64,16,512]{2,1,0:T(8,128)(2,1)S(1)}, u32[]{:S(2)}, u32[]{:S(2)}) %all-to-all-start.4) | async-done | bytes 1048608 | tf_op jit(solution)/shard_map/all_to_all | solution.py:33
  117.5 4.0 %all-to-all-start.3 = ((bf16[8,8,512]{2,1,0:T(8,128)(2,1)}), bf16[8,8,512]{2,1,0:T(8,128)(2,1)}, u32[]{:S(2)}, u32[]{:S(2)}) async-start(bf16[8,8,512]{2,1,0:T(8,128)(2,1)} %convert_element_type.171), calls=%async_computation.3 | async-start | bytes 131072 | tf_op jit(solution)/shard_map/all_to_all | solution.py:33
  140.4 6.3 %shard_map.125 = (bf16[64,4096]{1,0:T(8,128)(2,1)S(1)}, bf16[64,4096]{1,0:T(8,128)(2,1)S(1)}, bf16[64,4096]{1,0:T(8,128)(2,1)S(1)}, bf16[64,4096]{1,0:T(8,128)(2,1)S(1)}) custom-call(bf16[64,4096]{1,0:T(8,128)(2,1)} %get-tuple-element.19.refs_0_, bf16[64,4096]{1,0:T(8,128)(2,1)} %get-tuple-element.20.refs_1_, bf16[64,4096]{1,0:T(8,128)(2,1)} %get-tuple-element.21.refs_2_, ...), custom_call_target="tpu_custom_call" | custom-call | flops 2415919104 | bytes 13631488 | tf_op jit(solution)/shard_map/pallas_call | solution.py:146
  146.8 4.2 %shard_map.126 = (bf16[64,4096]{1,0:T(8,128)(2,1)S(1)}, bf16[64,4096]{1,0:T(8,128)(2,1)S(1)}) custom-call(bf16[64,4096]{1,0:T(8,128)(2,1)} %collective-permute-done.6.refs_0_, bf16[64,4096]{1,0:T(8,128)(2,1)} %collective-permute-done.7.refs_1_, bf16[4096,384]{1,0:T(8,128)(2,1)S(1)} %get-tuple-element.23.refs_4_.refs_2_, ...), custom_call_target="tpu_custom_call" | custom-call | flops 1207959552 | bytes 11534336 | tf_op jit(solution)/shard_map/pallas_call | solution.py:146
  151.0 2.7 %collective-permute-start.8 = (bf16[64,4096]{1,0:T(8,128)(2,1)S(1)}, bf16[64,4096]{1,0:T(8,128)(2,1)S(1)}, u32[]{:S(2)}, u32[]{:S(2)}) collective-permute-start(bf16[64,4096]{1,0:T(8,128)(2,1)S(1)} %get-tuple-element.27.refs_5_), channel_id=1, source_target_pairs={{0,192},{64,0},{128,64},{192,128},{1,193},{65,1},{129,65},{193,129... | collective-permute-start | bytes 1572872 | tf_op jit(solution)/shard_map/ppermute | solution.py:37
  153.7 3.5 %shard_map.127 = (bf16[64,4096]{1,0:T(8,128)(2,1)S(1)}, bf16[64,4096]{1,0:T(8,128)(2,1)S(1)}) custom-call(bf16[64,4096]{1,0:T(8,128)(2,1)S(1)} %collective-permute-done.9.refs_0_, bf16[64,4096]{1,0:T(8,128)(2,1)S(1)} %collective-permute-done.10.refs_1_, bf16[4096,384]{1,0:T(8,128)(2,1)S(1)} %get-tuple-element.23.refs_4_.refs_2_, ...), custom_call_target="tpu_custom_call" | custom-call | flops 1207959552 | bytes 11534336 | tf_op jit(solution)/shard_map/pallas_call | solution.py:146
  157.3 3.5 %collective-permute-start.12 = (bf16[64,4096]{1,0:T(8,128)(2,1)S(1)}, bf16[64,4096]{1,0:T(8,128)(2,1)S(1)}, u32[]{:S(2)}, u32[]{:S(2)}) collective-permute-start(bf16[64,4096]{1,0:T(8,128)(2,1)S(1)} %get-tuple-element.31), channel_id=1, source_target_pairs={{0,192},{64,0},{128,64},{192,128},{1,193},{65,1},{129,65},{193,129... | collective-permute-start | bytes 1572872 | tf_op jit(solution)/shard_map/ppermute | solution.py:37
  160.8 5.3 %collective-permute-done.8.refs_4_ = bf16[64,4096]{1,0:T(8,128)(2,1)S(1)} collective-permute-done((bf16[64,4096]{1,0:T(8,128)(2,1)S(1)}, bf16[64,4096]{1,0:T(8,128)(2,1)S(1)}, u32[]{:S(2)}, u32[]{:S(2)}) %collective-permute-start.8) | collective-permute-done | bytes 524320 | tf_op jit(solution)/shard_map/ppermute | solution.py:37
  166.1 3.7 %collective-permute-done.13.refs_5_ = bf16[64,4096]{1,0:T(8,128)(2,1)S(1)} collective-permute-done((bf16[64,4096]{1,0:T(8,128)(2,1)S(1)}, bf16[64,4096]{1,0:T(8,128)(2,1)S(1)}, u32[]{:S(2)}, u32[]{:S(2)}) %collective-permute-start.13) | collective-permute-done | bytes 524320 | tf_op jit(solution)/shard_map/ppermute | solution.py:37
  169.8 6.7 %collective-permute-done.11.refs_1_ = bf16[64,4096]{1,0:T(8,128)(2,1)S(1)} collective-permute-done((bf16[64,4096]{1,0:T(8,128)(2,1)S(1)}, bf16[64,4096]{1,0:T(8,128)(2,1)S(1)}, u32[]{:S(2)}, u32[]{:S(2)}) %collective-permute-start.11) | collective-permute-done | bytes 524320 | tf_op jit(solution)/shard_map/ppermute | solution.py:37
  177.0 3.2 %collective-permute-start.15 = (bf16[64,4096]{1,0:T(8,128)(2,1)S(1)}, bf16[64,4096]{1,0:T(8,128)(2,1)S(1)}, u32[]{:S(2)}, u32[]{:S(2)}) collective-permute-start(bf16[64,4096]{1,0:T(8,128)(2,1)S(1)} %get-tuple-element.35), channel_id=1, source_target_pairs={{0,192},{64,0},{128,64},{192,128},{1,193},{65,1},{129,65},{193,129... | collective-permute-start | bytes 1572872 | tf_op jit(solution)/shard_map/ppermute | solution.py:37
  180.3 7.2 %collective-permute-done.14 = bf16[64,4096]{1,0:T(8,128)(2,1)S(1)} collective-permute-done((bf16[64,4096]{1,0:T(8,128)(2,1)S(1)}, bf16[64,4096]{1,0:T(8,128)(2,1)S(1)}, u32[]{:S(2)}, u32[]{:S(2)}) %collective-permute-start.14) | collective-permute-done | bytes 524320 | tf_op jit(solution)/shard_map/ppermute | solution.py:37
  189.0 5.3 %all-to-all-start.5 = ((bf16[8,16,4096]{2,1,0:T(8,128)(2,1)}), bf16[8,16,4096]{2,1,0:T(8,128)(2,1)S(1)}, u32[]{:S(2)}, u32[]{:S(2)}) async-start(bf16[8,16,4096]{2,1,0:T(8,128)(2,1)} %bitcast.31), calls=%async_computation.5 | async-start | bytes 2097152 | tf_op jit(solution)/shard_map/all_to_all | solution.py:33
  194.7 14.0 %all-to-all-done.5 = bf16[8,16,4096]{2,1,0:T(8,128)(2,1)S(1)} async-done(((bf16[8,16,4096]{2,1,0:T(8,128)(2,1)}), bf16[8,16,4096]{2,1,0:T(8,128)(2,1)S(1)}, u32[]{:S(2)}, u32[]{:S(2)}) %all-to-all-start.5) | async-done | bytes 1048608 | tf_op jit(solution)/shard_map/all_to_all | solution.py:33
  209.5 21.9 %all_to_all.35 = bf16[8,8,4096]{2,1,0:T(8,128)(2,1)S(1)} all-to-all(bf16[8,8,4096]{2,1,0:T(8,128)(2,1)S(1)} %fusion.1), channel_id=1, replica_groups=mesh['y'=4,'z'=8,'x'=4,'core'=2] {'z'}, dimensions={0} | all-to-all | bytes 1048576 | tf_op jit(solution)/shard_map/all_to_all | solution.py:33
  (120 shorter events, 47.6 us)
Async XLA Ops:
  2.9 28.4 %all-to-all-start = ((bf16[32,32,256]{2,1,0:T(8,128)(2,1)}), bf16[32,32,256]{2,1,0:T(8,128)(2,1)S(1)}, u32[]{:S(2)}, u32[]{:S(2)}) async-start(bf16[32,32,256]{2,1,0:T(8,128)(2,1)} %broadcast_in_dim.54), calls=%async_computation | async-start | bytes 1048576 | tf_op jit(solution)/shard_map/all_to_all | solution.py:27
  14.4 12.7 %collective-permute-start = (bf16[512,128]{1,0:T(8,128)(2,1)}, bf16[512,128]{1,0:T(8,128)(2,1)S(1)}, u32[]{:S(2)}, u32[]{:S(2)}) collective-permute-start(bf16[512,128]{1,0:T(8,128)(2,1)} %param.15), channel_id=1, source_target_pairs={{0,192},{64,0},{128,64},{192,128},{1,193},{65,1},{129,65},{193,129... | collective-permute-start | bytes 393224 | tf_op jit(solution)/shard_map/ppermute | solution.py:37
  17.6 13.7 %collective-permute-start.1 = (bf16[512,128]{1,0:T(8,128)(2,1)}, bf16[512,128]{1,0:T(8,128)(2,1)S(1)}, u32[]{:S(2)}, u32[]{:S(2)}) collective-permute-start(bf16[512,128]{1,0:T(8,128)(2,1)} %param.15), channel_id=1, source_target_pairs={{0,128},{64,192},{128,0},{192,64},{1,129},{65,193},{129,1},{193,65... | collective-permute-start | bytes 393224 | tf_op jit(solution)/shard_map/ppermute | solution.py:37
  18.4 13.0 %collective-permute-start.2 = (bf16[512,128]{1,0:T(8,128)(2,1)}, bf16[512,128]{1,0:T(8,128)(2,1)S(1)}, u32[]{:S(2)}, u32[]{:S(2)}) collective-permute-start(bf16[512,128]{1,0:T(8,128)(2,1)} %param.15), channel_id=1, source_target_pairs={{0,64},{64,128},{128,192},{192,0},{1,65},{65,129},{129,193},{193,1... | collective-permute-start | bytes 393224 | tf_op jit(solution)/shard_map/ppermute | solution.py:37
  31.3 1.9 collective-permute-start.3
  36.5 25.0 %all-to-all-start.1 = ((bf16[8,80,512]{2,1,0:T(8,128)(2,1)}), bf16[8,80,512]{2,1,0:T(8,128)(2,1)S(1)}, u32[]{:S(2)}, u32[]{:S(2)}) async-start(bf16[8,80,512]{2,1,0:T(8,128)(2,1)} %pad_maximum_fusion.1), calls=%async_computation.1 | async-start | bytes 1310720 | tf_op jit(solution)/shard_map/all_to_all | solution.py:33
  63.6 13.7 %all-to-all-start.2 = ((bf16[8,8,8,512]{3,2,1,0:T(8,128)(2,1)}), bf16[8,8,8,512]{3,2,1,0:T(8,128)(2,1)S(1)}, u32[]{:S(2)}, u32[]{:S(2)}) async-start(bf16[8,8,8,512]{3,2,1,0:T(8,128)(2,1)} %copy.34), calls=%async_computation.2 | async-start | bytes 1048576 | tf_op jit(solution)/shard_map/all_to_all | solution.py:33
  78.8 34.6 %copy-start.3 = (f32[4096]{0:T(1024)S(1)}, f32[4096]{0:T(1024)}, u32[]{:S(2)}) copy-start(f32[4096]{0:T(1024)} %param.16) | copy-start | bytes 49156
  78.8 34.6 %all-to-all-start.4 = ((bf16[64,16,512]{2,1,0:T(8,128)(2,1)}), bf16[64,16,512]{2,1,0:T(8,128)(2,1)S(1)}, u32[]{:S(2)}, u32[]{:S(2)}) async-start(bf16[64,16,512]{2,1,0:T(8,128)(2,1)} %bitcast.26), calls=%async_computation.4 | async-start | bytes 2097152 | tf_op jit(solution)/shard_map/all_to_all | solution.py:33
  114.8 16.5 %collective-permute-start.4 = (bf16[64,4096]{1,0:T(8,128)(2,1)}, bf16[64,4096]{1,0:T(8,128)(2,1)}, u32[]{:S(2)}, u32[]{:S(2)}) collective-permute-start(bf16[64,4096]{1,0:T(8,128)(2,1)} %get-tuple-element.19.refs_0_), channel_id=1, source_target_pairs={{0,192},{64,0},{128,64},{192,128},{1,193},{65,1},{129,65},{193,129... | collective-permute-start | bytes 1572872 | tf_op jit(solution)/shard_map/ppermute | solution.py:37
  116.7 16.4 %collective-permute-start.5 = (bf16[64,4096]{1,0:T(8,128)(2,1)}, bf16[64,4096]{1,0:T(8,128)(2,1)}, u32[]{:S(2)}, u32[]{:S(2)}) collective-permute-start(bf16[64,4096]{1,0:T(8,128)(2,1)} %get-tuple-element.20.refs_1_), channel_id=1, source_target_pairs={{0,64},{64,128},{128,192},{192,0},{1,65},{65,129},{129,193},{193,1... | collective-permute-start | bytes 1572872 | tf_op jit(solution)/shard_map/ppermute | solution.py:37
  117.5 12.4 %all-to-all-start.3 = ((bf16[8,8,512]{2,1,0:T(8,128)(2,1)}), bf16[8,8,512]{2,1,0:T(8,128)(2,1)}, u32[]{:S(2)}, u32[]{:S(2)}) async-start(bf16[8,8,512]{2,1,0:T(8,128)(2,1)} %convert_element_type.171), calls=%async_computation.3 | async-start | bytes 131072 | tf_op jit(solution)/shard_map/all_to_all | solution.py:33
  121.5 25.3 %collective-permute-start.6 = (bf16[64,4096]{1,0:T(8,128)(2,1)}, bf16[64,4096]{1,0:T(8,128)(2,1)}, u32[]{:S(2)}, u32[]{:S(2)}) collective-permute-start(bf16[64,4096]{1,0:T(8,128)(2,1)} %get-tuple-element.19.refs_0_), channel_id=1, source_target_pairs={{0,64},{64,128},{128,192},{192,0},{1,65},{65,129},{129,193},{193,1... | collective-permute-start | bytes 1572872 | tf_op jit(solution)/shard_map/ppermute | solution.py:37
  122.1 24.6 %collective-permute-start.7 = (bf16[64,4096]{1,0:T(8,128)(2,1)}, bf16[64,4096]{1,0:T(8,128)(2,1)}, u32[]{:S(2)}, u32[]{:S(2)}) collective-permute-start(bf16[64,4096]{1,0:T(8,128)(2,1)} %get-tuple-element.20.refs_1_), channel_id=1, source_target_pairs={{0,192},{64,0},{128,64},{192,128},{1,193},{65,1},{129,65},{193,129... | collective-permute-start | bytes 1572872 | tf_op jit(solution)/shard_map/ppermute | solution.py:37
  133.1 20.6 %collective-permute-start.9 = (bf16[64,4096]{1,0:T(8,128)(2,1)}, bf16[64,4096]{1,0:T(8,128)(2,1)S(1)}, u32[]{:S(2)}, u32[]{:S(2)}) collective-permute-start(bf16[64,4096]{1,0:T(8,128)(2,1)} %get-tuple-element.21.refs_2_), channel_id=1, source_target_pairs={{0,192},{64,0},{128,64},{192,128},{1,193},{65,1},{129,65},{193,129... | collective-permute-start | bytes 1572872 | tf_op jit(solution)/shard_map/ppermute | solution.py:37
  134.5 19.2 %collective-permute-start.10 = (bf16[64,4096]{1,0:T(8,128)(2,1)}, bf16[64,4096]{1,0:T(8,128)(2,1)S(1)}, u32[]{:S(2)}, u32[]{:S(2)}) collective-permute-start(bf16[64,4096]{1,0:T(8,128)(2,1)} %get-tuple-element.22.refs_3_), channel_id=1, source_target_pairs={{0,64},{64,128},{128,192},{192,0},{1,65},{65,129},{129,193},{193,1... | collective-permute-start | bytes 1572872 | tf_op jit(solution)/shard_map/ppermute | solution.py:37
  151.0 15.1 %collective-permute-start.8 = (bf16[64,4096]{1,0:T(8,128)(2,1)S(1)}, bf16[64,4096]{1,0:T(8,128)(2,1)S(1)}, u32[]{:S(2)}, u32[]{:S(2)}) collective-permute-start(bf16[64,4096]{1,0:T(8,128)(2,1)S(1)} %get-tuple-element.27.refs_5_), channel_id=1, source_target_pairs={{0,192},{64,0},{128,64},{192,128},{1,193},{65,1},{129,65},{193,129... | collective-permute-start | bytes 1572872 | tf_op jit(solution)/shard_map/ppermute | solution.py:37
  153.7 16.1 %collective-permute-start.13 = (bf16[64,4096]{1,0:T(8,128)(2,1)S(1)}, bf16[64,4096]{1,0:T(8,128)(2,1)S(1)}, u32[]{:S(2)}, u32[]{:S(2)}) collective-permute-start(bf16[64,4096]{1,0:T(8,128)(2,1)S(1)} %get-tuple-element.32), channel_id=1, source_target_pairs={{0,64},{64,128},{128,192},{192,0},{1,65},{65,129},{129,193},{193,1... | collective-permute-start | bytes 1572872 | tf_op jit(solution)/shard_map/ppermute | solution.py:37
  157.2 19.3 %collective-permute-start.11 = (bf16[64,4096]{1,0:T(8,128)(2,1)S(1)}, bf16[64,4096]{1,0:T(8,128)(2,1)S(1)}, u32[]{:S(2)}, u32[]{:S(2)}) collective-permute-start(bf16[64,4096]{1,0:T(8,128)(2,1)S(1)} %get-tuple-element.29), channel_id=1, source_target_pairs={{0,64},{64,128},{128,192},{192,0},{1,65},{65,129},{129,193},{193,1... | collective-permute-start | bytes 1572872 | tf_op jit(solution)/shard_map/ppermute | solution.py:37
  157.3 19.2 %collective-permute-start.12 = (bf16[64,4096]{1,0:T(8,128)(2,1)S(1)}, bf16[64,4096]{1,0:T(8,128)(2,1)S(1)}, u32[]{:S(2)}, u32[]{:S(2)}) collective-permute-start(bf16[64,4096]{1,0:T(8,128)(2,1)S(1)} %get-tuple-element.31), channel_id=1, source_target_pairs={{0,192},{64,0},{128,64},{192,128},{1,193},{65,1},{129,65},{193,129... | collective-permute-start | bytes 1572872 | tf_op jit(solution)/shard_map/ppermute | solution.py:37
  176.9 10.5 %collective-permute-start.14 = (bf16[64,4096]{1,0:T(8,128)(2,1)S(1)}, bf16[64,4096]{1,0:T(8,128)(2,1)S(1)}, u32[]{:S(2)}, u32[]{:S(2)}) collective-permute-start(bf16[64,4096]{1,0:T(8,128)(2,1)S(1)} %get-tuple-element.33), channel_id=1, source_target_pairs={{0,64},{64,128},{128,192},{192,0},{1,65},{65,129},{129,193},{193,1... | collective-permute-start | bytes 1572872 | tf_op jit(solution)/shard_map/ppermute | solution.py:37
  177.0 10.7 %collective-permute-start.15 = (bf16[64,4096]{1,0:T(8,128)(2,1)S(1)}, bf16[64,4096]{1,0:T(8,128)(2,1)S(1)}, u32[]{:S(2)}, u32[]{:S(2)}) collective-permute-start(bf16[64,4096]{1,0:T(8,128)(2,1)S(1)} %get-tuple-element.35), channel_id=1, source_target_pairs={{0,192},{64,0},{128,64},{192,128},{1,193},{65,1},{129,65},{193,129... | collective-permute-start | bytes 1572872 | tf_op jit(solution)/shard_map/ppermute | solution.py:37
  189.0 19.8 %all-to-all-start.5 = ((bf16[8,16,4096]{2,1,0:T(8,128)(2,1)}), bf16[8,16,4096]{2,1,0:T(8,128)(2,1)S(1)}, u32[]{:S(2)}, u32[]{:S(2)}) async-start(bf16[8,16,4096]{2,1,0:T(8,128)(2,1)} %bitcast.31), calls=%async_computation.5 | async-start | bytes 2097152 | tf_op jit(solution)/shard_map/all_to_all | solution.py:33
  209.1 22.4 %copy-start.4 = (bf16[8,4,8,128]{3,0,2,1:T(8,128)(2,1)S(1)}, bf16[8,4,8,128]{3,0,2,1:T(8,128)(2,1)}, u32[]{:S(2)}) copy-start(bf16[8,4,8,128]{3,0,2,1:T(8,128)(2,1)} %copy.35) | copy-start | bytes 196612
  (5 other events, 52.8 us)

commit v7 on v3

--- a/solution.py
+++ b/solution.py
@@ -1,3 +1,5 @@
+import functools
+
 import jax
 import jax.numpy as jnp
 from jax import lax
@@ -16,6 +18,9 @@
 CTX = ("y", "z")
 EXP = ("x", "core")
 LANES = X * CORE
+VMEM_LIMIT = 20 * 1024 * 1024
+DOWN_LIMIT = 60 * 1024 * 1024
+LOAD_LIMIT = 53 * 1024 * 1024
 BF16 = jnp.bfloat16
 F32 = jnp.float32
 
@@ -64,7 +69,7 @@
         out_shape=[jax.ShapeDtypeStruct((rows, D), BF16)] * 2,
         in_specs=[pl.BlockSpec(memory_space=pltpu.VMEM)] * 2,
         out_specs=[pl.BlockSpec(memory_space=pltpu.VMEM)] * 2,
-        compiler_params=pltpu.CompilerParams(vmem_limit_bytes=32 * 1024 * 1024),
+        compiler_params=pltpu.CompilerParams(vmem_limit_bytes=VMEM_LIMIT),
         cost_estimate=pl.CostEstimate(flops=6 * rows * D, bytes_accessed=8 * rows * D, transcendentals=0),
     )(inbox, gain.reshape(1, D))
 
@@ -72,70 +77,159 @@
 STEPS = 4
 
 
-def expert_kernel(
-    low_ref, high_ref, gate_ref, up_ref, down_ref, out_low_ref, out_high_ref, gate_sum, up_sum, inner
-):
-    step = pl.program_id(0)
-    depth = gate_ref.shape[0]
-    rows = low_ref.shape[0]
-
-    @pl.when(step < STEPS)
-    def _():
-        columns = pl.ds(pl.multiple_of(step * depth, depth), depth)
-        x = jnp.concatenate([low_ref[:, columns], high_ref[:, columns]], axis=0)
-        gate_h = jnp.dot(x, gate_ref[...], preferred_element_type=F32)
-        up_h = jnp.dot(x, up_ref[...], preferred_element_type=F32)
-
-        @pl.when(step == 0)
-        def _():
-            gate_sum[...] = gate_h
-            up_sum[...] = up_h
-
-        @pl.when(step > 0)
-        def _():
-            gate_sum[...] += gate_h
-            up_sum[...] += up_h
-
-    @pl.when(step == STEPS - 1)
-    def _():
-        v = gate_sum[...]
-        inner[...] = (v / (1.0 + jnp.exp(-v)) * up_sum[...]).astype(BF16)
-
-    @pl.when(step >= STEPS)
-    def _():
-        out = jnp.dot(inner[...], down_ref[...], preferred_element_type=F32).astype(BF16)
-        out_low_ref[...] = out[:rows]
-        out_high_ref[...] = out[rows:]
-
-
-def expert(low, high, w_gate, w_up, w_down):
-    rows = low.shape[0]
-    width = w_gate.shape[1]
+def inner_kernel(count, joined, *refs):
+    blocks, (gate_w, up_w) = refs[:count], refs[count : count + 2]
+    x, sems = refs[-2:]
+    outs = refs[-2 - count // joined : -2]
+    rows = blocks[0].shape[0]
     piece = D // STEPS
-    whole = pl.BlockSpec((rows, D), lambda i: (0, 0))
-    into = pl.BlockSpec((piece, width), lambda i: (jnp.minimum(i, STEPS - 1), 0))
-    out_of = pl.BlockSpec((width, piece), lambda i: (0, jnp.maximum(i - STEPS, 0)))
-    result = pl.BlockSpec((rows, piece), lambda i: (0, jnp.maximum(i - STEPS, 0)))
+    parts = [slice(i * piece, (i + 1) * piece) for i in range(STEPS)]
+    copies = []
+    for i, part in enumerate(parts):
+        copies.append(
+            [
+                pltpu.make_async_copy(
+                    block.at[:, part], x.at[j * rows : (j + 1) * rows, part], sems.at[i, j]
+                )
+                for j, block in enumerate(blocks)
+            ]
+        )
+    for step in copies:
+        for copy in step:
+            copy.start()
+    gate_h, up_h = 0.0, 0.0
+    for i, part in enumerate(parts):
+        for copy in copies[i]:
+            copy.wait()
+        gate_h = gate_h + jnp.dot(x[:, part], gate_w[part], preferred_element_type=F32)
+        up_h = up_h + jnp.dot(x[:, part], up_w[part], preferred_element_type=F32)
+    inner = (gate_h / (1.0 + jnp.exp(-gate_h)) * up_h).astype(BF16)
+    for j, out_ref in enumerate(outs):
+        out_ref[...] = inner[joined * j * rows : joined * (j + 1) * rows]
+
+
+def inner_of(blocks, weights, joined, after=()):
+    rows = blocks[0].shape[0]
+    count = len(blocks)
+    width = weights[0].shape[1]
     return pl.pallas_call(
-        expert_kernel,
-        grid=(2 * STEPS,),
-        out_shape=[jax.ShapeDtypeStruct((rows, D), BF16)] * 2,
-        in_specs=[whole, whole, into, into, out_of],
-        out_specs=[result, result],
+        functools.partial(inner_kernel, count, joined),
+        out_shape=[jax.ShapeDtypeStruct((joined * rows, width), BF16)] * (count // joined),
+        in_specs=[pl.BlockSpec(memory_space=pl.ANY)] * count
+        + [pl.BlockSpec(memory_space=pltpu.VMEM)] * 2
+        + [pl.BlockSpec(memory_space=pl.ANY)] * len(after),
+        out_specs=[pl.BlockSpec(memory_space=pltpu.VMEM)] * (count // joined),
         scratch_shapes=[
-            pltpu.VMEM((2 * rows, width), F32),
-            pltpu.VMEM((2 * rows, width), F32),
-            pltpu.VMEM((2 * rows, width), BF16),
+            pltpu.VMEM((count * rows, D), BF16),
+            pltpu.SemaphoreType.DMA((STEPS, count)),
         ],
-        compiler_params=pltpu.CompilerParams(
-            dimension_semantics=("arbitrary",), vmem_limit_bytes=32 * 1024 * 1024
+        compiler_params=pltpu.CompilerParams(vmem_limit_bytes=VMEM_LIMIT),
+        cost_estimate=pl.CostEstimate(
+            flops=4 * count * rows * D * width,
+            bytes_accessed=4 * D * width + 2 * count * rows * D,
+            transcendentals=count * rows * width,
         ),
+    )(*blocks, *weights, *after)
+
+
+def down_kernel(stored, add, *refs):
+    count = len(stored)
+    inners, weights = refs[:count], list(refs[count : 2 * count])
+    held, sems = refs[-2:]
+    results = 1 if add else count
+    outs = refs[-2 - results : -2]
+    copies = []
+    for j in range(count):
+        if not stored[j]:
+            i = len(copies)
+            copies.append(pltpu.make_async_copy(weights[j], held.at[i], sems.at[i]))
+            weights[j] = held.at[i]
+    for copy in copies:
+        copy.start()
+    piece = D // STEPS
+    parts = [slice(i * piece, (i + 1) * piece) for i in range(STEPS)]
+
+    def product(j, part):
+        return jnp.dot(inners[j][...], weights[j][:, part], preferred_element_type=F32)
+
+    if not add:
+        for j in range(count):
+            if stored[j]:
+                for part in parts:
+                    outs[j][:, part] = product(j, part).astype(BF16)
+    for copy in copies:
+        copy.wait()
+    for part in parts:
+        if add:
+            outs[0][:, part] = sum(product(j, part) for j in range(count)).astype(BF16)
+        else:
+            for j in range(count):
+                if not stored[j]:
+                    outs[j][:, part] = product(j, part).astype(BF16)
+
+
+def down(inners, weights, stored, add, after):
+    count = len(inners)
+    rows, width = inners[0].shape
+    vmem, anywhere = pl.BlockSpec(memory_space=pltpu.VMEM), pl.BlockSpec(memory_space=pl.ANY)
+    results = 1 if add else count
+    return pl.pallas_call(
+        functools.partial(down_kernel, stored, add),
+        out_shape=[jax.ShapeDtypeStruct((rows, D), BF16)] * results,
+        in_specs=[vmem] * count
+        + [vmem if kept else anywhere for kept in stored]
+        + [anywhere] * len(after),
+        out_specs=[vmem] * results,
+        scratch_shapes=[
+            pltpu.VMEM((count - sum(stored), width, D), BF16),
+            pltpu.SemaphoreType.DMA((count - sum(stored),)),
+        ],
+        compiler_params=pltpu.CompilerParams(vmem_limit_bytes=DOWN_LIMIT),
         cost_estimate=pl.CostEstimate(
-            flops=12 * rows * D * width,
-            bytes_accessed=6 * D * width + 8 * rows * D,
-            transcendentals=2 * rows * width,
+            flops=2 * count * rows * D * width,
+            bytes_accessed=2 * count * D * width + 8 * rows * D,
+            transcendentals=0,
         ),
-    )(low, high, w_gate, w_up, w_down)
+    )(*inners, *weights, *after)
+
+
+def load_kernel(count, *refs):
+    sources, targets, sems = refs[:count], refs[-1 - count : -1], refs[-1]
+    copies = [
+        pltpu.make_async_copy(source, target, sems.at[i])
+        for i, (source, target) in enumerate(zip(sources, targets))
+    ]
+    for copy in copies:
+        copy.start()
+    for copy in copies:
+        copy.wait()
+
+
+def load(arrays, after):
+    count = len(arrays)
+    return pl.pallas_call(
+        functools.partial(load_kernel, count),
+        out_shape=[pltpu.VMEM(array.shape, array.dtype) for array in arrays],
+        in_specs=[pl.BlockSpec(memory_space=pl.ANY)] * (count + len(after)),
+        out_specs=[pl.BlockSpec(memory_space=pltpu.VMEM)] * count,
+        scratch_shapes=[pltpu.SemaphoreType.DMA((count,))],
+        compiler_params=pltpu.CompilerParams(vmem_limit_bytes=LOAD_LIMIT),
+    )(*arrays, *after)
+
+
+def hand_on_kernel(*refs):
+    pass
+
+
+def hand_on(blocks, after):
+    count = len(blocks)
+    return pl.pallas_call(
+        hand_on_kernel,
+        out_shape=[jax.ShapeDtypeStruct(block.shape, block.dtype) for block in blocks],
+        in_specs=[pl.BlockSpec(memory_space=pl.ANY)] * (count + len(after)),
+        out_specs=[pl.BlockSpec(memory_space=pl.ANY)] * count,
+        input_output_aliases={i: i for i in range(count)},
+    )(*blocks, *after)
 
 
 def slots_of(routes):
@@ -159,6 +253,10 @@
     ctx = lax.axis_index(CTX)
     core = lax.axis_index("core")
     scale = HEAD_SIZE ** (-0.5)
+
+    down_own = w_down[0]
+    down_after = shift(down_own, -1)
+    down_before = shift(down_own, 1)
 
     pieces = [out_weight] + [shift(out_weight, step) for step in range(1, Y)]
     by_distance = jnp.stack(pieces[::-1] * 2)
@@ -200,6 +298,7 @@
         (accumulated / totals[:, None]).reshape(rows_ctx, heads * HEAD_SIZE).astype(BF16)
     )
 
+    (attention,) = hand_on((attention,), pieces[1:])
     hidden_z = hidden.reshape(rows, Y, Z, HEAD_SIZE).transpose(2, 0, 1, 3).reshape(Z, rows, piece)
     gates_high = gates.astype(BF16)
     gates_rest = gates - gates_high.astype(F32)
@@ -232,38 +331,22 @@
     pick = pick.reshape(Z * LANES * Z * MOST, Z * rows).astype(BF16)
     outbox = jnp.dot(pick, residual_c, preferred_element_type=F32).astype(BF16)
     inbox = swap(outbox.reshape(Z * LANES, Z * MOST, piece), ("z",) + EXP)
-    inbox, projected_c = lax.optimization_barrier((inbox, projected_c.astype(BF16)))
     slots = LANES * Z * MOST
     low, high = normalise(inbox, norm_gain)
+    low, high = hand_on((low, high), (down_after, down_before))
 
     after_low = shift(low, -1)
     before_high = shift(high, 1)
     before_low = shift(low, 1)
     after_high = shift(high, -1)
+
+    projected = swap(projected_c.astype(BF16), "z").reshape(Z, rows, Y, HEAD_SIZE)
+    projected = projected.transpose(1, 2, 0, 3).reshape(rows, D)
+
+    after_low, before_high = hand_on((after_low, before_high), (projected,))
     across_low = shift(after_low, -1)
     across_high = shift(before_high, 1)
 
-    projected = swap(projected_c, "z").reshape(Z, rows, Y, HEAD_SIZE)
-    projected = projected.transpose(1, 2, 0, 3).reshape(rows, D)
-    residual = hidden.astype(F32) + projected.astype(F32)
-    attended = residual.astype(BF16)
-
-    weights = (w_gate[0], w_up[0], w_down[0])
-    own_low, own_high = expert(low, high, *weights)
-    out_after_low, out_before_high = expert(after_low, before_high, *weights)
-    out_before_low, out_after_high = expert(before_low, after_high, *weights)
-    home_low = shift(out_before_low, -1)
-    home_high = shift(out_after_high, 1)
-    out_across_low, out_across_high = expert(across_low, across_high, *weights)
-    far_low = shift(out_across_low, 1)
-    far_high = shift(out_across_high, -1)
-    sum_low = shift((out_after_low.astype(F32) + far_low.astype(F32)).astype(BF16), 1)
-    sum_high = shift((out_before_high.astype(F32) + far_high.astype(F32)).astype(BF16), -1)
-    home_low = own_low.astype(F32) + home_low.astype(F32) + sum_low.astype(F32)
-    home_high = own_high.astype(F32) + home_high.astype(F32) + sum_high.astype(F32)
-    returned = jnp.concatenate([home_low.astype(BF16), home_high.astype(BF16)], axis=0)
-
-    back = swap(returned.reshape(LANES, Z * MOST, D), EXP).reshape(slots, D)
     gate = jnp.sum(jnp.where(named, gates_c[..., None], 0.0), axis=2)
     place = jnp.where(chosen, gate[..., None], 0.0).reshape(Z, rows, Z, LANES, MOST)
     place = lax.dynamic_index_in_dim(place, lax.axis_index("z"), 2, keepdims=False)
@@ -271,10 +354,42 @@
     place = place.reshape(Z * rows, slots)
     place_high = place.astype(BF16)
     place_low = (place - place_high.astype(F32)).astype(BF16)
+
+    gate_w, up_w, after_w = load(
+        (w_gate[0], w_up[0], down_after), (place_high, place_low, down_before)
+    )
+    inner_own, inner_after, inner_before = inner_of(
+        (low, high, after_low, after_high, before_low, before_high), (gate_w, up_w), 2
+    )
+    inner_low, inner_high = inner_of(
+        (across_low, across_high), (gate_w, up_w), 1, after=(inner_own,)
+    )
+    from_after = shift(inner_before, -1)
+    from_before = shift(inner_after, 1)
+    relay_low, relay_high = down(
+        (shift(inner_low, 1), shift(inner_high, -1)),
+        (down_before, after_w),
+        (False, True),
+        False,
+        (from_after, from_before),
+    )
+    far = jnp.concatenate([shift(relay_low, 1), shift(relay_high, -1)], axis=0)
+    (near,) = down(
+        (inner_own, from_after, from_before),
+        (down_own, after_w, down_before),
+        (False, True, False),
+        True,
+        (relay_low,),
+    )
+    returned = (near.astype(F32) + far.astype(F32)).astype(BF16)
+
+    back = swap(returned.reshape(LANES, Z * MOST, D), EXP).reshape(slots, D)
     moe_z = jnp.dot(place_high, back, preferred_element_type=F32) + jnp.dot(
         place_low, back, preferred_element_type=F32
     )
     moe = jnp.sum(swap(moe_z.astype(BF16).reshape(Z, rows, D), "z").astype(F32), axis=0)
+    residual = hidden.astype(F32) + projected.astype(F32)
+    attended = residual.astype(BF16)
     mixed = (residual + moe).astype(BF16)
     return (attended, mixed)
 

time: 268 us -> 230 us (0.86)
  waiting for transfers between devices: 140 us -> 90.2 us
  blocking collectives: 0 us -> 22.8 us
  local copies, waits for them, and re-layouts: 25 us -> 15.1 us
  Pallas kernels: 21.2 us -> 25.2 us
  starting transfers between devices: 62.7 us -> 59.6 us
    ppermute x15 -> x17, waiting for transfers between devices: 44.7 us -> 12.9 us  [shift(): return lax.ppermute(block, 'y', [(i, (i + step) % Y) for i in range(Y)])]
    all_to_all x0 -> x1, blocking collectives: none -> 22.8 us  [swap(): return lax.all_to_all(blocks, axes, 0, 0, tiled=True)]
    all_to_all x6 -> x5, waiting for transfers between devices: 89.4 us -> 72.8 us  [swap(): return lax.all_to_all(blocks, axes, 0, 0, tiled=True)]
    all_to_all x6 -> x5, starting transfers between devices: 30.6 us -> 23.2 us  [swap(): return lax.all_to_all(blocks, axes, 0, 0, tiled=True)]
    unnamed x35 -> x55, local copies, waits for them, and re-layouts: 10.6 us -> 4.28 us
    pallas_call x4 -> x8, Pallas kernels: 19.4 us -> 24.7 us  [the longest x2 13.1 us: down(): pl.pallas_call(functools.partial(down_kernel, stored, add), out_shape=[ja...]
    ppermute x15 -> x17, starting transfers between devices: 20.6 us -> 24.9 us  [shift(): return lax.ppermute(block, 'y', [(i, (i + step) % Y) for i in range(Y)])]
  transfers between devices with their start and end apart: 23 -> 24, of which waited for: 14 -> 12; matrix products, arithmetic and copies ran while one was open for 7% -> 8% of each run, Pallas kernels for 7% -> 9%
where the time goes in v7:
time: 230 us; the launch traced here: 228 us
  waiting for transfers between devices  90.2 us (39%)
  starting transfers between devices  59.6 us (26%)
  Pallas kernels  25.2 us (11%)
  blocking collectives  22.8 us (10%)
  local copies, waits for them, and re-layouts  15.1 us (7%)
  other arithmetic  9.8 us (4%)
  matrix products  4.36 us (2%)
    all_to_all x5, waiting for transfers between devices, swap(): return lax.all_to_all(blocks, axes, 0, 0, tiled=True)  72.8 us
    ppermute x17, starting transfers between devices, shift(): return lax.ppermute(block, 'y', [(i, (i + step) % Y) for i in range(Y)])  24.9 us
    all_to_all x5, starting transfers between devices, swap(): return lax.all_to_all(blocks, axes, 0, 0, tiled=True)  23.2 us
    all_to_all x1, blocking collectives, swap(): return lax.all_to_all(blocks, axes, 0, 0, tiled=True)  22.8 us
    pallas_call x2, Pallas kernels, down(): pl.pallas_call(functools.partial(down_kernel, stored, add), out_shape=[ja...  13.1 us
    ppermute x17, waiting for transfers between devices, shift(): return lax.ppermute(block, 'y', [(i, (i + step) % Y) for i in range(Y)])  12.9 us
    all_to_all x1, starting transfers between devices, spread(): lax.all_to_all(jnp.broadcast_to(block[None], (count,) + block.shape), axe...  11.5 us
    pallas_call x2, Pallas kernels, inner_of(): pl.pallas_call(functools.partial(inner_kernel, count, joined), out_shape=...  7.76 us
  transfers between devices with their start and end apart: 24, of which 12 were waited for; matrix products, arithmetic and copies ran while one was open for 8% of the time, Pallas kernels for 9%

profile of v7, /device:TPU:2, one launch (start us, length us, event | category | flops | bytes accessed | tf_op | source)
XLA Modules:
  0.0 228.4 jit_solution(15426564798556435644)
XLA Ops:
  2.9 11.5 %all-to-all-start = ((bf16[32,32,256]{2,1,0:T(8,128)(2,1)}), bf16[32,32,256]{2,1,0:T(8,128)(2,1)S(1)}, u32[]{:S(2)}, u32[]{:S(2)}) async-start(bf16[32,32,256]{2,1,0:T(8,128)(2,1)} %broadcast_in_dim.54), calls=%async_computation | async-start | bytes 1048576 | tf_op jit(solution)/shard_map/all_to_all | solution.py:29
  14.4 3.1 %collective-permute-start = (bf16[512,128]{1,0:T(8,128)(2,1)}, bf16[512,128]{1,0:T(8,128)(2,1)S(1)}, u32[]{:S(2)}, u32[]{:S(2)}) collective-permute-start(bf16[512,128]{1,0:T(8,128)(2,1)} %param.15), channel_id=1, source_target_pairs={{0,192},{64,0},{128,64},{192,128},{1,193},{65,1},{129,65},{193,129... | collective-permute-start | bytes 393224 | tf_op jit(solution)/shard_map/ppermute | solution.py:39
  28.2 3.0 %all-to-all-done = bf16[32,32,256]{2,1,0:T(8,128)(2,1)S(1)} async-done(((bf16[32,32,256]{2,1,0:T(8,128)(2,1)}), bf16[32,32,256]{2,1,0:T(8,128)(2,1)S(1)}, u32[]{:S(2)}, u32[]{:S(2)}) %all-to-all-start) | async-done | bytes 524320 | tf_op jit(solution)/shard_map/all_to_all | solution.py:29
  38.0 4.4 %all-to-all-start.1 = ((bf16[8,80,512]{2,1,0:T(8,128)(2,1)}), bf16[8,80,512]{2,1,0:T(8,128)(2,1)S(1)}, u32[]{:S(2)}, u32[]{:S(2)}) async-start(bf16[8,80,512]{2,1,0:T(8,128)(2,1)} %pad_maximum_fusion), calls=%async_computation.1 | async-start | bytes 1310720 | tf_op jit(solution)/shard_map/all_to_all | solution.py:35
  42.8 20.2 %all-to-all-done.1 = bf16[8,80,512]{2,1,0:T(8,128)(2,1)S(1)} async-done(((bf16[8,80,512]{2,1,0:T(8,128)(2,1)}), bf16[8,80,512]{2,1,0:T(8,128)(2,1)S(1)}, u32[]{:S(2)}, u32[]{:S(2)}) %all-to-all-start.1) | async-done | bytes 655392 | tf_op jit(solution)/shard_map/all_to_all | solution.py:35
  64.8 4.8 %all-to-all-start.2 = ((bf16[8,8,8,512]{3,2,1,0:T(8,128)(2,1)}), bf16[8,8,8,512]{3,2,1,0:T(8,128)(2,1)S(1)}, u32[]{:S(2)}, u32[]{:S(2)}) async-start(bf16[8,8,8,512]{3,2,1,0:T(8,128)(2,1)} %copy.39), calls=%async_computation.2 | async-start | bytes 1048576 | tf_op jit(solution)/shard_map/all_to_all | solution.py:35
  72.7 5.8 %all-to-all-done.2 = bf16[8,8,8,512]{3,2,1,0:T(8,128)(2,1)S(1)} async-done(((bf16[8,8,8,512]{3,2,1,0:T(8,128)(2,1)}), bf16[8,8,8,512]{3,2,1,0:T(8,128)(2,1)S(1)}, u32[]{:S(2)}, u32[]{:S(2)}) %all-to-all-start.2) | async-done | bytes 524320 | tf_op jit(solution)/shard_map/all_to_all | solution.py:35
  80.0 5.9 %all-to-all-start.4 = ((bf16[64,16,512]{2,1,0:T(8,128)(2,1)}), bf16[64,16,512]{2,1,0:T(8,128)(2,1)S(1)}, u32[]{:S(2)}, u32[]{:S(2)}) async-start(bf16[64,16,512]{2,1,0:T(8,128)(2,1)} %bitcast.27), calls=%async_computation.4 | async-start | bytes 2097152 | tf_op jit(solution)/shard_map/all_to_all | solution.py:35
  86.9 27.8 %all-to-all-done.4.x_ref = bf16[64,16,512]{2,1,0:T(8,128)(2,1)S(1)} async-done(((bf16[64,16,512]{2,1,0:T(8,128)(2,1)}), bf16[64,16,512]{2,1,0:T(8,128)(2,1)S(1)}, u32[]{:S(2)}, u32[]{:S(2)}) %all-to-all-start.4) | async-done | bytes 1048608 | tf_op jit(solution)/shard_map/all_to_all | solution.py:35
  120.3 3.4 %all-to-all-start.3 = ((bf16[8,8,512]{2,1,0:T(8,128)(2,1)}), bf16[8,8,512]{2,1,0:T(8,128)(2,1)S(1)}, u32[]{:S(2)}, u32[]{:S(2)}) async-start(bf16[8,8,512]{2,1,0:T(8,128)(2,1)} %convert_element_type.151), calls=%async_computation.3 | async-start | bytes 131072 | tf_op jit(solution)/shard_map/all_to_all | solution.py:35
  123.7 3.3 %collective-permute-start.8 = (bf16[64,4096]{1,0:T(8,128)(2,1)}, bf16[64,4096]{1,0:T(8,128)(2,1)}, u32[]{:S(2)}, u32[]{:S(2)}) collective-permute-start(bf16[64,4096]{1,0:T(8,128)(2,1)} %get-tuple-element.21.refs_1_), channel_id=1, source_target_pairs={{0,192},{64,0},{128,64},{192,128},{1,193},{65,1},{129,65},{193,129... | collective-permute-start | bytes 1572872 | tf_op jit(solution)/shard_map/ppermute | solution.py:39
  127.0 5.0 %all-to-all-done.3 = bf16[8,8,512]{2,1,0:T(8,128)(2,1)S(1)} async-done(((bf16[8,8,512]{2,1,0:T(8,128)(2,1)}), bf16[8,8,512]{2,1,0:T(8,128)(2,1)S(1)}, u32[]{:S(2)}, u32[]{:S(2)}) %all-to-all-start.3) | async-done | bytes 65568 | tf_op jit(solution)/shard_map/all_to_all | solution.py:35
  132.6 3.3 %collective-permute-done.7.refs_1_ = bf16[64,4096]{1,0:T(8,128)(2,1)S(1)} collective-permute-done((bf16[64,4096]{1,0:T(8,128)(2,1)}, bf16[64,4096]{1,0:T(8,128)(2,1)S(1)}, u32[]{:S(2)}, u32[]{:S(2)}) %collective-permute-start.7) | collective-permute-done | bytes 524320 | tf_op jit(solution)/shard_map/ppermute | solution.py:39
  139.8 3.9 %shard_map.126 = (bf16[4096,384]{1,0:T(8,128)(2,1)S(1)}, bf16[4096,384]{1,0:T(8,128)(2,1)S(1)}, bf16[384,4096]{1,0:T(8,128)(2,1)S(1)}) custom-call(bf16[4096,384]{1,0:T(8,128)(2,1)} %bitcast.94, bf16[4096,384]{1,0:T(8,128)(2,1)} %bitcast.95, bf16[384,4096]{1,0:T(8,128)(2,1)} %collective-permute-done.4.refs_2_, bf16[64,128]{1,0:T(8,128)(2,1)} %get-tuple-element.37.refs_3_, ...), custom_call_target="tpu_custom_call" | custom-call | tf_op jit(solution)/shard_map/pallas_call | solution.py:210
  143.7 3.5 %collective-permute-done.9.refs_4_ = bf16[64,4096]{1,0:T(8,128)(2,1)} collective-permute-done((bf16[64,4096]{1,0:T(8,128)(2,1)}, bf16[64,4096]{1,0:T(8,128)(2,1)}, u32[]{:S(2)}, u32[]{:S(2)}) %collective-permute-start.9) | collective-permute-done | bytes 524320 | tf_op jit(solution)/shard_map/ppermute | solution.py:39
  148.3 5.0 %shard_map.127 = (bf16[128,384]{1,0:T(8,128)(2,1)S(1)}, bf16[128,384]{1,0:T(8,128)(2,1)S(1)}, bf16[128,384]{1,0:T(8,128)(2,1)S(1)}) custom-call(bf16[64,4096]{1,0:T(8,128)(2,1)S(1)} %copy-done.2, bf16[64,4096]{1,0:T(8,128)(2,1)S(1)} %copy-done.4, bf16[64,4096]{1,0:T(8,128)(2,1)S(1)} %copy-done.6, bf16[64,4096]{1,0:T(8,128)(2,1)} %collective-permute-done.8.refs_3_, ...), custom_call_target="tpu_custom_call" | custom-call | flops 2415919104 | bytes 9437184 | tf_op jit(solution)/shard_map/pallas_call | solution.py:115
  157.1 2.8 %shard_map.128 = (bf16[64,384]{1,0:T(8,128)(2,1)S(1)}, bf16[64,384]{1,0:T(8,128)(2,1)S(1)}) custom-call(bf16[64,4096]{1,0:T(8,128)(2,1)} %collective-permute-done.12.refs_0_, bf16[64,4096]{1,0:T(8,128)(2,1)} %collective-permute-done.13.refs_1_, bf16[4096,384]{1,0:T(8,128)(2,1)S(1)} %get-tuple-element.24.refs_6_.refs_2_, ...), custom_call_target="tpu_custom_call" | custom-call | flops 805306368 | bytes 7340032 | tf_op jit(solution)/shard_map/pallas_call | solution.py:115
  160.0 3.2 %collective-permute-start.15 = (bf16[64,384]{1,0:T(8,128)(2,1)S(1)}, bf16[64,384]{1,0:T(8,128)(2,1)S(1)}, u32[]{:S(2)}, u32[]{:S(2)}) collective-permute-start(bf16[64,384]{1,0:T(8,128)(2,1)S(1)} %get-tuple-element.31), channel_id=1, source_target_pairs={{0,192},{64,0},{128,64},{192,128},{1,193},{65,1},{129,65},{193,129... | collective-permute-start | bytes 147464 | tf_op jit(solution)/shard_map/ppermute | solution.py:39
  165.9 5.4 %shard_map.129 = (bf16[64,4096]{1,0:T(8,128)(2,1)}, bf16[64,4096]{1,0:T(8,128)(2,1)}) custom-call(bf16[64,384]{1,0:T(8,128)(2,1)} %copy-done.22, bf16[64,384]{1,0:T(8,128)(2,1)} %copy-done.23, bf16[384,4096]{1,0:T(8,128)(2,1)} %collective-permute-done.5.refs_3_.refs_5_.refs_2_, bf16[384,4096]{1,0:T(8,128)(2,1)} %copy-done, bf16[128,384]{1,0:T(8,128)(2,1)} %copy-done.19, ...), custom_call_target="tpu_custom_call" | custom-call | flops 402653184 | bytes 8388608 | tf_op jit(solution)/shard_map/pallas_call | solution.py:176
  171.4 3.3 %collective-permute-start.17 = (bf16[64,4096]{1,0:T(8,128)(2,1)}, bf16[64,4096]{1,0:T(8,128)(2,1)S(1)}, u32[]{:S(2)}, u32[]{:S(2)}) collective-permute-start(bf16[64,4096]{1,0:T(8,128)(2,1)} %get-tuple-element.33), channel_id=1, source_target_pairs={{0,192},{64,0},{128,64},{192,128},{1,193},{65,1},{129,65},{193,129... | collective-permute-start | bytes 1572872 | tf_op jit(solution)/shard_map/ppermute | solution.py:39
  174.7 7.7 %shard_map.130 = bf16[128,4096]{1,0:T(8,128)(2,1)} custom-call(bf16[128,384]{1,0:T(8,128)(2,1)} %copy-done.9, bf16[128,384]{1,0:T(8,128)(2,1)} %copy-done.19, bf16[128,384]{1,0:T(8,128)(2,1)} %copy-done.20, bf16[384,4096]{1,0:T(8,128)(2,1)} %bitcast.98, bf16[384,4096]{1,0:T(8,128)(2,1)} %copy-done, ...), custom_call_target="tpu_custom_call" | custom-call | flops 1207959552 | bytes 13631488 | tf_op jit(solution)/shard_map/pallas_call | solution.py:176
  184.8 4.8 %all-to-all-start.5 = ((bf16[8,16,4096]{2,1,0:T(8,128)(2,1)}), bf16[8,16,4096]{2,1,0:T(8,128)(2,1)S(1)}, u32[]{:S(2)}, u32[]{:S(2)}) async-start(bf16[8,16,4096]{2,1,0:T(8,128)(2,1)} %bitcast.32), calls=%async_computation.5 | async-start | bytes 2097152 | tf_op jit(solution)/shard_map/all_to_all | solution.py:35
  190.1 14.0 %all-to-all-done.5 = bf16[8,16,4096]{2,1,0:T(8,128)(2,1)S(1)} async-done(((bf16[8,16,4096]{2,1,0:T(8,128)(2,1)}), bf16[8,16,4096]{2,1,0:T(8,128)(2,1)S(1)}, u32[]{:S(2)}, u32[]{:S(2)}) %all-to-all-start.5) | async-done | bytes 1048608 | tf_op jit(solution)/shard_map/all_to_all | solution.py:35
  204.8 22.8 %all_to_all.35 = bf16[8,8,4096]{2,1,0:T(8,128)(2,1)S(1)} all-to-all(bf16[8,8,4096]{2,1,0:T(8,128)(2,1)S(1)} %fusion.1), channel_id=1, replica_groups=mesh['y'=4,'z'=8,'x'=4,'core'=2] {'z'}, dimensions={0} | all-to-all | bytes 1048576 | tf_op jit(solution)/shard_map/all_to_all | solution.py:35
  (157 shorter events, 49.2 us)
Async XLA Ops:
  2.9 28.4 %all-to-all-start = ((bf16[32,32,256]{2,1,0:T(8,128)(2,1)}), bf16[32,32,256]{2,1,0:T(8,128)(2,1)S(1)}, u32[]{:S(2)}, u32[]{:S(2)}) async-start(bf16[32,32,256]{2,1,0:T(8,128)(2,1)} %broadcast_in_dim.54), calls=%async_computation | async-start | bytes 1048576 | tf_op jit(solution)/shard_map/all_to_all | solution.py:29
  14.4 13.8 %collective-permute-start = (bf16[512,128]{1,0:T(8,128)(2,1)}, bf16[512,128]{1,0:T(8,128)(2,1)S(1)}, u32[]{:S(2)}, u32[]{:S(2)}) collective-permute-start(bf16[512,128]{1,0:T(8,128)(2,1)} %param.15), channel_id=1, source_target_pairs={{0,192},{64,0},{128,64},{192,128},{1,193},{65,1},{129,65},{193,129... | collective-permute-start | bytes 393224 | tf_op jit(solution)/shard_map/ppermute | solution.py:39
  17.5 13.8 %collective-permute-start.1 = (bf16[512,128]{1,0:T(8,128)(2,1)}, bf16[512,128]{1,0:T(8,128)(2,1)S(1)}, u32[]{:S(2)}, u32[]{:S(2)}) collective-permute-start(bf16[512,128]{1,0:T(8,128)(2,1)} %param.15), channel_id=1, source_target_pairs={{0,128},{64,192},{128,0},{192,64},{1,129},{65,193},{129,1},{193,65... | collective-permute-start | bytes 393224 | tf_op jit(solution)/shard_map/ppermute | solution.py:39
  18.4 13.0 %collective-permute-start.2 = (bf16[512,128]{1,0:T(8,128)(2,1)}, bf16[512,128]{1,0:T(8,128)(2,1)S(1)}, u32[]{:S(2)}, u32[]{:S(2)}) collective-permute-start(bf16[512,128]{1,0:T(8,128)(2,1)} %param.15), channel_id=1, source_target_pairs={{0,64},{64,128},{128,192},{192,0},{1,65},{65,129},{129,193},{193,1... | collective-permute-start | bytes 393224 | tf_op jit(solution)/shard_map/ppermute | solution.py:39
  19.2 97.7 %collective-permute-start.5 = (bf16[384,4096]{1,0:T(8,128)(2,1)}, bf16[384,4096]{1,0:T(8,128)(2,1)}, u32[]{:S(2)}, u32[]{:S(2)}) collective-permute-start(bf16[384,4096]{1,0:T(8,128)(2,1)} %bitcast.96), channel_id=1, source_target_pairs={{0,64},{64,128},{128,192},{192,0},{1,65},{65,129},{129,193},{193,1... | collective-permute-start | bytes 9437192 | tf_op jit(solution)/shard_map/ppermute | solution.py:39
  21.0 95.9 %collective-permute-start.4 = (bf16[384,4096]{1,0:T(8,128)(2,1)}, bf16[384,4096]{1,0:T(8,128)(2,1)}, u32[]{:S(2)}, u32[]{:S(2)}) collective-permute-start(bf16[384,4096]{1,0:T(8,128)(2,1)} %bitcast.97), channel_id=1, source_target_pairs={{0,192},{64,0},{128,64},{192,128},{1,193},{65,1},{129,65},{193,129... | collective-permute-start | bytes 9437192 | tf_op jit(solution)/shard_map/ppermute | solution.py:39
  31.3 1.9 collective-permute-start.3
  38.0 25.0 %all-to-all-start.1 = ((bf16[8,80,512]{2,1,0:T(8,128)(2,1)}), bf16[8,80,512]{2,1,0:T(8,128)(2,1)S(1)}, u32[]{:S(2)}, u32[]{:S(2)}) async-start(bf16[8,80,512]{2,1,0:T(8,128)(2,1)} %pad_maximum_fusion), calls=%async_computation.1 | async-start | bytes 1310720 | tf_op jit(solution)/shard_map/all_to_all | solution.py:35
  64.8 13.7 %all-to-all-start.2 = ((bf16[8,8,8,512]{3,2,1,0:T(8,128)(2,1)}), bf16[8,8,8,512]{3,2,1,0:T(8,128)(2,1)S(1)}, u32[]{:S(2)}, u32[]{:S(2)}) async-start(bf16[8,8,8,512]{3,2,1,0:T(8,128)(2,1)} %copy.39), calls=%async_computation.2 | async-start | bytes 1048576 | tf_op jit(solution)/shard_map/all_to_all | solution.py:35
  80.0 34.8 %all-to-all-start.4 = ((bf16[64,16,512]{2,1,0:T(8,128)(2,1)}), bf16[64,16,512]{2,1,0:T(8,128)(2,1)S(1)}, u32[]{:S(2)}, u32[]{:S(2)}) async-start(bf16[64,16,512]{2,1,0:T(8,128)(2,1)} %bitcast.27), calls=%async_computation.4 | async-start | bytes 2097152 | tf_op jit(solution)/shard_map/all_to_all | solution.py:35
  116.9 15.7 %collective-permute-start.6 = (bf16[64,4096]{1,0:T(8,128)(2,1)}, bf16[64,4096]{1,0:T(8,128)(2,1)S(1)}, u32[]{:S(2)}, u32[]{:S(2)}) collective-permute-start(bf16[64,4096]{1,0:T(8,128)(2,1)} %get-tuple-element.20.refs_0_), channel_id=1, source_target_pairs={{0,192},{64,0},{128,64},{192,128},{1,193},{65,1},{129,65},{193,129... | collective-permute-start | bytes 1572872 | tf_op jit(solution)/shard_map/ppermute | solution.py:39
  119.7 16.3 %collective-permute-start.7 = (bf16[64,4096]{1,0:T(8,128)(2,1)}, bf16[64,4096]{1,0:T(8,128)(2,1)S(1)}, u32[]{:S(2)}, u32[]{:S(2)}) collective-permute-start(bf16[64,4096]{1,0:T(8,128)(2,1)} %get-tuple-element.21.refs_1_), channel_id=1, source_target_pairs={{0,64},{64,128},{128,192},{192,0},{1,65},{65,129},{129,193},{193,1... | collective-permute-start | bytes 1572872 | tf_op jit(solution)/shard_map/ppermute | solution.py:39
  120.3 11.7 %all-to-all-start.3 = ((bf16[8,8,512]{2,1,0:T(8,128)(2,1)}), bf16[8,8,512]{2,1,0:T(8,128)(2,1)S(1)}, u32[]{:S(2)}, u32[]{:S(2)}) async-start(bf16[8,8,512]{2,1,0:T(8,128)(2,1)} %convert_element_type.151), calls=%async_computation.3 | async-start | bytes 131072 | tf_op jit(solution)/shard_map/all_to_all | solution.py:35
  123.7 20.1 %collective-permute-start.8 = (bf16[64,4096]{1,0:T(8,128)(2,1)}, bf16[64,4096]{1,0:T(8,128)(2,1)}, u32[]{:S(2)}, u32[]{:S(2)}) collective-permute-start(bf16[64,4096]{1,0:T(8,128)(2,1)} %get-tuple-element.21.refs_1_), channel_id=1, source_target_pairs={{0,192},{64,0},{128,64},{192,128},{1,193},{65,1},{129,65},{193,129... | collective-permute-start | bytes 1572872 | tf_op jit(solution)/shard_map/ppermute | solution.py:39
  127.0 20.3 %collective-permute-start.9 = (bf16[64,4096]{1,0:T(8,128)(2,1)}, bf16[64,4096]{1,0:T(8,128)(2,1)}, u32[]{:S(2)}, u32[]{:S(2)}) collective-permute-start(bf16[64,4096]{1,0:T(8,128)(2,1)} %get-tuple-element.20.refs_0_), channel_id=1, source_target_pairs={{0,64},{64,128},{128,192},{192,0},{1,65},{65,129},{129,193},{193,1... | collective-permute-start | bytes 1572872 | tf_op jit(solution)/shard_map/ppermute | solution.py:39
  136.7 18.7 %collective-permute-start.12 = (bf16[64,4096]{1,0:T(8,128)(2,1)}, bf16[64,4096]{1,0:T(8,128)(2,1)}, u32[]{:S(2)}, u32[]{:S(2)}) collective-permute-start(bf16[64,4096]{1,0:T(8,128)(2,1)} %get-tuple-element.22.refs_2_), channel_id=1, source_target_pairs={{0,192},{64,0},{128,64},{192,128},{1,193},{65,1},{129,65},{193,129... | collective-permute-start | bytes 1572872 | tf_op jit(solution)/shard_map/ppermute | solution.py:39
  136.9 20.1 %collective-permute-start.13 = (bf16[64,4096]{1,0:T(8,128)(2,1)}, bf16[64,4096]{1,0:T(8,128)(2,1)}, u32[]{:S(2)}, u32[]{:S(2)}) collective-permute-start(bf16[64,4096]{1,0:T(8,128)(2,1)} %get-tuple-element.23.refs_5_), channel_id=1, source_target_pairs={{0,64},{64,128},{128,192},{192,0},{1,65},{65,129},{129,193},{193,1... | collective-permute-start | bytes 1572872 | tf_op jit(solution)/shard_map/ppermute | solution.py:39
  153.3 9.9 %collective-permute-start.10 = (bf16[128,384]{1,0:T(8,128)(2,1)S(1)}, bf16[128,384]{1,0:T(8,128)(2,1)S(1)}, u32[]{:S(2)}, u32[]{:S(2)}) collective-permute-start(bf16[128,384]{1,0:T(8,128)(2,1)S(1)} %get-tuple-element.27), channel_id=1, source_target_pairs={{0,192},{64,0},{128,64},{192,128},{1,193},{65,1},{129,65},{193,129... | collective-permute-start | bytes 294920 | tf_op jit(solution)/shard_map/ppermute | solution.py:39
  153.4 9.8 %collective-permute-start.11 = (bf16[128,384]{1,0:T(8,128)(2,1)S(1)}, bf16[128,384]{1,0:T(8,128)(2,1)S(1)}, u32[]{:S(2)}, u32[]{:S(2)}) collective-permute-start(bf16[128,384]{1,0:T(8,128)(2,1)S(1)} %get-tuple-element.28), channel_id=1, source_target_pairs={{0,64},{64,128},{128,192},{192,0},{1,65},{65,129},{129,193},{193,1... | collective-permute-start | bytes 294920 | tf_op jit(solution)/shard_map/ppermute | solution.py:39
  159.9 5.4 %collective-permute-start.14 = (bf16[64,384]{1,0:T(8,128)(2,1)S(1)}, bf16[64,384]{1,0:T(8,128)(2,1)S(1)}, u32[]{:S(2)}, u32[]{:S(2)}) collective-permute-start(bf16[64,384]{1,0:T(8,128)(2,1)S(1)} %get-tuple-element.30), channel_id=1, source_target_pairs={{0,64},{64,128},{128,192},{192,0},{1,65},{65,129},{129,193},{193,1... | collective-permute-start | bytes 147464 | tf_op jit(solution)/shard_map/ppermute | solution.py:39
  160.0 5.3 %collective-permute-start.15 = (bf16[64,384]{1,0:T(8,128)(2,1)S(1)}, bf16[64,384]{1,0:T(8,128)(2,1)S(1)}, u32[]{:S(2)}, u32[]{:S(2)}) collective-permute-start(bf16[64,384]{1,0:T(8,128)(2,1)S(1)} %get-tuple-element.31), channel_id=1, source_target_pairs={{0,192},{64,0},{128,64},{192,128},{1,193},{65,1},{129,65},{193,129... | collective-permute-start | bytes 147464 | tf_op jit(solution)/shard_map/ppermute | solution.py:39
  171.3 11.1 %collective-permute-start.16 = (bf16[64,4096]{1,0:T(8,128)(2,1)}, bf16[64,4096]{1,0:T(8,128)(2,1)S(1)}, u32[]{:S(2)}, u32[]{:S(2)}) collective-permute-start(bf16[64,4096]{1,0:T(8,128)(2,1)} %get-tuple-element.32.refs_6_), channel_id=1, source_target_pairs={{0,64},{64,128},{128,192},{192,0},{1,65},{65,129},{129,193},{193,1... | collective-permute-start | bytes 1572872 | tf_op jit(solution)/shard_map/ppermute | solution.py:39
  171.4 11.0 %collective-permute-start.17 = (bf16[64,4096]{1,0:T(8,128)(2,1)}, bf16[64,4096]{1,0:T(8,128)(2,1)S(1)}, u32[]{:S(2)}, u32[]{:S(2)}) collective-permute-start(bf16[64,4096]{1,0:T(8,128)(2,1)} %get-tuple-element.33), channel_id=1, source_target_pairs={{0,192},{64,0},{128,64},{192,128},{1,193},{65,1},{129,65},{193,129... | collective-permute-start | bytes 1572872 | tf_op jit(solution)/shard_map/ppermute | solution.py:39
  184.8 19.3 %all-to-all-start.5 = ((bf16[8,16,4096]{2,1,0:T(8,128)(2,1)}), bf16[8,16,4096]{2,1,0:T(8,128)(2,1)S(1)}, u32[]{:S(2)}, u32[]{:S(2)}) async-start(bf16[8,16,4096]{2,1,0:T(8,128)(2,1)} %bitcast.32), calls=%async_computation.5 | async-start | bytes 2097152 | tf_op jit(solution)/shard_map/all_to_all | solution.py:35
  (24 other events, 170.1 us)

commit v8 on v7

--- a/solution.py
+++ b/solution.py
@@ -298,7 +298,6 @@
         (accumulated / totals[:, None]).reshape(rows_ctx, heads * HEAD_SIZE).astype(BF16)
     )
 
-    (attention,) = hand_on((attention,), pieces[1:])
     hidden_z = hidden.reshape(rows, Y, Z, HEAD_SIZE).transpose(2, 0, 1, 3).reshape(Z, rows, piece)
     gates_high = gates.astype(BF16)
     gates_rest = gates - gates_high.astype(F32)
@@ -314,6 +313,7 @@
         ],
         axis=1,
     )
+    (parcel,) = hand_on((parcel,), pieces[1:])
     parcel = swap(parcel, "z")
     attention_z = parcel[:, :rows_ctx].reshape(Z, LANES, rows, piece)
     hidden_c = parcel[:, rows_ctx : rows_ctx + rows].astype(F32)

time: 230 us -> 229 us (level)
  no operation moved by 1% of the time
where the time goes in v8:
time: 229 us; the launch traced here: 227 us
  waiting for transfers between devices  90.2 us (39%)
  starting transfers between devices  59.7 us (26%)
  Pallas kernels  25.2 us (11%)
  blocking collectives  22.8 us (10%)
  local copies, waits for them, and re-layouts  13.5 us (6%)
  other arithmetic  9.81 us (4%)
  matrix products  4.36 us (2%)
    all_to_all x5, waiting for transfers between devices, swap(): return lax.all_to_all(blocks, axes, 0, 0, tiled=True)  72.8 us
    ppermute x17, starting transfers between devices, shift(): return lax.ppermute(block, 'y', [(i, (i + step) % Y) for i in range(Y)])  24.9 us
    all_to_all x5, starting transfers between devices, swap(): return lax.all_to_all(blocks, axes, 0, 0, tiled=True)  23.4 us
    all_to_all x1, blocking collectives, swap(): return lax.all_to_all(blocks, axes, 0, 0, tiled=True)  22.8 us
    pallas_call x2, Pallas kernels, down(): pl.pallas_call(functools.partial(down_kernel, stored, add), out_shape=[ja...  13.1 us
    ppermute x17, waiting for transfers between devices, shift(): return lax.ppermute(block, 'y', [(i, (i + step) % Y) for i in range(Y)])  12.9 us
    all_to_all x1, starting transfers between devices, spread(): lax.all_to_all(jnp.broadcast_to(block[None], (count,) + block.shape), axe...  11.5 us
    pallas_call x2, Pallas kernels, inner_of(): pl.pallas_call(functools.partial(inner_kernel, count, joined), out_shape=...  7.75 us
  transfers between devices with their start and end apart: 24, of which 12 were waited for; matrix products, arithmetic and copies ran while one was open for 8% of the time, Pallas kernels for 9%

profile of v8, /device:TPU:2, one launch (start us, length us, event | category | flops | bytes accessed | tf_op | source)
XLA Modules:
  0.0 227.0 jit_solution(10951530342387631396)
XLA Ops:
  2.9 11.5 %all-to-all-start = ((bf16[32,32,256]{2,1,0:T(8,128)(2,1)}), bf16[32,32,256]{2,1,0:T(8,128)(2,1)S(1)}, u32[]{:S(2)}, u32[]{:S(2)}) async-start(bf16[32,32,256]{2,1,0:T(8,128)(2,1)} %broadcast_in_dim.54), calls=%async_computation | async-start | bytes 1048576 | tf_op jit(solution)/shard_map/all_to_all | solution.py:29
  14.4 3.1 %collective-permute-start = (bf16[512,128]{1,0:T(8,128)(2,1)}, bf16[512,128]{1,0:T(8,128)(2,1)S(1)}, u32[]{:S(2)}, u32[]{:S(2)}) collective-permute-start(bf16[512,128]{1,0:T(8,128)(2,1)} %param.15), channel_id=1, source_target_pairs={{0,192},{64,0},{128,64},{192,128},{1,193},{65,1},{129,65},{193,129... | collective-permute-start | bytes 393224 | tf_op jit(solution)/shard_map/ppermute | solution.py:39
  28.2 3.0 %all-to-all-done = bf16[32,32,256]{2,1,0:T(8,128)(2,1)S(1)} async-done(((bf16[32,32,256]{2,1,0:T(8,128)(2,1)}), bf16[32,32,256]{2,1,0:T(8,128)(2,1)S(1)}, u32[]{:S(2)}, u32[]{:S(2)}) %all-to-all-start) | async-done | bytes 524320 | tf_op jit(solution)/shard_map/all_to_all | solution.py:29
  36.5 4.6 %all-to-all-start.1 = ((bf16[8,80,512]{2,1,0:T(8,128)(2,1)}), bf16[8,80,512]{2,1,0:T(8,128)(2,1)S(1)}, u32[]{:S(2)}, u32[]{:S(2)}) async-start(bf16[8,80,512]{2,1,0:T(8,128)(2,1)} %shard_map.122), calls=%async_computation.1 | async-start | bytes 1310720 | tf_op jit(solution)/shard_map/all_to_all | solution.py:35
  41.5 20.2 %all-to-all-done.1 = bf16[8,80,512]{2,1,0:T(8,128)(2,1)S(1)} async-done(((bf16[8,80,512]{2,1,0:T(8,128)(2,1)}), bf16[8,80,512]{2,1,0:T(8,128)(2,1)S(1)}, u32[]{:S(2)}, u32[]{:S(2)}) %all-to-all-start.1) | async-done | bytes 655392 | tf_op jit(solution)/shard_map/all_to_all | solution.py:35
  63.4 4.8 %all-to-all-start.2 = ((bf16[8,8,8,512]{3,2,1,0:T(8,128)(2,1)}), bf16[8,8,8,512]{3,2,1,0:T(8,128)(2,1)S(1)}, u32[]{:S(2)}, u32[]{:S(2)}) async-start(bf16[8,8,8,512]{3,2,1,0:T(8,128)(2,1)} %copy.40), calls=%async_computation.2 | async-start | bytes 1048576 | tf_op jit(solution)/shard_map/all_to_all | solution.py:35
  71.3 5.8 %all-to-all-done.2 = bf16[8,8,8,512]{3,2,1,0:T(8,128)(2,1)S(1)} async-done(((bf16[8,8,8,512]{3,2,1,0:T(8,128)(2,1)}), bf16[8,8,8,512]{3,2,1,0:T(8,128)(2,1)S(1)}, u32[]{:S(2)}, u32[]{:S(2)}) %all-to-all-start.2) | async-done | bytes 524320 | tf_op jit(solution)/shard_map/all_to_all | solution.py:35
  78.6 5.9 %all-to-all-start.4 = ((bf16[64,16,512]{2,1,0:T(8,128)(2,1)}), bf16[64,16,512]{2,1,0:T(8,128)(2,1)S(1)}, u32[]{:S(2)}, u32[]{:S(2)}) async-start(bf16[64,16,512]{2,1,0:T(8,128)(2,1)} %bitcast.27), calls=%async_computation.4 | async-start | bytes 2097152 | tf_op jit(solution)/shard_map/all_to_all | solution.py:35
  85.6 27.8 %all-to-all-done.4.x_ref = bf16[64,16,512]{2,1,0:T(8,128)(2,1)S(1)} async-done(((bf16[64,16,512]{2,1,0:T(8,128)(2,1)}), bf16[64,16,512]{2,1,0:T(8,128)(2,1)S(1)}, u32[]{:S(2)}, u32[]{:S(2)}) %all-to-all-start.4) | async-done | bytes 1048608 | tf_op jit(solution)/shard_map/all_to_all | solution.py:35
  119.0 3.4 %all-to-all-start.3 = ((bf16[8,8,512]{2,1,0:T(8,128)(2,1)}), bf16[8,8,512]{2,1,0:T(8,128)(2,1)S(1)}, u32[]{:S(2)}, u32[]{:S(2)}) async-start(bf16[8,8,512]{2,1,0:T(8,128)(2,1)} %convert_element_type.156), calls=%async_computation.3 | async-start | bytes 131072 | tf_op jit(solution)/shard_map/all_to_all | solution.py:35
  122.3 3.3 %collective-permute-start.8 = (bf16[64,4096]{1,0:T(8,128)(2,1)}, bf16[64,4096]{1,0:T(8,128)(2,1)}, u32[]{:S(2)}, u32[]{:S(2)}) collective-permute-start(bf16[64,4096]{1,0:T(8,128)(2,1)} %get-tuple-element.21.refs_1_), channel_id=1, source_target_pairs={{0,192},{64,0},{128,64},{192,128},{1,193},{65,1},{129,65},{193,129... | collective-permute-start | bytes 1572872 | tf_op jit(solution)/shard_map/ppermute | solution.py:39
  125.6 5.0 %all-to-all-done.3 = bf16[8,8,512]{2,1,0:T(8,128)(2,1)S(1)} async-done(((bf16[8,8,512]{2,1,0:T(8,128)(2,1)}), bf16[8,8,512]{2,1,0:T(8,128)(2,1)S(1)}, u32[]{:S(2)}, u32[]{:S(2)}) %all-to-all-start.3) | async-done | bytes 65568 | tf_op jit(solution)/shard_map/all_to_all | solution.py:35
  131.3 3.3 %collective-permute-done.7.refs_1_ = bf16[64,4096]{1,0:T(8,128)(2,1)S(1)} collective-permute-done((bf16[64,4096]{1,0:T(8,128)(2,1)}, bf16[64,4096]{1,0:T(8,128)(2,1)S(1)}, u32[]{:S(2)}, u32[]{:S(2)}) %collective-permute-start.7) | collective-permute-done | bytes 524320 | tf_op jit(solution)/shard_map/ppermute | solution.py:39
  138.5 3.9 %shard_map.126 = (bf16[4096,384]{1,0:T(8,128)(2,1)S(1)}, bf16[4096,384]{1,0:T(8,128)(2,1)S(1)}, bf16[384,4096]{1,0:T(8,128)(2,1)S(1)}) custom-call(bf16[4096,384]{1,0:T(8,128)(2,1)} %bitcast.94, bf16[4096,384]{1,0:T(8,128)(2,1)} %bitcast.95, bf16[384,4096]{1,0:T(8,128)(2,1)} %collective-permute-done.4.refs_2_, bf16[64,128]{1,0:T(8,128)(2,1)} %get-tuple-element.37.refs_3_, ...), custom_call_target="tpu_custom_call" | custom-call | tf_op jit(solution)/shard_map/pallas_call | solution.py:210
  142.4 3.5 %collective-permute-done.9.refs_4_ = bf16[64,4096]{1,0:T(8,128)(2,1)} collective-permute-done((bf16[64,4096]{1,0:T(8,128)(2,1)}, bf16[64,4096]{1,0:T(8,128)(2,1)}, u32[]{:S(2)}, u32[]{:S(2)}) %collective-permute-start.9) | collective-permute-done | bytes 524320 | tf_op jit(solution)/shard_map/ppermute | solution.py:39
  147.0 5.0 %shard_map.127 = (bf16[128,384]{1,0:T(8,128)(2,1)S(1)}, bf16[128,384]{1,0:T(8,128)(2,1)S(1)}, bf16[128,384]{1,0:T(8,128)(2,1)S(1)}) custom-call(bf16[64,4096]{1,0:T(8,128)(2,1)S(1)} %copy-done.2, bf16[64,4096]{1,0:T(8,128)(2,1)S(1)} %copy-done.4, bf16[64,4096]{1,0:T(8,128)(2,1)S(1)} %copy-done.6, bf16[64,4096]{1,0:T(8,128)(2,1)} %collective-permute-done.8.refs_3_, ...), custom_call_target="tpu_custom_call" | custom-call | flops 2415919104 | bytes 9437184 | tf_op jit(solution)/shard_map/pallas_call | solution.py:115
  155.7 2.8 %shard_map.128 = (bf16[64,384]{1,0:T(8,128)(2,1)S(1)}, bf16[64,384]{1,0:T(8,128)(2,1)S(1)}) custom-call(bf16[64,4096]{1,0:T(8,128)(2,1)} %collective-permute-done.12.refs_0_, bf16[64,4096]{1,0:T(8,128)(2,1)} %collective-permute-done.13.refs_1_, bf16[4096,384]{1,0:T(8,128)(2,1)S(1)} %get-tuple-element.24.refs_6_.refs_2_, ...), custom_call_target="tpu_custom_call" | custom-call | flops 805306368 | bytes 7340032 | tf_op jit(solution)/shard_map/pallas_call | solution.py:115
  158.6 3.2 %collective-permute-start.15 = (bf16[64,384]{1,0:T(8,128)(2,1)S(1)}, bf16[64,384]{1,0:T(8,128)(2,1)S(1)}, u32[]{:S(2)}, u32[]{:S(2)}) collective-permute-start(bf16[64,384]{1,0:T(8,128)(2,1)S(1)} %get-tuple-element.31), channel_id=1, source_target_pairs={{0,192},{64,0},{128,64},{192,128},{1,193},{65,1},{129,65},{193,129... | collective-permute-start | bytes 147464 | tf_op jit(solution)/shard_map/ppermute | solution.py:39
  164.5 5.4 %shard_map.129 = (bf16[64,4096]{1,0:T(8,128)(2,1)}, bf16[64,4096]{1,0:T(8,128)(2,1)}) custom-call(bf16[64,384]{1,0:T(8,128)(2,1)} %copy-done.22, bf16[64,384]{1,0:T(8,128)(2,1)} %copy-done.23, bf16[384,4096]{1,0:T(8,128)(2,1)} %collective-permute-done.5.refs_3_.refs_5_.refs_2_, bf16[384,4096]{1,0:T(8,128)(2,1)} %copy-done, bf16[128,384]{1,0:T(8,128)(2,1)} %copy-done.19, ...), custom_call_target="tpu_custom_call" | custom-call | flops 402653184 | bytes 8388608 | tf_op jit(solution)/shard_map/pallas_call | solution.py:176
  170.0 3.3 %collective-permute-start.17 = (bf16[64,4096]{1,0:T(8,128)(2,1)}, bf16[64,4096]{1,0:T(8,128)(2,1)S(1)}, u32[]{:S(2)}, u32[]{:S(2)}) collective-permute-start(bf16[64,4096]{1,0:T(8,128)(2,1)} %get-tuple-element.33), channel_id=1, source_target_pairs={{0,192},{64,0},{128,64},{192,128},{1,193},{65,1},{129,65},{193,129... | collective-permute-start | bytes 1572872 | tf_op jit(solution)/shard_map/ppermute | solution.py:39
  173.3 7.7 %shard_map.130 = bf16[128,4096]{1,0:T(8,128)(2,1)} custom-call(bf16[128,384]{1,0:T(8,128)(2,1)} %copy-done.9, bf16[128,384]{1,0:T(8,128)(2,1)} %copy-done.19, bf16[128,384]{1,0:T(8,128)(2,1)} %copy-done.20, bf16[384,4096]{1,0:T(8,128)(2,1)} %bitcast.98, bf16[384,4096]{1,0:T(8,128)(2,1)} %copy-done, ...), custom_call_target="tpu_custom_call" | custom-call | flops 1207959552 | bytes 13631488 | tf_op jit(solution)/shard_map/pallas_call | solution.py:176
  183.5 4.8 %all-to-all-start.5 = ((bf16[8,16,4096]{2,1,0:T(8,128)(2,1)}), bf16[8,16,4096]{2,1,0:T(8,128)(2,1)S(1)}, u32[]{:S(2)}, u32[]{:S(2)}) async-start(bf16[8,16,4096]{2,1,0:T(8,128)(2,1)} %bitcast.33), calls=%async_computation.5 | async-start | bytes 2097152 | tf_op jit(solution)/shard_map/all_to_all | solution.py:35
  188.7 14.0 %all-to-all-done.5 = bf16[8,16,4096]{2,1,0:T(8,128)(2,1)S(1)} async-done(((bf16[8,16,4096]{2,1,0:T(8,128)(2,1)}), bf16[8,16,4096]{2,1,0:T(8,128)(2,1)S(1)}, u32[]{:S(2)}, u32[]{:S(2)}) %all-to-all-start.5) | async-done | bytes 1048608 | tf_op jit(solution)/shard_map/all_to_all | solution.py:35
  203.4 22.8 %all_to_all.35 = bf16[8,8,4096]{2,1,0:T(8,128)(2,1)S(1)} all-to-all(bf16[8,8,4096]{2,1,0:T(8,128)(2,1)S(1)} %fusion.1), channel_id=1, replica_groups=mesh['y'=4,'z'=8,'x'=4,'core'=2] {'z'}, dimensions={0} | all-to-all | bytes 1048576 | tf_op jit(solution)/shard_map/all_to_all | solution.py:35
  (157 shorter events, 47.7 us)
Async XLA Ops:
  2.9 28.4 %all-to-all-start = ((bf16[32,32,256]{2,1,0:T(8,128)(2,1)}), bf16[32,32,256]{2,1,0:T(8,128)(2,1)S(1)}, u32[]{:S(2)}, u32[]{:S(2)}) async-start(bf16[32,32,256]{2,1,0:T(8,128)(2,1)} %broadcast_in_dim.54), calls=%async_computation | async-start | bytes 1048576 | tf_op jit(solution)/shard_map/all_to_all | solution.py:29
  14.4 13.8 %collective-permute-start = (bf16[512,128]{1,0:T(8,128)(2,1)}, bf16[512,128]{1,0:T(8,128)(2,1)S(1)}, u32[]{:S(2)}, u32[]{:S(2)}) collective-permute-start(bf16[512,128]{1,0:T(8,128)(2,1)} %param.15), channel_id=1, source_target_pairs={{0,192},{64,0},{128,64},{192,128},{1,193},{65,1},{129,65},{193,129... | collective-permute-start | bytes 393224 | tf_op jit(solution)/shard_map/ppermute | solution.py:39
  17.5 13.8 %collective-permute-start.1 = (bf16[512,128]{1,0:T(8,128)(2,1)}, bf16[512,128]{1,0:T(8,128)(2,1)S(1)}, u32[]{:S(2)}, u32[]{:S(2)}) collective-permute-start(bf16[512,128]{1,0:T(8,128)(2,1)} %param.15), channel_id=1, source_target_pairs={{0,128},{64,192},{128,0},{192,64},{1,129},{65,193},{129,1},{193,65... | collective-permute-start | bytes 393224 | tf_op jit(solution)/shard_map/ppermute | solution.py:39
  18.4 13.0 %collective-permute-start.2 = (bf16[512,128]{1,0:T(8,128)(2,1)}, bf16[512,128]{1,0:T(8,128)(2,1)S(1)}, u32[]{:S(2)}, u32[]{:S(2)}) collective-permute-start(bf16[512,128]{1,0:T(8,128)(2,1)} %param.15), channel_id=1, source_target_pairs={{0,64},{64,128},{128,192},{192,0},{1,65},{65,129},{129,193},{193,1... | collective-permute-start | bytes 393224 | tf_op jit(solution)/shard_map/ppermute | solution.py:39
  19.2 96.3 %collective-permute-start.5 = (bf16[384,4096]{1,0:T(8,128)(2,1)}, bf16[384,4096]{1,0:T(8,128)(2,1)}, u32[]{:S(2)}, u32[]{:S(2)}) collective-permute-start(bf16[384,4096]{1,0:T(8,128)(2,1)} %bitcast.96), channel_id=1, source_target_pairs={{0,64},{64,128},{128,192},{192,0},{1,65},{65,129},{129,193},{193,1... | collective-permute-start | bytes 9437192 | tf_op jit(solution)/shard_map/ppermute | solution.py:39
  21.0 94.5 %collective-permute-start.4 = (bf16[384,4096]{1,0:T(8,128)(2,1)}, bf16[384,4096]{1,0:T(8,128)(2,1)}, u32[]{:S(2)}, u32[]{:S(2)}) collective-permute-start(bf16[384,4096]{1,0:T(8,128)(2,1)} %bitcast.97), channel_id=1, source_target_pairs={{0,192},{64,0},{128,64},{192,128},{1,193},{65,1},{129,65},{193,129... | collective-permute-start | bytes 9437192 | tf_op jit(solution)/shard_map/ppermute | solution.py:39
  31.3 1.9 collective-permute-start.3
  36.5 25.2 %all-to-all-start.1 = ((bf16[8,80,512]{2,1,0:T(8,128)(2,1)}), bf16[8,80,512]{2,1,0:T(8,128)(2,1)S(1)}, u32[]{:S(2)}, u32[]{:S(2)}) async-start(bf16[8,80,512]{2,1,0:T(8,128)(2,1)} %shard_map.122), calls=%async_computation.1 | async-start | bytes 1310720 | tf_op jit(solution)/shard_map/all_to_all | solution.py:35
  63.4 13.7 %all-to-all-start.2 = ((bf16[8,8,8,512]{3,2,1,0:T(8,128)(2,1)}), bf16[8,8,8,512]{3,2,1,0:T(8,128)(2,1)S(1)}, u32[]{:S(2)}, u32[]{:S(2)}) async-start(bf16[8,8,8,512]{3,2,1,0:T(8,128)(2,1)} %copy.40), calls=%async_computation.2 | async-start | bytes 1048576 | tf_op jit(solution)/shard_map/all_to_all | solution.py:35
  78.6 34.8 %all-to-all-start.4 = ((bf16[64,16,512]{2,1,0:T(8,128)(2,1)}), bf16[64,16,512]{2,1,0:T(8,128)(2,1)S(1)}, u32[]{:S(2)}, u32[]{:S(2)}) async-start(bf16[64,16,512]{2,1,0:T(8,128)(2,1)} %bitcast.27), calls=%async_computation.4 | async-start | bytes 2097152 | tf_op jit(solution)/shard_map/all_to_all | solution.py:35
  115.6 15.7 %collective-permute-start.6 = (bf16[64,4096]{1,0:T(8,128)(2,1)}, bf16[64,4096]{1,0:T(8,128)(2,1)S(1)}, u32[]{:S(2)}, u32[]{:S(2)}) collective-permute-start(bf16[64,4096]{1,0:T(8,128)(2,1)} %get-tuple-element.20.refs_0_), channel_id=1, source_target_pairs={{0,192},{64,0},{128,64},{192,128},{1,193},{65,1},{129,65},{193,129... | collective-permute-start | bytes 1572872 | tf_op jit(solution)/shard_map/ppermute | solution.py:39
  118.3 16.3 %collective-permute-start.7 = (bf16[64,4096]{1,0:T(8,128)(2,1)}, bf16[64,4096]{1,0:T(8,128)(2,1)S(1)}, u32[]{:S(2)}, u32[]{:S(2)}) collective-permute-start(bf16[64,4096]{1,0:T(8,128)(2,1)} %get-tuple-element.21.refs_1_), channel_id=1, source_target_pairs={{0,64},{64,128},{128,192},{192,0},{1,65},{65,129},{129,193},{193,1... | collective-permute-start | bytes 1572872 | tf_op jit(solution)/shard_map/ppermute | solution.py:39
  119.0 11.7 %all-to-all-start.3 = ((bf16[8,8,512]{2,1,0:T(8,128)(2,1)}), bf16[8,8,512]{2,1,0:T(8,128)(2,1)S(1)}, u32[]{:S(2)}, u32[]{:S(2)}) async-start(bf16[8,8,512]{2,1,0:T(8,128)(2,1)} %convert_element_type.156), calls=%async_computation.3 | async-start | bytes 131072 | tf_op jit(solution)/shard_map/all_to_all | solution.py:35
  122.3 20.1 %collective-permute-start.8 = (bf16[64,4096]{1,0:T(8,128)(2,1)}, bf16[64,4096]{1,0:T(8,128)(2,1)}, u32[]{:S(2)}, u32[]{:S(2)}) collective-permute-start(bf16[64,4096]{1,0:T(8,128)(2,1)} %get-tuple-element.21.refs_1_), channel_id=1, source_target_pairs={{0,192},{64,0},{128,64},{192,128},{1,193},{65,1},{129,65},{193,129... | collective-permute-start | bytes 1572872 | tf_op jit(solution)/shard_map/ppermute | solution.py:39
  125.6 20.3 %collective-permute-start.9 = (bf16[64,4096]{1,0:T(8,128)(2,1)}, bf16[64,4096]{1,0:T(8,128)(2,1)}, u32[]{:S(2)}, u32[]{:S(2)}) collective-permute-start(bf16[64,4096]{1,0:T(8,128)(2,1)} %get-tuple-element.20.refs_0_), channel_id=1, source_target_pairs={{0,64},{64,128},{128,192},{192,0},{1,65},{65,129},{129,193},{193,1... | collective-permute-start | bytes 1572872 | tf_op jit(solution)/shard_map/ppermute | solution.py:39
  135.4 18.7 %collective-permute-start.12 = (bf16[64,4096]{1,0:T(8,128)(2,1)}, bf16[64,4096]{1,0:T(8,128)(2,1)}, u32[]{:S(2)}, u32[]{:S(2)}) collective-permute-start(bf16[64,4096]{1,0:T(8,128)(2,1)} %get-tuple-element.22.refs_2_), channel_id=1, source_target_pairs={{0,192},{64,0},{128,64},{192,128},{1,193},{65,1},{129,65},{193,129... | collective-permute-start | bytes 1572872 | tf_op jit(solution)/shard_map/ppermute | solution.py:39
  135.6 20.1 %collective-permute-start.13 = (bf16[64,4096]{1,0:T(8,128)(2,1)}, bf16[64,4096]{1,0:T(8,128)(2,1)}, u32[]{:S(2)}, u32[]{:S(2)}) collective-permute-start(bf16[64,4096]{1,0:T(8,128)(2,1)} %get-tuple-element.23.refs_5_), channel_id=1, source_target_pairs={{0,64},{64,128},{128,192},{192,0},{1,65},{65,129},{129,193},{193,1... | collective-permute-start | bytes 1572872 | tf_op jit(solution)/shard_map/ppermute | solution.py:39
  152.0 9.9 %collective-permute-start.10 = (bf16[128,384]{1,0:T(8,128)(2,1)S(1)}, bf16[128,384]{1,0:T(8,128)(2,1)S(1)}, u32[]{:S(2)}, u32[]{:S(2)}) collective-permute-start(bf16[128,384]{1,0:T(8,128)(2,1)S(1)} %get-tuple-element.27), channel_id=1, source_target_pairs={{0,192},{64,0},{128,64},{192,128},{1,193},{65,1},{129,65},{193,129... | collective-permute-start | bytes 294920 | tf_op jit(solution)/shard_map/ppermute | solution.py:39
  152.1 9.8 %collective-permute-start.11 = (bf16[128,384]{1,0:T(8,128)(2,1)S(1)}, bf16[128,384]{1,0:T(8,128)(2,1)S(1)}, u32[]{:S(2)}, u32[]{:S(2)}) collective-permute-start(bf16[128,384]{1,0:T(8,128)(2,1)S(1)} %get-tuple-element.28), channel_id=1, source_target_pairs={{0,64},{64,128},{128,192},{192,0},{1,65},{65,129},{129,193},{193,1... | collective-permute-start | bytes 294920 | tf_op jit(solution)/shard_map/ppermute | solution.py:39
  158.5 5.4 %collective-permute-start.14 = (bf16[64,384]{1,0:T(8,128)(2,1)S(1)}, bf16[64,384]{1,0:T(8,128)(2,1)S(1)}, u32[]{:S(2)}, u32[]{:S(2)}) collective-permute-start(bf16[64,384]{1,0:T(8,128)(2,1)S(1)} %get-tuple-element.30), channel_id=1, source_target_pairs={{0,64},{64,128},{128,192},{192,0},{1,65},{65,129},{129,193},{193,1... | collective-permute-start | bytes 147464 | tf_op jit(solution)/shard_map/ppermute | solution.py:39
  158.6 5.3 %collective-permute-start.15 = (bf16[64,384]{1,0:T(8,128)(2,1)S(1)}, bf16[64,384]{1,0:T(8,128)(2,1)S(1)}, u32[]{:S(2)}, u32[]{:S(2)}) collective-permute-start(bf16[64,384]{1,0:T(8,128)(2,1)S(1)} %get-tuple-element.31), channel_id=1, source_target_pairs={{0,192},{64,0},{128,64},{192,128},{1,193},{65,1},{129,65},{193,129... | collective-permute-start | bytes 147464 | tf_op jit(solution)/shard_map/ppermute | solution.py:39
  169.9 11.1 %collective-permute-start.16 = (bf16[64,4096]{1,0:T(8,128)(2,1)}, bf16[64,4096]{1,0:T(8,128)(2,1)S(1)}, u32[]{:S(2)}, u32[]{:S(2)}) collective-permute-start(bf16[64,4096]{1,0:T(8,128)(2,1)} %get-tuple-element.32.refs_6_), channel_id=1, source_target_pairs={{0,64},{64,128},{128,192},{192,0},{1,65},{65,129},{129,193},{193,1... | collective-permute-start | bytes 1572872 | tf_op jit(solution)/shard_map/ppermute | solution.py:39
  170.0 11.0 %collective-permute-start.17 = (bf16[64,4096]{1,0:T(8,128)(2,1)}, bf16[64,4096]{1,0:T(8,128)(2,1)S(1)}, u32[]{:S(2)}, u32[]{:S(2)}) collective-permute-start(bf16[64,4096]{1,0:T(8,128)(2,1)} %get-tuple-element.33), channel_id=1, source_target_pairs={{0,192},{64,0},{128,64},{192,128},{1,193},{65,1},{129,65},{193,129... | collective-permute-start | bytes 1572872 | tf_op jit(solution)/shard_map/ppermute | solution.py:39
  183.5 19.3 %all-to-all-start.5 = ((bf16[8,16,4096]{2,1,0:T(8,128)(2,1)}), bf16[8,16,4096]{2,1,0:T(8,128)(2,1)S(1)}, u32[]{:S(2)}, u32[]{:S(2)}) async-start(bf16[8,16,4096]{2,1,0:T(8,128)(2,1)} %bitcast.33), calls=%async_computation.5 | async-start | bytes 2097152 | tf_op jit(solution)/shard_map/all_to_all | solution.py:35
  (24 other events, 163.7 us)
